TPU v7x, 128 devices: a whole 4x4x4 slice. The times are simulated.
128 devices in a mesh: row: 8 (over y, core), col: 16 (over x, z).
Axes of the slice: x: 4, y: 4, z: 4, core: 2. Of those that a mesh axis runs over, the one named last changes fastest.
Arguments:
- object_field: float32 [2, 4096, 8192], P(None, 'row', 'col'), may hold values from -6 to 6
- probe: float32 [4, 2, 256, 256], replicated, may hold values from -4 to 4
- amplitudes: bfloat16 [512, 256, 256], P(('row', 'col')), may hold values from 0 to 2
- owner: int32 [512], P(('row', 'col')), may hold values from 0 to 15, as said below
- offsets: int32 [512, 2], P(('row', 'col')), may hold values from 0 to 511
Outputs:
- object_out: float32 [2, 4096, 8192], P(None, 'row', 'col')
- probe_gradient: float32 [4, 2, 256, 256], replicated
Inputs may be any that keep to these rules, and one draw needn't show every extreme that they name: owner[p] is a tile column of the same tile row as the device holding p. The patterns of one device that share an owner number at most 1, and on every device some owner receives exactly 1 of them. Every tile comes to own either exactly 12 patterns or one or two.
All inputs are finite; a program needn't handle non-finite values.
Results may differ from a plain program's by a relative error of at most 0.0024.
Values may be sent and summed in bfloat16 or wider, within the bound.
A program may use at most 128 MiB of HBM per device.

v0:
```python
import math

import jax
import jax.numpy as jnp
from jax import lax
from jax.sharding import PartitionSpec as P


def shifted(value, axis, by):
    size = lax.axis_size(axis)
    pairs = [(i, i + by) for i in range(size) if 0 <= i + by < size]
    return lax.ppermute(value, axis, pairs)


def padded(cells, sides, width):
    for axis, dim in sides:
        count = lax.axis_size(axis)
        ends = count - 1
        head = lax.slice_in_dim(cells, 0, width, axis=dim)
        tail = lax.slice_in_dim(cells, cells.shape[dim] - width, cells.shape[dim], axis=dim)
        cells = jnp.concatenate(
            [
                lax.ppermute(tail, axis, [(i, (i + 1) % count) for i in range(ends)]),
                cells,
                lax.ppermute(head, axis, [((i + 1) % count, i) for i in range(ends)]),
            ],
            axis=dim,
        )
    return cells


def dft_tables(side_length):
    series = jnp.arange(side_length, dtype=jnp.int32)
    product = series[:, None] * series[None, :] % side_length
    angles = product.astype(jnp.float32) * (2.0 * math.pi / side_length)
    factor = 1.0 / math.sqrt(side_length)
    table_re = (jnp.cos(angles) * factor).astype(jnp.bfloat16)
    table_im = (-jnp.sin(angles) * factor).astype(jnp.bfloat16)
    return (table_re, table_im)


def left_pass(table_re, table_im, field_re, field_im):

    def multiply(table, field):
        return jnp.einsum("jk,mkl->mjl", table, field, preferred_element_type=jnp.float32)

    real_part = multiply(table_re, field_re) - multiply(table_im, field_im)
    imag_part = multiply(table_re, field_im) + multiply(table_im, field_re)
    return (real_part, imag_part)


def right_pass(field_re, field_im, table_re, table_im):

    def multiply(field, table):
        return jnp.einsum("mjk,kl->mjl", field, table, preferred_element_type=jnp.float32)

    real_part = multiply(field_re, table_re) - multiply(field_im, table_im)
    imag_part = multiply(field_im, table_re) + multiply(field_re, table_im)
    return (real_part, imag_part)


def pattern_terms(patch, probe, amp_one, table_re, table_im, live_one):
    probe_re = probe[:, 0]
    probe_im = probe[:, 1]
    patch_re = patch[0]
    patch_im = patch[1]
    exit_re = probe_re * patch_re - probe_im * patch_im
    exit_im = probe_re * patch_im + probe_im * patch_re
    half_re, half_im = left_pass(
        table_re, table_im, exit_re.astype(jnp.bfloat16), exit_im.astype(jnp.bfloat16)
    )
    far_re, far_im = right_pass(
        half_re.astype(jnp.bfloat16), half_im.astype(jnp.bfloat16), table_re, table_im
    )
    model = jnp.sqrt(jnp.sum(far_re * far_re + far_im * far_im, axis=0))
    ratio = amp_one.astype(jnp.float32) / jnp.maximum(model, 0.5)
    repl_re = (far_re * ratio).astype(jnp.bfloat16)
    repl_im = (far_im * ratio).astype(jnp.bfloat16)
    conj_im = -table_im
    back_re, back_im = left_pass(table_re, conj_im, repl_re, repl_im)
    ret_re, ret_im = right_pass(
        back_re.astype(jnp.bfloat16), back_im.astype(jnp.bfloat16), table_re, conj_im
    )
    change_re = (ret_re - exit_re) * live_one
    change_im = (ret_im - exit_im) * live_one
    numer_one = jnp.stack(
        [
            jnp.sum(probe_re * change_re + probe_im * change_im, axis=0),
            jnp.sum(probe_re * change_im - probe_im * change_re, axis=0),
        ]
    )
    grad_one = jnp.stack(
        [patch_re * change_re + patch_im * change_im, patch_re * change_im - patch_im * change_re],
        axis=1,
    )
    return (numer_one, grad_one)


def add_window(whole_array, piece, corner):
    current = lax.dynamic_slice(whole_array, corner, piece.shape)
    return lax.dynamic_update_slice(whole_array, current + piece, corner)


def pass_rows(numer_rim, weight_rim, offset_by):
    return shifted((numer_rim, weight_rim), "row", offset_by)


def pass_cols(numer_rim, weight_rim, offset_by):
    return shifted((numer_rim, weight_rim), "col", offset_by)


def settle(numer, weight, tile_side, half_width):
    pattern_side = 2 * half_width
    from_below = pass_rows(numer[:, :half_width], weight[:half_width], -1)
    from_above = pass_rows(numer[:, tile_side + half_width :], weight[tile_side + half_width :], 1)
    numer = numer.at[:, tile_side : tile_side + half_width].add(from_below[0])
    numer = numer.at[:, half_width:pattern_side].add(from_above[0])
    weight = weight.at[tile_side : tile_side + half_width].add(from_below[1])
    weight = weight.at[half_width:pattern_side].add(from_above[1])
    numer = numer[:, half_width : half_width + tile_side]
    weight = weight[half_width : half_width + tile_side]
    from_right = pass_cols(numer[:, :, :half_width], weight[:, :half_width], -1)
    from_left = pass_cols(
        numer[:, :, tile_side + half_width :], weight[:, tile_side + half_width :], 1
    )
    numer = numer.at[:, :, tile_side : tile_side + half_width].add(from_right[0])
    numer = numer.at[:, :, half_width:pattern_side].add(from_left[0])
    weight = weight.at[:, tile_side : tile_side + half_width].add(from_right[1])
    weight = weight.at[:, half_width:pattern_side].add(from_left[1])
    return (
        numer[:, :, half_width : half_width + tile_side],
        weight[:, half_width : half_width + tile_side],
    )


def on_device(object_field, probe, amplitudes, owner, offsets):
    tile_across = lax.axis_size("col")
    held_count = amplitudes.shape[0]
    total_count = lax.axis_size("row") * tile_across * held_count
    tile_side = object_field.shape[1]
    pattern_side = probe.shape[-1]
    half_width = pattern_side // 2
    quarter = tile_across // 4
    capacity = (held_count - 2) // quarter + 1
    most_slots = 4 * (held_count - 1)
    slots_all = tile_across * capacity
    table_re, table_im = dft_tables(pattern_side)
    power = jnp.sum(probe[:, 0] * probe[:, 0] + probe[:, 1] * probe[:, 1], axis=0)
    extended = padded(object_field, (("row", 1), ("col", 2)), half_width)
    series_held = jnp.arange(held_count, dtype=jnp.int32)
    same_owner = owner[:, None] == owner[None, :]
    earlier = series_held[None, :] < series_held[:, None]
    rank_held = jnp.sum((same_owner & earlier).astype(jnp.int32), axis=1)
    target_slot = owner * capacity + rank_held
    select = target_slot[None, :] == jnp.arange(slots_all, dtype=jnp.int32)[:, None]
    details = jnp.stack([jnp.ones((held_count,), jnp.int32), offsets[:, 0], offsets[:, 1]], axis=1)
    send_details = jnp.sum(select[:, :, None].astype(jnp.int32) * details[None], axis=1)
    zero_index = jnp.zeros((), jnp.int32)
    numer_start = jnp.zeros(extended.shape, jnp.float32)
    weight_start = jnp.zeros(extended.shape[1:], jnp.float32)
    grad_start = jnp.zeros(probe.shape, jnp.float32)
    flat_amp = amplitudes.reshape(held_count, pattern_side * pattern_side)
    send_amp = jnp.dot(
        select.astype(jnp.bfloat16), flat_amp, preferred_element_type=jnp.float32
    ).astype(jnp.bfloat16)
    got_amp, got_details = (
        lax.all_to_all(send_amp, "col", split_axis=0, concat_axis=0, tiled=True),
        lax.all_to_all(send_details, "col", split_axis=0, concat_axis=0, tiled=True),
    )
    live_got = got_details[:, 0]
    order_got = jnp.cumsum(live_got) - 1
    pick = (live_got[None, :] == 1) & (
        order_got[None, :] == jnp.arange(most_slots, dtype=jnp.int32)[:, None]
    )
    packed_amp = jnp.dot(
        pick.astype(jnp.bfloat16), got_amp, preferred_element_type=jnp.float32
    ).astype(jnp.bfloat16)
    packed_amp = packed_amp.reshape(most_slots, pattern_side, pattern_side)
    packed_details = jnp.sum(pick[:, :, None].astype(jnp.int32) * got_details[None], axis=1)

    def visit(carry, item):
        numer_acc, weight_acc, grad_acc = carry
        amp_one, detail_one = item
        live_one = detail_one[0].astype(jnp.float32)
        corner = (zero_index, detail_one[1], detail_one[2])
        patch = lax.dynamic_slice(extended, corner, (2, pattern_side, pattern_side))
        numer_one, grad_one = pattern_terms(patch, probe, amp_one, table_re, table_im, live_one)
        numer_acc = add_window(numer_acc, numer_one, corner)
        weight_acc = add_window(weight_acc, power * live_one, (detail_one[1], detail_one[2]))
        return ((numer_acc, weight_acc, grad_acc + grad_one), None)

    (numer, weight, gradient), skipped = lax.scan(
        visit, (numer_start, weight_start, grad_start), (packed_amp, packed_details)
    )
    numer_core, weight_core = settle(numer, weight, tile_side, half_width)
    object_out = object_field + numer_core / (weight_core + 1.0)
    gradient_total = lax.psum(gradient, ("row", "col"))
    probe_gradient = gradient_total * (1.0 / math.sqrt(total_count))
    return (object_out, probe_gradient)


def solution(mesh):
    return jax.shard_map(
        on_device,
        mesh=mesh,
        in_specs=(
            P(None, "row", "col"),
            P(),
            P(("row", "col"), None, None),
            P(("row", "col")),
            P(("row", "col"), None),
        ),
        out_specs=(P(None, "row", "col"), P()),
        check_vma=False,
    )
```

profile of v0, /device:TPU:1, one launch (start us, length us, event | category | flops | bytes accessed | tf_op | source)
XLA Modules:
  0.0 875.5 jit_solution(11631103920254479434)
XLA Ops:
  9.5 4.6 collective-permute-start
  19.1 7.6 all-to-all-start
  31.4 4.0 reshape.344
  35.4 6.7 all-to-all-start.1
  54.6 27.1 %collective-permute-done.2 = f32[2,768,128]{2,1,0:T(8,128)S(1)} collective-permute-done((f32[2,768,128]{2,1,0:T(8,128)}, f32[2,768,128]{2,1,0:T(8,128)S(1)}, u32[]{:S(2)}, u32[]{:S(2)}) %collective-permute-start.2) | collective-permute-done | bytes 786464 | tf_op jit(solution)/shard_map/ppermute | solution.py:23
  83.6 4.6 pad_maximum_fusion
  88.2 10.5 %reshape.345 = bf16[16,1,65536]{2,1,0:T(2,128)(2,1)} reshape(bf16[16,2,32768]{2,1,0:T(2,128)(2,1)} %all-to-all-done.1) | data formatting | bytes 4194304
  98.7 4.6 convolution_convert_fusion
  109.0 559.1 %while.25 = (s32[]{:T(128)}, f32[2,768,768]{2,1,0:T(8,128)}, f32[768,768]{1,0:T(8,128)}, f32[4,2,256,256]{3,2,0,1:T(8,128)}, s32[12,3]{0,1:T(4,128)S(1)}, /*inde...) while((s32[]{:T(128)}, f32[2,768,768]{2,1,0:T(8,128)}, ...), condition=%wide.region_9.10_spmd.clone.clone, body=%wide.region_5.9_spmd.clone.clone.sunk | while | flops 2181169152 | bytes 64094588 | solution.py:192
  136.0 3.9 add_bitcast_fusion.2
  144.2 6.8 dynamic_update_slice.14
  152.1 3.9 dynamic_update_slice.15
  183.0 3.9 add_bitcast_fusion.2
  186.9 3.5 maximum_add_fusion.5
  191.9 6.7 dynamic_update_slice.14
  199.7 3.9 dynamic_update_slice.15
  230.6 3.9 add_bitcast_fusion.2
  234.5 3.5 maximum_add_fusion.5
  239.4 5.9 dynamic_update_slice.14
  277.0 3.9 add_bitcast_fusion.2
  280.9 3.5 maximum_add_fusion.5
  285.9 5.9 dynamic_update_slice.14
  323.5 3.9 add_bitcast_fusion.2
  327.4 3.5 maximum_add_fusion.5
  332.3 5.9 dynamic_update_slice.14
  369.9 3.9 add_bitcast_fusion.2
  373.8 3.5 maximum_add_fusion.5
  378.8 5.9 dynamic_update_slice.14
  416.4 3.9 add_bitcast_fusion.2
  420.3 3.5 maximum_add_fusion.5
  425.2 5.9 dynamic_update_slice.14
  462.8 3.9 add_bitcast_fusion.2
  466.7 3.5 maximum_add_fusion.5
  471.7 5.9 dynamic_update_slice.14
  509.3 3.9 add_bitcast_fusion.2
  518.1 5.9 dynamic_update_slice.14
  555.7 3.9 add_bitcast_fusion.2
  564.6 5.9 dynamic_update_slice.14
  602.2 3.9 add_bitcast_fusion.2
  606.1 3.5 maximum_add_fusion.5
  611.1 5.9 dynamic_update_slice.14
  648.6 3.9 add_bitcast_fusion.2
  657.5 5.9 dynamic_update_slice.14
  676.1 11.0 %collective-permute-done.8 = f32[128,768]{1,0:T(8,128)} collective-permute-done((f32[128,768]{1,0:T(8,128)S(1)}, f32[128,768]{1,0:T(8,128)}, u32[]{:S(2)}, u32[]{:S(2)}) %collective-permute-start.8) | collective-permute-done | bytes 393248 | tf_op jit(solution)/shard_map/ppermute | solution.py:12
  701.1 16.1 %collective-permute-start.11 = (f32[512,128]{1,0:T(8,128)S(1)}, f32[512,128]{1,0:T(8,128)S(1)}, u32[]{:S(2)}, u32[]{:S(2)}) collective-permute-start(f32[512,128]{1,0:T(8,128)S(1)} %get-tuple-element.412), channel_id=1, source_target_pairs={{0,1},{1,2},{2,3},{3,4},{4,5},{5,6},{6,7},{7,8},{8,9},{9,10},{10,1... | collective-permute-start | bytes 786440 | tf_op jit(solution)/shard_map/ppermute | solution.py:12
  717.2 125.1 %all-reduce.3.cloned.1.call-done = f32[4,2,256,256]{3,2,1,0:T(8,128)} async-done(((f32[4,2,256,256]{3,2,1,0:T(8,128)}), f32[4,2,256,256]{3,2,1,0:T(8,128)}) %all-reduce.3.cloned.1.call-update) | async-done | bytes 2097168 | tf_op jit(solution)/shard_map/psum | solution.py:197
  852.7 4.0 collective-permute-start.7
  857.0 6.6 collective-permute-done.6
  (414 shorter events, 416.7 us)
Async XLA Ops:
  7.2 19.5 %copy-start.9 = (bf16[4,256,256]{2,1,0:T(8,128)(2,1)S(1)}, bf16[4,256,256]{2,1,0:T(8,128)(2,1)}, u32[]{:S(2)}) copy-start(bf16[4,256,256]{2,1,0:T(8,128)(2,1)} %param.25) | copy-start | bytes 1572868
  9.5 34.4 %collective-permute-start = (f32[2,128,512]{2,1,0:T(8,128)}, f32[2,128,512]{2,1,0:T(8,128)S(1)}, u32[]{:S(2)}, u32[]{:S(2)}) collective-permute-start(f32[2,128,512]{2,1,0:T(8,128)} %get-tuple-element.417), channel_id=1, source_target_pairs={{0,16},{16,32},{32,48},{48,64},{64,80},{80,96},{96,112},{1,17},{17... | collective-permute-start | bytes 1572872 | tf_op jit(solution)/shard_map/ppermute | solution.py:23
  14.1 31.7 %collective-permute-start.1 = (f32[2,128,512]{2,1,0:T(8,128)}, f32[2,128,512]{2,1,0:T(8,128)S(1)}, u32[]{:S(2)}, u32[]{:S(2)}) collective-permute-start(f32[2,128,512]{2,1,0:T(8,128)} %get-tuple-element.416), channel_id=1, source_target_pairs={{16,0},{32,16},{48,32},{64,48},{80,64},{96,80},{112,96},{17,1},{33... | collective-permute-start | bytes 1572872 | tf_op jit(solution)/shard_map/ppermute | solution.py:25
  19.1 16.3 %all-to-all-start = ((s32[16,1,3]{2,1,0:T(1,128)}), s32[16,1,3]{2,1,0:T(1,128)S(1)}, u32[]{:S(2)}, u32[]{:S(2)}) async-start(s32[16,1,3]{2,1,0:T(1,128)} %copy.113), calls=%async_computation | async-start | bytes 16384 | tf_op jit(solution)/shard_map/all_to_all | solution.py:168
  35.4 52.8 %all-to-all-start.1 = ((bf16[16,2,32768]{2,1,0:T(2,128)(2,1)}), bf16[16,2,32768]{2,1,0:T(2,128)(2,1)}, u32[]{:S(2)}, u32[]{:S(2)}) async-start(bf16[16,2,32768]{2,1,0:T(2,128)(2,1)} %reshape.344), calls=%async_computation.1 | async-start | bytes 4194304 | tf_op jit(solution)/shard_map/all_to_all | solution.py:167
  42.1 800.1 %all-reduce.3.cloned.1.call-start = ((), (), s32[]{:S(2)}) async-start(), calls=%async_computation.2 | async-start | bytes 4194304 | tf_op jit(solution)/shard_map/psum | solution.py:197
  45.7 7.6 copy-start.8
  45.8 1.7 copy-start.7
  48.7 33.0 %collective-permute-start.2 = (f32[2,768,128]{2,1,0:T(8,128)}, f32[2,768,128]{2,1,0:T(8,128)S(1)}, u32[]{:S(2)}, u32[]{:S(2)}) collective-permute-start(f32[2,768,128]{2,1,0:T(8,128)} %get-tuple-element.410), channel_id=1, source_target_pairs={{0,1},{1,2},{2,3},{3,4},{4,5},{5,6},{6,7},{7,8},{8,9},{9,10},{10,1... | collective-permute-start | bytes 2359304 | tf_op jit(solution)/shard_map/ppermute | solution.py:23
  52.0 31.6 %collective-permute-start.3 = (f32[2,768,128]{2,1,0:T(8,128)}, f32[2,768,128]{2,1,0:T(8,128)}, u32[]{:S(2)}, u32[]{:S(2)}) collective-permute-start(f32[2,768,128]{2,1,0:T(8,128)} %get-tuple-element.411), channel_id=1, source_target_pairs={{1,0},{2,1},{3,2},{4,3},{5,4},{6,5},{7,6},{8,7},{9,8},{10,9},{11,1... | collective-permute-start | bytes 2359304 | tf_op jit(solution)/shard_map/ppermute | solution.py:25
  139.9 2.9 copy-start.2
  142.8 8.2 copy-start.6
  186.9 3.5 copy-start.2
  190.5 8.1 copy-start.6
  234.5 3.5 copy-start.2
  238.0 7.3 copy-start.6
  280.9 3.5 copy-start.2
  284.5 7.3 copy-start.6
  327.4 3.5 copy-start.2
  330.9 7.3 copy-start.6
  373.8 3.5 copy-start.2
  377.4 7.3 copy-start.6
  420.3 3.5 copy-start.2
  423.8 7.3 copy-start.6
  466.7 3.5 copy-start.2
  470.3 7.3 copy-start.6
  513.2 3.5 copy-start.2
  516.7 7.3 copy-start.6
  559.6 3.5 copy-start.2
  563.2 7.3 copy-start.6
  606.1 3.5 copy-start.2
  609.6 7.3 copy-start.6
  652.5 3.5 copy-start.2
  656.1 7.3 copy-start.6
  668.1 6.5 copy-start
  669.4 23.1 %collective-permute-start.4 = (f32[2,128,768]{2,1,0:T(8,128)S(1)}, f32[2,128,768]{2,1,0:T(8,128)}, u32[]{:S(2)}, u32[]{:S(2)}) collective-permute-start(f32[2,128,768]{2,1,0:T(8,128)S(1)} %slice.281), channel_id=1, source_target_pairs={{16,0},{32,16},{48,32},{64,48},{80,64},{96,80},{112,96},{17,1},{33... | collective-permute-start | bytes 2359304 | tf_op jit(solution)/shard_map/ppermute | solution.py:12
  672.7 14.4 %collective-permute-start.8 = (f32[128,768]{1,0:T(8,128)S(1)}, f32[128,768]{1,0:T(8,128)}, u32[]{:S(2)}, u32[]{:S(2)}) collective-permute-start(f32[128,768]{1,0:T(8,128)S(1)} %slice.291), channel_id=1, source_target_pairs={{16,0},{32,16},{48,32},{64,48},{80,64},{96,80},{112,96},{17,1},{33... | collective-permute-start | bytes 1179656 | tf_op jit(solution)/shard_map/ppermute | solution.py:12
  689.1 9.1 %copy-start.3 = (f32[768,768]{1,0:T(8,128)S(1)}, f32[768,768]{1,0:T(8,128)}, u32[]{:S(2)}) copy-start(f32[768,768]{1,0:T(8,128)} %get-tuple-element.415) | copy-start | bytes 7077892
  689.1 9.1 %collective-permute-start.9 = (f32[128,768]{1,0:T(8,128)S(1)}, f32[128,768]{1,0:T(8,128)S(1)}, u32[]{:S(2)}, u32[]{:S(2)}) collective-permute-start(f32[128,768]{1,0:T(8,128)S(1)} %get-tuple-element.414), channel_id=1, source_target_pairs={{0,16},{16,32},{32,48},{48,64},{64,80},{80,96},{96,112},{1,17},{17... | collective-permute-start | bytes 1179656 | tf_op jit(solution)/shard_map/ppermute | solution.py:12
  695.4 149.9 %collective-permute-start.5 = (f32[2,128,768]{2,1,0:T(8,128)}, f32[2,128,768]{2,1,0:T(8,128)S(1)}, u32[]{:S(2)}, u32[]{:S(2)}) collective-permute-start(f32[2,128,768]{2,1,0:T(8,128)} %get-tuple-element.408), channel_id=1, source_target_pairs={{0,16},{16,32},{32,48},{48,64},{64,80},{80,96},{96,112},{1,17},{17... | collective-permute-start | bytes 2359304 | tf_op jit(solution)/shard_map/ppermute | solution.py:12
  698.4 1.4 copy-start.4
  699.8 150.5 %collective-permute-start.10 = (f32[512,128]{1,0:T(8,128)S(1)}, f32[512,128]{1,0:T(8,128)S(1)}, u32[]{:S(2)}, u32[]{:S(2)}) collective-permute-start(f32[512,128]{1,0:T(8,128)S(1)} %get-tuple-element.413), channel_id=1, source_target_pairs={{1,0},{2,1},{3,2},{4,3},{5,4},{6,5},{7,6},{8,7},{9,8},{10,9},{11,1... | collective-permute-start | bytes 786440 | tf_op jit(solution)/shard_map/ppermute | solution.py:12
  701.1 150.8 %collective-permute-start.11 = (f32[512,128]{1,0:T(8,128)S(1)}, f32[512,128]{1,0:T(8,128)S(1)}, u32[]{:S(2)}, u32[]{:S(2)}) collective-permute-start(f32[512,128]{1,0:T(8,128)S(1)} %get-tuple-element.412), channel_id=1, source_target_pairs={{0,1},{1,2},{2,3},{3,4},{4,5},{5,6},{6,7},{7,8},{8,9},{9,10},{10,1... | collective-permute-start | bytes 786440 | tf_op jit(solution)/shard_map/ppermute | solution.py:12
  847.4 9.4 %copy-start.1 = (f32[2,768,768]{2,1,0:T(8,128)S(1)}, f32[2,768,768]{2,1,0:T(8,128)}, u32[]{:S(2)}) copy-start(f32[2,768,768]{2,1,0:T(8,128)} %fusion.149) | copy-start | bytes 14155780
  848.9 14.8 %collective-permute-start.6 = (f32[2,512,128]{2,1,0:T(8,128)S(1)}, f32[2,512,128]{2,1,0:T(8,128)S(1)}, u32[]{:S(2)}, u32[]{:S(2)}) collective-permute-start(f32[2,512,128]{2,1,0:T(8,128)S(1)} %get-tuple-element.407), channel_id=1, source_target_pairs={{1,0},{2,1},{3,2},{4,3},{5,4},{6,5},{7,6},{8,7},{9,8},{10,9},{11,1... | collective-permute-start | bytes 1572872 | tf_op jit(solution)/shard_map/ppermute | solution.py:12
  852.7 14.2 %collective-permute-start.7 = (f32[2,512,128]{2,1,0:T(8,128)S(1)}, f32[2,512,128]{2,1,0:T(8,128)S(1)}, u32[]{:S(2)}, u32[]{:S(2)}) collective-permute-start(f32[2,512,128]{2,1,0:T(8,128)S(1)} %get-tuple-element.406), channel_id=1, source_target_pairs={{0,1},{1,2},{2,3},{3,4},{4,5},{5,6},{6,7},{7,8},{8,9},{9,10},{10,1... | collective-permute-start | bytes 1572872 | tf_op jit(solution)/shard_map/ppermute | solution.py:12
  857.0 9.9 %copy-start.5 = (f32[2,512,512]{2,1,0:T(8,128)S(1)}, f32[2,512,512]{2,1,0:T(8,128)}, u32[]{:S(2)}) copy-start(f32[2,512,512]{2,1,0:T(8,128)} %param.23) | copy-start | bytes 6291460
Sparse Core Ops, SparseCore 0:
  676.2 165.9 all-reduce.2
where the time goes:
time: 888 us; the launch traced here: 876 us
  matrix products  281 us (32%)
  local copies, waits for them, and re-layouts  178 us (20%)
  waiting for transfers between devices  175 us (20%)
  other arithmetic  114 us (13%)
  starting transfers between devices  57.2 us (6%)
  loops' own time  56 us (6%)
  between operations  14.4 us (2%)
    dot_general x96, matrix products, multiply(): jnp.einsum('mjk,kl->mjl', field, table, preferred_element_type=jnp.float32)  154 us
    psum x1, waiting for transfers between devices, on_device(): gradient_total = lax.psum(gradient, ('row', 'col'))  125 us
    dot_general x96, matrix products, multiply(): jnp.einsum('jk,mkl->mjl', table, field, preferred_element_type=jnp.float32)  122 us
    dynamic_update_slice x24, local copies, waits for them, and re-layouts, add_window(): return lax.dynamic_update_slice(whole_array, current + piece, corner)  116 us
    another operation x1, loops' own time, on_device(): lax.scan(visit, (numer_start, weight_start, grad_start), (packed_amp, pac...  56 us
    add x12, other arithmetic, visit(): return ((numer_acc, weight_acc, grad_acc + grad_one), None)  41.8 us
    ppermute x8, starting transfers between devices, shifted(): return lax.ppermute(value, axis, pairs)  31.8 us
    add x24, other arithmetic, add_window(): return lax.dynamic_update_slice(whole_array, current + piece, corner)  30.4 us
  transfers between devices with their start and end apart: 15, of which 6 were waited for; matrix products, arithmetic and copies ran while one was open for 5% of the time, Pallas kernels for 0%

commit v1 on v0

v1 whole, which is shorter than its diff:
```python
import functools
import math

import jax
import jax.numpy as jnp
import numpy as np
from jax import lax
from jax.experimental import pallas as pl
from jax.experimental.pallas import tpu as pltpu
from jax.sharding import PartitionSpec as P

F32, BF16 = jnp.float32, jnp.bfloat16

def tables(side):
    series = np.arange(side, dtype=np.int32)
    angles = (series[:, None] * series[None, :] % side).astype(np.float32) * np.float32(2.0 * math.pi / side)
    factor = np.float32(1.0 / math.sqrt(side))
    re = jnp.asarray(np.cos(angles) * factor).astype(BF16)
    im = jnp.asarray(-np.sin(angles) * factor).astype(BF16)
    return re, im

def dot(a, b):
    return jnp.dot(a, b, preferred_element_type=F32)

def kernel(slots, modes, side, det_ref, ext_ref, probe_ref, amp_ref, tab_ref,
           num_ref, wgt_ref, grad_ref,
           patch, ebuf, hbuf, far, pow_ref, ssum, nbuf):
    wide, tall = side + 128, side + 8
    num_ref[...] = jnp.zeros_like(num_ref)
    wgt_ref[...] = jnp.zeros_like(wgt_ref)
    grad_ref[...] = jnp.zeros_like(grad_ref)
    ssum[...] = jnp.zeros_like(ssum)
    power = jnp.zeros((side, side), F32)
    for m in range(modes):
        power += probe_ref[m, 0] * probe_ref[m, 0] + probe_ref[m, 1] * probe_ref[m, 1]
    pow_ref[...] = jnp.zeros_like(pow_ref)
    pow_ref[:side, :side] = power
    nbuf[...] = jnp.zeros_like(nbuf)

    def visit(s, carry):
        @pl.when(det_ref[s, 0] == 1)
        def _():
            r = det_ref[s, 1]
            c = det_ref[s, 2]
            c0 = pl.multiple_of((c // 128) * 128, 128)
            cc = c - c0
            r0 = pl.multiple_of((r // 8) * 8, 8)
            rr0 = r - r0
            for q in range(2):
                w = ext_ref[q, pl.ds(r0, tall), pl.ds(c0, wide)]
                w = pltpu.roll(w, wide - cc, 1)[:, :side]
                patch[q] = pltpu.roll(w, tall - rr0, 0)[:side]
            ssum[...] += patch[0] * patch[0] + patch[1] * patch[1]
            for m in range(modes):
                pr, pi = probe_ref[m, 0], probe_ref[m, 1]
                xr, xi = patch[0], patch[1]
                ebuf[m, :side] = (pr * xr - pi * xi).astype(BF16)
                ebuf[m, side:] = (pr * xi + pi * xr).astype(BF16)
                half = dot(tab_ref[0], ebuf[m])
                hbuf[m, :, :side] = half[:side].astype(BF16)
                hbuf[m, :, side:] = half[side:].astype(BF16)
                far[m] = dot(hbuf[m], tab_ref[1])
            tot = jnp.zeros((side, side), F32)
            for m in range(modes):
                fr, fi = far[m, :, :side], far[m, :, side:]
                tot += fr * fr + fi * fi
            ratio = amp_ref[s].astype(F32) * lax.rsqrt(jnp.maximum(tot, 0.25))
            xr, xi = patch[0], patch[1]
            nbuf[:, :side, :side] = jnp.zeros((2, side, side), F32)
            for m in range(modes):
                ebuf[m, :side] = (far[m, :, :side] * ratio).astype(BF16)
                ebuf[m, side:] = (far[m, :, side:] * ratio).astype(BF16)
                half = dot(tab_ref[2], ebuf[m])
                hbuf[m, :, :side] = half[:side].astype(BF16)
                hbuf[m, :, side:] = half[side:].astype(BF16)
                ret = dot(hbuf[m], tab_ref[3])
                rr, ri = ret[:, :side], ret[:, side:]
                pr, pi = probe_ref[m, 0], probe_ref[m, 1]
                nbuf[0, :side, :side] += pr * rr + pi * ri
                nbuf[1, :side, :side] += pr * ri - pi * rr
                grad_ref[m, 0] += xr * rr + xi * ri
                grad_ref[m, 1] += xr * ri - xi * rr
            for q in range(2):
                num_ref[q, pl.ds(r0, tall), pl.ds(c0, wide)] += pltpu.roll(pltpu.roll(nbuf[q], rr0, 0), cc, 1)
            wgt_ref[pl.ds(r0, tall), pl.ds(c0, wide)] += pltpu.roll(pltpu.roll(pow_ref[...], rr0, 0), cc, 1)
        return carry
    lax.fori_loop(0, slots, visit, 0)
    for m in range(modes):
        for q in range(2):
            grad_ref[m, q] -= probe_ref[m, q] * ssum[...]

def pattern_call(det, ext, probe, amp):
    slots, side = amp.shape[0], amp.shape[1]
    modes = probe.shape[0]
    tr, ti = tables(side)
    def left(a, b):
        return jnp.concatenate([jnp.concatenate([a, -b], 1), jnp.concatenate([b, a], 1)], 0)
    def right(a, b):
        return jnp.concatenate([jnp.concatenate([a, b], 1), jnp.concatenate([-b, a], 1)], 0)
    tab = jnp.stack([left(tr, ti), right(tr, ti), left(tr, -ti), right(tr, -ti)])
    V = pl.BlockSpec(memory_space=pltpu.VMEM)
    S = pl.BlockSpec(memory_space=pltpu.SMEM)
    big = ext.shape[1]
    return pl.pallas_call(
        functools.partial(kernel, slots, modes, side),
        out_shape=[jax.ShapeDtypeStruct(ext.shape, F32), jax.ShapeDtypeStruct(ext.shape[1:], F32), jax.ShapeDtypeStruct(probe.shape, F32)],
        in_specs=[S, V, V, V, V], out_specs=[V, V, V],
        scratch_shapes=[
            pltpu.VMEM((2, side, side), F32),
            pltpu.VMEM((modes, 2 * side, side), BF16),
            pltpu.VMEM((modes, side, 2 * side), BF16),
            pltpu.VMEM((modes, side, 2 * side), F32),
            pltpu.VMEM((side + 8, side + 128), F32),
            pltpu.VMEM((side, side), F32),
            pltpu.VMEM((2, side + 8, side + 128), F32),
        ],
        compiler_params=pltpu.CompilerParams(vmem_limit_bytes=56 * 2**20),
        name="patterns",
    )(det, ext, probe, amp, tab)


def shifted(value, axis, by):
    size = lax.axis_size(axis)
    pairs = [(i, i + by) for i in range(size) if 0 <= i + by < size]
    return lax.ppermute(value, axis, pairs)


def padded(cells, sides, width):
    for axis, dim in sides:
        count = lax.axis_size(axis)
        ends = count - 1
        head = lax.slice_in_dim(cells, 0, width, axis=dim)
        tail = lax.slice_in_dim(cells, cells.shape[dim] - width, cells.shape[dim], axis=dim)
        cells = jnp.concatenate(
            [
                lax.ppermute(tail, axis, [(i, (i + 1) % count) for i in range(ends)]),
                cells,
                lax.ppermute(head, axis, [((i + 1) % count, i) for i in range(ends)]),
            ],
            axis=dim,
        )
    return cells


def pass_rows(numer_rim, weight_rim, offset_by):
    return shifted((numer_rim, weight_rim), "row", offset_by)


def pass_cols(numer_rim, weight_rim, offset_by):
    return shifted((numer_rim, weight_rim), "col", offset_by)


def settle(numer, weight, tile_side, half_width):
    pattern_side = 2 * half_width
    from_below = pass_rows(numer[:, :half_width], weight[:half_width], -1)
    from_above = pass_rows(numer[:, tile_side + half_width :], weight[tile_side + half_width :], 1)
    numer = numer.at[:, tile_side : tile_side + half_width].add(from_below[0])
    numer = numer.at[:, half_width:pattern_side].add(from_above[0])
    weight = weight.at[tile_side : tile_side + half_width].add(from_below[1])
    weight = weight.at[half_width:pattern_side].add(from_above[1])
    numer = numer[:, half_width : half_width + tile_side]
    weight = weight[half_width : half_width + tile_side]
    from_right = pass_cols(numer[:, :, :half_width], weight[:, :half_width], -1)
    from_left = pass_cols(
        numer[:, :, tile_side + half_width :], weight[:, tile_side + half_width :], 1
    )
    numer = numer.at[:, :, tile_side : tile_side + half_width].add(from_right[0])
    numer = numer.at[:, :, half_width:pattern_side].add(from_left[0])
    weight = weight.at[:, tile_side : tile_side + half_width].add(from_right[1])
    weight = weight.at[:, half_width:pattern_side].add(from_left[1])
    return (
        numer[:, :, half_width : half_width + tile_side],
        weight[:, half_width : half_width + tile_side],
    )


def on_device(object_field, probe, amplitudes, owner, offsets):
    tile_across = lax.axis_size("col")
    held_count = amplitudes.shape[0]
    total_count = lax.axis_size("row") * tile_across * held_count
    tile_side = object_field.shape[1]
    pattern_side = probe.shape[-1]
    half_width = pattern_side // 2
    quarter = tile_across // 4
    capacity = (held_count - 2) // quarter + 1
    slots_all = tile_across * capacity
    extended = padded(object_field, (("row", 1), ("col", 2)), half_width)
    series_held = jnp.arange(held_count, dtype=jnp.int32)
    same_owner = owner[:, None] == owner[None, :]
    earlier = series_held[None, :] < series_held[:, None]
    rank_held = jnp.sum((same_owner & earlier).astype(jnp.int32), axis=1)
    target_slot = owner * capacity + rank_held
    select = target_slot[None, :] == jnp.arange(slots_all, dtype=jnp.int32)[:, None]
    details = jnp.stack([jnp.ones((held_count,), jnp.int32), offsets[:, 0], offsets[:, 1]], axis=1)
    send_details = jnp.sum(select[:, :, None].astype(jnp.int32) * details[None], axis=1)
    flat_amp = amplitudes.reshape(held_count, pattern_side * pattern_side)
    send_amp = jnp.dot(
        select.astype(jnp.bfloat16), flat_amp, preferred_element_type=jnp.float32
    ).astype(jnp.bfloat16)
    got_amp, got_details = (
        lax.all_to_all(send_amp, "col", split_axis=0, concat_axis=0, tiled=True),
        lax.all_to_all(send_details, "col", split_axis=0, concat_axis=0, tiled=True),
    )
    got_amp = got_amp.reshape(slots_all, pattern_side, pattern_side)
    numer, weight, gradient = pattern_call(got_details, extended, probe, got_amp)
    numer_core, weight_core = settle(numer, weight, tile_side, half_width)
    object_out = (object_field + numer_core) / (weight_core + 1.0)
    gradient_total = lax.psum(gradient, ("row", "col"))
    probe_gradient = gradient_total * (1.0 / math.sqrt(total_count))
    return (object_out, probe_gradient)


def solution(mesh):
    return jax.shard_map(
        on_device,
        mesh=mesh,
        in_specs=(
            P(None, "row", "col"),
            P(),
            P(("row", "col"), None, None),
            P(("row", "col")),
            P(("row", "col"), None),
        ),
        out_specs=(P(None, "row", "col"), P()),
        check_vma=False,
    )
```

time: 888 us -> 379 us (0.43)
  matrix products: 281 us -> 0.85 us
  local copies, waits for them, and re-layouts: 178 us -> 32 us
  other arithmetic: 114 us -> 39.3 us
  loops' own time: 56 us -> 0 us
  starting transfers between devices: 57.2 us -> 95.3 us
  Pallas kernels: 0 us -> 17.5 us
    dot_general x193 -> x0, matrix products: 280 us -> none  [the longest x96 154 us: multiply(): jnp.einsum('mjk,kl->mjl', field, table, preferred_element_type=jnp.float32)]
    dynamic_update_slice x24 -> x0, local copies, waits for them, and re-layouts: 116 us -> none  [add_window(): return lax.dynamic_update_slice(whole_array, current + piece, corner)]
    add x38 -> x1, other arithmetic: 74.1 us -> 0.12 us  [on_device(): object_out = (object_field + numer_core) / (weight_core + 1.0)]
    another operation x1 -> x0, loops' own time: 56 us -> none  [on_device(): lax.scan(visit, (numer_start, weight_start, grad_start), (packed_amp, pac...]
    ppermute x8, starting transfers between devices: 31.8 us -> 65.5 us  [shifted(): return lax.ppermute(value, axis, pairs)]
    pallas_call x0 -> x1, Pallas kernels: none -> 17.5 us  [pattern_call(): pl.pallas_call(functools.partial(kernel, slots, modes, side), out_shape=[...]
    mul x12 -> x0, local copies, waits for them, and re-layouts: 16.1 us -> none  [pattern_terms(): exit_re = probe_re * patch_re - probe_im * patch_im]
    all_to_all x1 -> x2, other arithmetic: 2.89 us -> 16.6 us  [on_device(): lax.all_to_all(send_amp, 'col', split_axis=0, concat_axis=0, tiled=True)]
  transfers between devices with their start and end apart: 15 -> 15, of which waited for: 6 -> 7; matrix products, arithmetic and copies ran while one was open for 5% -> 17% of each run, Pallas kernels for 0% -> 0%
where the time goes in v1:
time: 379 us; the launch traced here: 372 us
  waiting for transfers between devices  173 us (46%)
  starting transfers between devices  95.3 us (25%)
  other arithmetic  39.3 us (10%)
  local copies, waits for them, and re-layouts  32 us (8%)
  Pallas kernels  17.5 us (5%)
  between operations  14.3 us (4%)
    psum x1, waiting for transfers between devices, on_device(): gradient_total = lax.psum(gradient, ('row', 'col'))  120 us
    ppermute x8, starting transfers between devices, shifted(): return lax.ppermute(value, axis, pairs)  65.5 us
    ppermute x8, waiting for transfers between devices, shifted(): return lax.ppermute(value, axis, pairs)  22.5 us
    unnamed x24, local copies, waits for them, and re-layouts  21.4 us
    ppermute x2, waiting for transfers between devices, padded(): lax.ppermute(tail, axis, [(i, (i + 1) % count) for i in range(ends)])  20.2 us
    pallas_call x1, Pallas kernels, pattern_call(): pl.pallas_call(functools.partial(kernel, slots, modes, side), out_shape=[...  17.5 us
    all_to_all x2, other arithmetic, on_device(): lax.all_to_all(send_amp, 'col', split_axis=0, concat_axis=0, tiled=True)  16.6 us
    all_to_all x1, starting transfers between devices, on_device(): lax.all_to_all(send_details, 'col', split_axis=0, concat_axis=0, tiled=True)  10.8 us
  transfers between devices with their start and end apart: 15, of which 7 were waited for; matrix products, arithmetic and copies ran while one was open for 17% of the time, Pallas kernels for 0%

profile of v1, /device:TPU:1, one launch (start us, length us, event | category | flops | bytes accessed | tf_op | source)
XLA Modules:
  0.0 372.4 jit_solution(16062440120456135609)
XLA Ops:
  7.2 2.2 fusion.16
  9.3 4.6 %collective-permute-start = (f32[2,128,512]{2,1,0:T(8,128)}, f32[2,128,512]{2,1,0:T(8,128)S(1)}, u32[]{:S(2)}, u32[]{:S(2)}) collective-permute-start(f32[2,128,512]{2,1,0:T(8,128)} %get-tuple-element.115), channel_id=1, source_target_pairs={{0,16},{16,32},{32,48},{48,64},{64,80},{80,96},{96,112},{1,17},{17... | collective-permute-start | bytes 1572872 | tf_op jit(solution)/shard_map/ppermute | solution.py:136
  13.9 0.9 convert_reduce_fusion
  15.9 0.8 fusion
  17.3 2.9 reduce.29
  20.2 4.0 %reshape.250 = bf16[16,2,32768]{2,1,0:T(2,128)(2,1)} reshape(bf16[16,65536]{1,0:T(8,128)(2,1)} %reduce.29) | data formatting | bytes 4194304
  24.2 7.8 %all-to-all-start.1 = ((bf16[16,2,32768]{2,1,0:T(2,128)(2,1)}), bf16[16,2,32768]{2,1,0:T(2,128)(2,1)}, u32[]{:S(2)}, u32[]{:S(2)}) async-start(bf16[16,2,32768]{2,1,0:T(2,128)(2,1)} %reshape.250), calls=%async_computation.1 | async-start | bytes 4194304 | tf_op jit(solution)/shard_map/all_to_all | solution.py:201
  32.0 1.9 collective-permute-start.1
  34.1 8.7 %collective-permute-done.1 = f32[2,128,512]{2,1,0:T(8,128)S(1)} collective-permute-done((f32[2,128,512]{2,1,0:T(8,128)S(1)}, f32[2,128,512]{2,1,0:T(8,128)S(1)}, u32[]{:S(2)}, u32[]{:S(2)}) %collective-permute-start.1) | collective-permute-done | bytes 524320 | tf_op jit(solution)/shard_map/ppermute | solution.py:138
  42.9 1.7 copy-done.2
  44.6 1.2 fusion.13
  45.8 3.2 collective-permute-start.2
  49.1 1.3 collective-permute-start.3
  50.6 0.7 copy.21
  51.2 20.2 %collective-permute-done.2 = f32[2,768,128]{2,1,0:T(8,128)S(1)} collective-permute-done((f32[2,768,128]{2,1,0:T(8,128)}, f32[2,768,128]{2,1,0:T(8,128)S(1)}, u32[]{:S(2)}, u32[]{:S(2)}) %collective-permute-start.2) | collective-permute-done | bytes 786464 | tf_op jit(solution)/shard_map/ppermute | solution.py:136
  71.5 1.8 collective-permute-done.3
  73.3 4.7 %pad_maximum_fusion.ext_ref = f32[2,768,768]{2,1,0:T(8,128)} fusion(f32[2,768,128]{2,1,0:T(8,128)} %collective-permute-done.3, f32[2,768,512]{2,1,0:T(8,128)} %copy-done.2, f32[2,768,128]{2,1,0:T(8,128)S(1)} %collective-permute-done.2), kind=kLoop, calls=%fused_computation.2 | loop fusion | flops 2359296 | bytes 9437184 | tf_op jit(solution)/shard_map/concatenate | solution.py:134
  78.0 10.8 %all-to-all-start = ((s32[16,1,3]{2,1,0:T(1,128)}), s32[16,1,3]{2,1,0:T(1,128)S(1)}, u32[]{:S(2)}, u32[]{:S(2)}) async-start(s32[16,1,3]{2,1,0:T(1,128)} %copy.21), calls=%async_computation | async-start | bytes 16384 | tf_op jit(solution)/shard_map/all_to_all | solution.py:202
  89.0 10.5 %reshape.251 = bf16[16,1,65536]{2,1,0:T(2,128)(2,1)} reshape(bf16[16,2,32768]{2,1,0:T(2,128)(2,1)} %all-to-all-done.1) | data formatting | bytes 4194304
  99.4 13.7 %reduce.26 = bf16[16,65536]{1,0:T(8,128)(2,1)} reduce(bf16[16,1,65536]{2,1,0:T(2,128)(2,1)} %reshape.251, bf16[]{:T(256)} %constant.243), dimensions={1}, to_apply=%all_to_all.17.reduce_sub_computation | reduce | bytes 4194306 | tf_op jit(solution)/shard_map/all_to_all | solution.py:201
  113.1 3.4 copy.27
  117.1 17.5 %patterns.1 = (f32[2,768,768]{2,1,0:T(8,128)}, f32[768,768]{1,0:T(8,128)}, f32[4,2,256,256]{3,2,1,0:T(8,128)}) custom-call(s32[16,3]{1,0:T(8,128)} %bitcast.13, f32[2,768,768]{2,1,0:T(8,128)} %pad_maximum_fusion.ext_ref, f32[4,2,256,256]{3,2,1,0:T(8,128)} %probe_ref.1, bf16[16,256,256]{2,1,0:T(8,128)(2,1)} %bitcast.10, bf16[4,512,512]{2,1,0:T(8,128)(2,1)} %constant.242.tab_ref), custom_call_target="tpu_custom_call" | custom-call | tf_op jit(solution)/shard_map/patterns/pallas_call | solution.py:104
  134.6 1.2 slice.234
  135.8 1.9 collective-permute-start.4
  137.8 1.0 slice.244
  138.8 1.9 collective-permute-start.8
  140.7 12.7 %collective-permute-done.8 = f32[128,768]{1,0:T(8,128)} collective-permute-done((f32[128,768]{1,0:T(8,128)S(1)}, f32[128,768]{1,0:T(8,128)}, u32[]{:S(2)}, u32[]{:S(2)}) %collective-permute-start.8) | collective-permute-done | bytes 393248 | tf_op jit(solution)/shard_map/ppermute | solution.py:125
  153.5 2.1 fusion.15
  155.5 2.0 collective-permute-start.9
  157.6 0.7 compare_reduce_fusion.1
  158.3 0.7 compare_reduce_fusion
  159.0 2.9 fusion.12
  161.9 48.6 %collective-permute-start.5 = (f32[2,128,768]{2,1,0:T(8,128)}, f32[2,128,768]{2,1,0:T(8,128)S(1)}, u32[]{:S(2)}, u32[]{:S(2)}) collective-permute-start(f32[2,128,768]{2,1,0:T(8,128)} %get-tuple-element.106), channel_id=1, source_target_pairs={{0,16},{16,32},{32,48},{48,64},{64,80},{80,96},{96,112},{1,17},{17... | collective-permute-start | bytes 2359304 | tf_op jit(solution)/shard_map/ppermute | solution.py:125
  210.7 1.3 slice.263
  212.6 0.7 fusion.14
  213.3 1.3 collective-permute-start.10
  214.6 4.3 %collective-permute-start.11 = (f32[512,128]{1,0:T(8,128)S(1)}, f32[512,128]{1,0:T(8,128)S(1)}, u32[]{:S(2)}, u32[]{:S(2)}) collective-permute-start(f32[512,128]{1,0:T(8,128)S(1)} %get-tuple-element.110), channel_id=1, source_target_pairs={{0,1},{1,2},{2,3},{3,4},{4,5},{5,6},{6,7},{7,8},{8,9},{9,10},{10,1... | collective-permute-start | bytes 786440 | tf_op jit(solution)/shard_map/ppermute | solution.py:125
  219.0 119.9 %all-reduce.3.cloned.1.call-done = f32[4,2,256,256]{3,2,1,0:T(8,128)} async-done(((f32[4,2,256,256]{3,2,1,0:T(8,128)}), f32[4,2,256,256]{3,2,1,0:T(8,128)}) %all-reduce.3.cloned.1.call-update) | async-done | bytes 2097168 | tf_op jit(solution)/shard_map/psum | solution.py:208
  338.8 3.1 broadcast_multiply_fusion
  341.9 2.2 fusion.2
  344.2 1.4 fusion.11
  345.6 1.4 collective-permute-start.6
  347.1 1.7 fusion.6
  348.8 0.7 fusion.7
  349.6 4.0 %collective-permute-start.7 = (f32[2,512,128]{2,1,0:T(8,128)S(1)}, f32[2,512,128]{2,1,0:T(8,128)S(1)}, u32[]{:S(2)}, u32[]{:S(2)}) collective-permute-start(f32[2,512,128]{2,1,0:T(8,128)S(1)} %get-tuple-element.104), channel_id=1, source_target_pairs={{0,1},{1,2},{2,3},{3,4},{4,5},{5,6},{6,7},{7,8},{8,9},{9,10},{10,1... | collective-permute-start | bytes 1572872 | tf_op jit(solution)/shard_map/ppermute | solution.py:125
  353.9 6.5 %collective-permute-done.6 = f32[2,512,128]{2,1,0:T(8,128)S(1)} collective-permute-done((f32[2,512,128]{2,1,0:T(8,128)S(1)}, f32[2,512,128]{2,1,0:T(8,128)S(1)}, u32[]{:S(2)}, u32[]{:S(2)}) %collective-permute-start.6) | collective-permute-done | bytes 524320 | tf_op jit(solution)/shard_map/ppermute | solution.py:125
  360.4 3.3 collective-permute-done.7
  363.9 1.7 fusion.1
  (41 shorter events, 4.1 us)
Async XLA Ops:
  7.2 8.3 %copy-start.6 = (bf16[4,256,256]{2,1,0:T(8,128)(2,1)S(1)}, bf16[4,256,256]{2,1,0:T(8,128)(2,1)}, u32[]{:S(2)}) copy-start(bf16[4,256,256]{2,1,0:T(8,128)(2,1)} %param.25) | copy-start | bytes 1572868
  9.3 24.6 %collective-permute-start = (f32[2,128,512]{2,1,0:T(8,128)}, f32[2,128,512]{2,1,0:T(8,128)S(1)}, u32[]{:S(2)}, u32[]{:S(2)}) collective-permute-start(f32[2,128,512]{2,1,0:T(8,128)} %get-tuple-element.115), channel_id=1, source_target_pairs={{0,16},{16,32},{32,48},{48,64},{64,80},{80,96},{96,112},{1,17},{17... | collective-permute-start | bytes 1572872 | tf_op jit(solution)/shard_map/ppermute | solution.py:136
  24.2 9.8 %copy-start = (f32[2,512,512]{2,1,0:T(8,128)S(1)}, f32[2,512,512]{2,1,0:T(8,128)}, u32[]{:S(2)}) copy-start(f32[2,512,512]{2,1,0:T(8,128)} %param.23) | copy-start | bytes 6291460
  24.2 53.8 %all-to-all-start.1 = ((bf16[16,2,32768]{2,1,0:T(2,128)(2,1)}), bf16[16,2,32768]{2,1,0:T(2,128)(2,1)}, u32[]{:S(2)}, u32[]{:S(2)}) async-start(bf16[16,2,32768]{2,1,0:T(2,128)(2,1)} %reshape.250), calls=%async_computation.1 | async-start | bytes 4194304 | tf_op jit(solution)/shard_map/all_to_all | solution.py:201
  32.0 10.9 %collective-permute-start.1 = (f32[2,128,512]{2,1,0:T(8,128)S(1)}, f32[2,128,512]{2,1,0:T(8,128)S(1)}, u32[]{:S(2)}, u32[]{:S(2)}) collective-permute-start(f32[2,128,512]{2,1,0:T(8,128)S(1)} %get-tuple-element.114), channel_id=1, source_target_pairs={{16,0},{32,16},{48,32},{64,48},{80,64},{96,80},{112,96},{17,1},{33... | collective-permute-start | bytes 1572872 | tf_op jit(solution)/shard_map/ppermute | solution.py:138
  34.1 16.3 %copy-start.8 = (s32[4,2]{0,1:T(2,128)S(1)}, s32[4,2]{0,1:T(2,128)}, u32[]{:S(2)}) copy-start(s32[4,2]{0,1:T(2,128)} %param.27) | copy-start | bytes 100
  42.9 1.7 copy-start.2
  45.8 25.6 %collective-permute-start.2 = (f32[2,768,128]{2,1,0:T(8,128)}, f32[2,768,128]{2,1,0:T(8,128)S(1)}, u32[]{:S(2)}, u32[]{:S(2)}) collective-permute-start(f32[2,768,128]{2,1,0:T(8,128)} %get-tuple-element.108), channel_id=1, source_target_pairs={{0,1},{1,2},{2,3},{3,4},{4,5},{5,6},{6,7},{7,8},{8,9},{9,10},{10,1... | collective-permute-start | bytes 2359304 | tf_op jit(solution)/shard_map/ppermute | solution.py:136
  49.1 24.2 %collective-permute-start.3 = (f32[2,768,128]{2,1,0:T(8,128)}, f32[2,768,128]{2,1,0:T(8,128)}, u32[]{:S(2)}, u32[]{:S(2)}) collective-permute-start(f32[2,768,128]{2,1,0:T(8,128)} %get-tuple-element.109), channel_id=1, source_target_pairs={{1,0},{2,1},{3,2},{4,3},{5,4},{6,5},{7,6},{8,7},{9,8},{10,9},{11,1... | collective-permute-start | bytes 2359304 | tf_op jit(solution)/shard_map/ppermute | solution.py:138
  78.0 38.6 %all-to-all-start = ((s32[16,1,3]{2,1,0:T(1,128)}), s32[16,1,3]{2,1,0:T(1,128)S(1)}, u32[]{:S(2)}, u32[]{:S(2)}) async-start(s32[16,1,3]{2,1,0:T(1,128)} %copy.21), calls=%async_computation | async-start | bytes 16384 | tf_op jit(solution)/shard_map/all_to_all | solution.py:202
  88.7 250.1 %all-reduce.3.cloned.1.call-start = ((), (), s32[]{:S(2)}) async-start(), calls=%async_computation.2 | async-start | bytes 4194304 | tf_op jit(solution)/shard_map/psum | solution.py:208
  116.5 0.6 copy-start.7
  135.8 23.2 %collective-permute-start.4 = (f32[2,128,768]{2,1,0:T(8,128)S(1)}, f32[2,128,768]{2,1,0:T(8,128)}, u32[]{:S(2)}, u32[]{:S(2)}) collective-permute-start(f32[2,128,768]{2,1,0:T(8,128)S(1)} %slice.234), channel_id=1, source_target_pairs={{16,0},{32,16},{48,32},{64,48},{80,64},{96,80},{112,96},{17,1},{33... | collective-permute-start | bytes 2359304 | tf_op jit(solution)/shard_map/ppermute | solution.py:125
  138.8 14.7 %collective-permute-start.8 = (f32[128,768]{1,0:T(8,128)S(1)}, f32[128,768]{1,0:T(8,128)}, u32[]{:S(2)}, u32[]{:S(2)}) collective-permute-start(f32[128,768]{1,0:T(8,128)S(1)} %slice.244), channel_id=1, source_target_pairs={{16,0},{32,16},{48,32},{64,48},{80,64},{96,80},{112,96},{17,1},{33... | collective-permute-start | bytes 1179656 | tf_op jit(solution)/shard_map/ppermute | solution.py:125
  155.5 55.0 %copy-start.3 = (f32[768,768]{1,0:T(8,128)S(1)}, f32[768,768]{1,0:T(8,128)}, u32[]{:S(2)}) copy-start(f32[768,768]{1,0:T(8,128)} %get-tuple-element.113) | copy-start | bytes 7077892
  155.5 55.0 %collective-permute-start.9 = (f32[128,768]{1,0:T(8,128)S(1)}, f32[128,768]{1,0:T(8,128)S(1)}, u32[]{:S(2)}, u32[]{:S(2)}) collective-permute-start(f32[128,768]{1,0:T(8,128)S(1)} %get-tuple-element.112), channel_id=1, source_target_pairs={{0,16},{16,32},{32,48},{48,64},{64,80},{80,96},{96,112},{1,17},{17... | collective-permute-start | bytes 1179656 | tf_op jit(solution)/shard_map/ppermute | solution.py:125
  161.9 180.0 %collective-permute-start.5 = (f32[2,128,768]{2,1,0:T(8,128)}, f32[2,128,768]{2,1,0:T(8,128)S(1)}, u32[]{:S(2)}, u32[]{:S(2)}) collective-permute-start(f32[2,128,768]{2,1,0:T(8,128)} %get-tuple-element.106), channel_id=1, source_target_pairs={{0,16},{16,32},{32,48},{48,64},{64,80},{80,96},{96,112},{1,17},{17... | collective-permute-start | bytes 2359304 | tf_op jit(solution)/shard_map/ppermute | solution.py:125
  210.6 2.0 copy-start.4
  213.3 133.7 %collective-permute-start.10 = (f32[512,128]{1,0:T(8,128)}, f32[512,128]{1,0:T(8,128)}, u32[]{:S(2)}, u32[]{:S(2)}) collective-permute-start(f32[512,128]{1,0:T(8,128)} %get-tuple-element.111), channel_id=1, source_target_pairs={{1,0},{2,1},{3,2},{4,3},{5,4},{6,5},{7,6},{8,7},{9,8},{10,9},{11,1... | collective-permute-start | bytes 786440 | tf_op jit(solution)/shard_map/ppermute | solution.py:125
  214.6 134.2 %collective-permute-start.11 = (f32[512,128]{1,0:T(8,128)S(1)}, f32[512,128]{1,0:T(8,128)S(1)}, u32[]{:S(2)}, u32[]{:S(2)}) collective-permute-start(f32[512,128]{1,0:T(8,128)S(1)} %get-tuple-element.110), channel_id=1, source_target_pairs={{0,1},{1,2},{2,3},{3,4},{4,5},{5,6},{6,7},{7,8},{8,9},{9,10},{10,1... | collective-permute-start | bytes 786440 | tf_op jit(solution)/shard_map/ppermute | solution.py:125
  341.9 5.1 %copy-start.5 = (f32[512,768]{1,0:T(8,128)S(1)}, f32[512,768]{1,0:T(8,128)}, u32[]{:S(2)}) copy-start(f32[512,768]{1,0:T(8,128)} %slice.263) | copy-start | bytes 4718596
  344.2 9.5 %copy-start.1 = (f32[2,768,768]{2,1,0:T(8,128)S(1)}, f32[2,768,768]{2,1,0:T(8,128)}, u32[]{:S(2)}) copy-start(f32[2,768,768]{2,1,0:T(8,128)} %fusion.2) | copy-start | bytes 14155780
  345.6 14.8 %collective-permute-start.6 = (f32[2,512,128]{2,1,0:T(8,128)S(1)}, f32[2,512,128]{2,1,0:T(8,128)S(1)}, u32[]{:S(2)}, u32[]{:S(2)}) collective-permute-start(f32[2,512,128]{2,1,0:T(8,128)S(1)} %get-tuple-element.105), channel_id=1, source_target_pairs={{1,0},{2,1},{3,2},{4,3},{5,4},{6,5},{7,6},{8,7},{9,8},{10,9},{11,1... | collective-permute-start | bytes 1572872 | tf_op jit(solution)/shard_map/ppermute | solution.py:125
  349.6 14.2 %collective-permute-start.7 = (f32[2,512,128]{2,1,0:T(8,128)S(1)}, f32[2,512,128]{2,1,0:T(8,128)S(1)}, u32[]{:S(2)}, u32[]{:S(2)}) collective-permute-start(f32[2,512,128]{2,1,0:T(8,128)S(1)} %get-tuple-element.104), channel_id=1, source_target_pairs={{0,1},{1,2},{2,3},{3,4},{4,5},{5,6},{6,7},{7,8},{8,9},{9,10},{10,1... | collective-permute-start | bytes 1572872 | tf_op jit(solution)/shard_map/ppermute | solution.py:125
Sparse Core Ops, SparseCore 0:
  140.9 197.9 all-reduce.2

commit v2 on v1

v2 whole, which is shorter than its diff:
```python
import functools
import math

import jax
import jax.numpy as jnp
import numpy as np
from jax import lax
from jax.experimental import pallas as pl
from jax.experimental.pallas import tpu as pltpu
from jax.sharding import PartitionSpec as P

F32, BF16 = jnp.float32, jnp.bfloat16
MESH = pl.DeviceIdType.MESH

def tables(side):
    series = np.arange(side, dtype=np.int32)
    angles = (series[:, None] * series[None, :] % side).astype(np.float32) * np.float32(2.0 * math.pi / side)
    factor = np.float32(1.0 / math.sqrt(side))
    re = jnp.asarray(np.cos(angles) * factor).astype(BF16)
    im = jnp.asarray(-np.sin(angles) * factor).astype(BF16)
    return re, im

def dot(a, b):
    return jnp.dot(a, b, preferred_element_type=F32)

def kernel(slots, modes, side, rows, cols, held, meta_ref, ext_hbm, probe_ref, amp_ref, tab_ref,
           rim_ref, core_ref, grad_ref,
           ext_ref, num_ref, esem, patch, ebuf, hbuf, far, pow_ref, ssum, nbuf):
    wide, tall = side + 128, side + 8
    row, col = lax.axis_index("row"), lax.axis_index("col")
    fetch = pltpu.make_async_copy(ext_hbm, ext_ref, esem)
    fetch.start()
    num_ref[...] = jnp.zeros_like(num_ref)
    grad_ref[...] = jnp.zeros_like(grad_ref)
    ssum[...] = jnp.zeros_like(ssum)
    power = jnp.zeros((side, side), F32)
    for m in range(modes):
        power += probe_ref[m, 0] * probe_ref[m, 0] + probe_ref[m, 1] * probe_ref[m, 1]
    pow_ref[...] = jnp.zeros_like(pow_ref)
    pow_ref[:side, :side] = power
    nbuf[...] = jnp.zeros_like(nbuf)

    fetch.wait()
    big, half = ext_ref.shape[1], side // 2

    @pl.when(row == 0)
    def _():
        ext_ref[:, :half, :] = jnp.zeros((2, half, big), F32)

    @pl.when(row == rows - 1)
    def _():
        ext_ref[:, big - half:, :] = jnp.zeros((2, half, big), F32)

    @pl.when(col == 0)
    def _():
        ext_ref[:, :, :half] = jnp.zeros((2, big, half), F32)

    @pl.when(col == cols - 1)
    def _():
        ext_ref[:, :, big - half:] = jnp.zeros((2, big, half), F32)

    def visit(s, carry):
        live, r, c = jnp.int32(0), jnp.int32(0), jnp.int32(0)
        for h in range(held):
            hit = meta_ref[s, 0, h] == col
            live = jnp.where(hit, 1, live)
            r = jnp.where(hit, meta_ref[s, 0, held + 2 * h], r)
            c = jnp.where(hit, meta_ref[s, 0, held + 2 * h + 1], c)

        @pl.when(live == 1)
        def _():
            c0 = pl.multiple_of((c // 128) * 128, 128)
            cc = c - c0
            r0 = pl.multiple_of((r // 8) * 8, 8)
            rr0 = r - r0
            for q in range(2):
                w = ext_ref[q, pl.ds(r0, tall), pl.ds(c0, wide)]
                w = pltpu.roll(w, wide - cc, 1)[:, :side]
                patch[q] = pltpu.roll(w, tall - rr0, 0)[:side]
            ssum[...] += patch[0] * patch[0] + patch[1] * patch[1]
            for m in range(modes):
                pr, pi = probe_ref[m, 0], probe_ref[m, 1]
                xr, xi = patch[0], patch[1]
                ebuf[m, :side] = (pr * xr - pi * xi).astype(BF16)
                ebuf[m, side:] = (pr * xi + pi * xr).astype(BF16)
                half = dot(tab_ref[0], ebuf[m])
                hbuf[m, :, :side] = half[:side].astype(BF16)
                hbuf[m, :, side:] = half[side:].astype(BF16)
                far[m] = dot(hbuf[m], tab_ref[1])
            tot = jnp.zeros((side, side), F32)
            for m in range(modes):
                fr, fi = far[m, :, :side], far[m, :, side:]
                tot += fr * fr + fi * fi
            ratio = amp_ref[s].astype(F32) * lax.rsqrt(jnp.maximum(tot, 0.25))
            xr, xi = patch[0], patch[1]
            nbuf[:, :side, :side] = jnp.zeros((2, side, side), F32)
            for m in range(modes):
                ebuf[m, :side] = (far[m, :, :side] * ratio).astype(BF16)
                ebuf[m, side:] = (far[m, :, side:] * ratio).astype(BF16)
                half = dot(tab_ref[2], ebuf[m])
                hbuf[m, :, :side] = half[:side].astype(BF16)
                hbuf[m, :, side:] = half[side:].astype(BF16)
                ret = dot(hbuf[m], tab_ref[3])
                rr, ri = ret[:, :side], ret[:, side:]
                pr, pi = probe_ref[m, 0], probe_ref[m, 1]
                nbuf[0, :side, :side] += pr * rr + pi * ri
                nbuf[1, :side, :side] += pr * ri - pi * rr
                grad_ref[pl.ds(2 * m * side, side)] += xr * rr + xi * ri
                grad_ref[pl.ds((2 * m + 1) * side, side)] += xr * ri - xi * rr
            for q in range(2):
                num_ref[q, pl.ds(r0, tall), pl.ds(c0, wide)] += pltpu.roll(pltpu.roll(nbuf[q], rr0, 0), cc, 1)
            num_ref[2, pl.ds(r0, tall), pl.ds(c0, wide)] += pltpu.roll(pltpu.roll(pow_ref[...], rr0, 0), cc, 1)
        return carry
    lax.fori_loop(0, slots, visit, 0)
    for m in range(modes):
        for q in range(2):
            grad_ref[pl.ds((2 * m + q) * side, side)] -= probe_ref[m, q] * ssum[...]
    wgt = num_ref[2]
    for q in range(2):
        num_ref[q] -= ext_ref[q] * wgt
    for q in range(3):
        rim_ref[q] = num_ref[q].astype(BF16)
        core_ref[q] = num_ref[q, half:big - half, half:big - half]

def pattern_call(meta, ext, probe, amp, rows, cols, held):
    slots, side = amp.shape[0], amp.shape[1]
    modes = probe.shape[0]
    tr, ti = tables(side)

    def left(a, b):
        return jnp.concatenate([jnp.concatenate([a, -b], 1), jnp.concatenate([b, a], 1)], 0)

    def right(a, b):
        return jnp.concatenate([jnp.concatenate([a, b], 1), jnp.concatenate([-b, a], 1)], 0)

    tab = jnp.stack([left(tr, ti), right(tr, ti), left(tr, -ti), right(tr, -ti)])
    V = pl.BlockSpec(memory_space=pltpu.VMEM)
    S = pl.BlockSpec(memory_space=pltpu.SMEM)
    A = pl.BlockSpec(memory_space=pl.ANY)
    big = ext.shape[1]
    core = big - side
    return pl.pallas_call(
        functools.partial(kernel, slots, modes, side, rows, cols, held),
        out_shape=[
            jax.ShapeDtypeStruct((3, big, big), BF16),
            jax.ShapeDtypeStruct((3, core, core), F32),
            jax.ShapeDtypeStruct((modes * 2 * side, side), F32),
        ],
        in_specs=[S, A, V, V, V],
        out_specs=[V, V, V],
        scratch_shapes=[
            pltpu.VMEM((2, big, big), F32),
            pltpu.VMEM((3, big, big), F32),
            pltpu.SemaphoreType.DMA,
            pltpu.VMEM((2, side, side), F32),
            pltpu.VMEM((modes, 2 * side, side), BF16),
            pltpu.VMEM((modes, side, 2 * side), BF16),
            pltpu.VMEM((modes, side, 2 * side), F32),
            pltpu.VMEM((side + 8, side + 128), F32),
            pltpu.VMEM((side, side), F32),
            pltpu.VMEM((2, side + 8, side + 128), F32),
        ],
        compiler_params=pltpu.CompilerParams(vmem_limit_bytes=56 * 2**20),
        name="patterns",
    )(meta, ext, probe, amp, tab)


def around(row, col, dr, dc, rows, cols):
    return lax.rem(row + dr + rows, rows), lax.rem(col + dc + cols, cols)


NEAR = [(dr, dc) for dr in (-1, 0, 1) for dc in (-1, 0, 1) if (dr, dc) != (0, 0)]


def span(step, tile, half):
    return {-1: (0, half), 0: (half, tile), 1: (half + tile, half)}[step]


def landing(step, tile, half):
    return {-1: (tile - half, half), 0: (0, tile), 1: (0, half)}[step]


class Sends:
    def __init__(self, send_sem, recv_sem):
        self.send_sem, self.recv_sem, self.at, self.all = send_sem, recv_sem, 0, []

    def __call__(self, src, dst, device):
        n = self.at
        self.at += 1
        copy = pltpu.make_async_remote_copy(
            src_ref=src, dst_ref=dst, send_sem=self.send_sem.at[n], recv_sem=self.recv_sem.at[n],
            device_id=device, device_id_type=MESH)
        copy.start()
        self.all.append(copy)
        return copy

    def finish(self):
        for copy in self.all:
            copy.wait_send()


def greet(devices):
    barrier = pltpu.get_barrier_semaphore()
    for device in devices:
        pl.semaphore_signal(barrier, inc=1, device_id=device, device_id_type=MESH)
    pl.semaphore_wait(barrier, len(devices))


def post_kernel(rows, cols, tile, half, scale, rim_ref, core_ref, obj_ref, grad_ref, out_ref, pg_ref,
                wsum, rims, mate, sum_a, sum_b, got_a, got_b, part_a, part_b, got_a2, got_b2, all16, gsend, grecv):
    row, col = lax.axis_index("row"), lax.axis_index("col")
    core, y = lax.rem(row, 2), row // 2
    ys = rows // 2
    other = (row + 1 - 2 * core, col)
    y_peers = [(lax.rem(y + s, ys) * 2 + core, col) for s in range(1, ys)]
    c_peers = [(row, lax.rem(col + s, cols)) for s in range(1, cols)]
    near = [around(row, col, dr, dc, rows, cols) for dr, dc in NEAR]
    greet([other] + y_peers + c_peers + near)
    send = Sends(gsend, grecv)
    n = grad_ref.shape[0] // 2
    na, nb = n // ys, n // cols
    fin = n // (ys * cols)
    theirs = pl.ds(pl.multiple_of((1 - core) * n, n), n)
    mine = pl.ds(pl.multiple_of(core * n, n), n)
    pair = send(grad_ref.at[theirs], mate, other)
    rim_copies = []
    for i, (dr, dc) in enumerate(NEAR):
        r0, rl = span(dr, tile, half)
        c0, cl = span(dc, tile, half)
        rim_copies.append(send(rim_ref.at[:, r0:r0 + rl, c0:c0 + cl], rims.at[i, :, 0:rl, 0:cl], near[i]))
    pair.wait_recv()
    h = grad_ref[mine, :] + mate[...]
    sum_a[...] = h[:, :128]
    sum_b[...] = h[:, 128:]
    y_at = [lax.rem(y + s, ys) for s in range(1, ys)]
    c_at = [lax.rem(col + s, cols) for s in range(1, cols)]

    def piece(k, size):
        return pl.ds(pl.multiple_of(k * size, size), size)

    a1 = [send(sum_a.at[piece(y_at[s], na)], got_a.at[s], y_peers[s]) for s in range(ys - 1)]
    b1 = [send(sum_b.at[piece(c_at[s], nb)], got_b.at[s], c_peers[s]) for s in range(cols - 1)]
    for c in a1:
        c.wait_recv()
    tot = sum_a[piece(y, na), :]
    for s in range(ys - 1):
        tot += got_a[s]
    part_a[...] = tot
    a2 = [send(part_a.at[piece(c_at[s], fin)], got_a2.at[s], c_peers[s]) for s in range(cols - 1)]
    for c in b1:
        c.wait_recv()
    tot = sum_b[piece(col, nb), :]
    for s in range(cols - 1):
        tot += got_b[s]
    part_b[...] = tot
    b2 = [send(part_b.at[piece(y_at[s], fin)], got_b2.at[s], y_peers[s]) for s in range(ys - 1)]
    for c in a2:
        c.wait_recv()
    tot = part_a[piece(col, fin), :]
    for s in range(cols - 1):
        tot += got_a2[s]
    at_a = piece(y * cols + col, fin)
    all16[core, 0, at_a, :] = (tot * scale).astype(all16.dtype)
    a3 = [send(all16.at[core, 0, at_a], all16.at[core, 0, at_a], p) for p in c_peers]
    for c in b2:
        c.wait_recv()
    tot = part_b[piece(y, fin), :]
    for s in range(ys - 1):
        tot += got_b2[s]
    at_b = piece(col * ys + y, fin)
    all16[core, 1, at_b, :] = (tot * scale).astype(all16.dtype)
    b3 = [send(all16.at[core, 1, at_b], all16.at[core, 1, at_b], p) for p in y_peers]
    for c in a3:
        c.wait_recv()
    big_a = piece(y, na)
    a4 = [send(all16.at[core, 0, big_a], all16.at[core, 0, big_a], p) for p in y_peers]
    for c in b3:
        c.wait_recv()
    big_b = piece(col, nb)
    b4 = [send(all16.at[core, 1, big_b], all16.at[core, 1, big_b], p) for p in c_peers]
    for c in rim_copies:
        c.wait_recv()
    out_ref[...] = core_ref[0:2]
    wsum[...] = core_ref[2]
    for i, (dr, dc) in enumerate(NEAR):
        r0, rl = landing(dr, tile, half)
        c0, cl = landing(dc, tile, half)
        keep = (row != -1) & (col != -1)
        if dr:
            keep = keep & (row != (0 if dr == 1 else rows - 1))
        if dc:
            keep = keep & (col != (0 if dc == 1 else cols - 1))

        @pl.when(keep)
        def _(i=i, r0=r0, rl=rl, c0=c0, cl=cl):
            for q in range(2):
                out_ref[q, r0:r0 + rl, c0:c0 + cl] += rims[i, q, 0:rl, 0:cl].astype(F32)
            wsum[r0:r0 + rl, c0:c0 + cl] += rims[i, 2, 0:rl, 0:cl].astype(F32)

    for q in range(2):
        out_ref[q] = obj_ref[q] + out_ref[q] / (wsum[...] + 1.0)
    for c in a4 + b4:
        c.wait_recv()
    last = send(all16.at[core], all16.at[core], other)
    for k in range(2):
        pg_ref[mine, 128 * k:128 * (k + 1)] = all16[core, k].astype(F32)
    last.wait_recv()
    for k in range(2):
        pg_ref[theirs, 128 * k:128 * (k + 1)] = all16[1 - core, k].astype(F32)
    send.finish()


def post_call(rim, core, obj, grad, rows, cols, scale):
    tile, wide = obj.shape[1], rim.shape[1]
    half = (wide - tile) // 2
    total = grad.shape[0]
    ys, n = rows // 2, total // 2
    na, nb, fin = n // ys, n // cols, n // (ys * cols)
    copies = 1 + 8 + 2 * (ys - 1) + 2 * (cols - 1) + 2 * (ys - 1) + 2 * (cols - 1) + 1
    V = pl.BlockSpec(memory_space=pltpu.VMEM)
    A = pl.BlockSpec(memory_space=pl.ANY)
    return pl.pallas_call(
        functools.partial(post_kernel, rows, cols, tile, half, scale),
        out_shape=[jax.ShapeDtypeStruct(obj.shape, F32), jax.ShapeDtypeStruct(grad.shape, F32)],
        in_specs=[A, V, V, V],
        out_specs=[V, V],
        scratch_shapes=[
            pltpu.VMEM((tile, tile), F32),
            pltpu.VMEM((8, 3, tile, tile), BF16),
            pltpu.VMEM((n, 256), F32),
            pltpu.VMEM((n, 128), F32),
            pltpu.VMEM((n, 128), F32),
            pltpu.VMEM((ys - 1, na, 128), F32),
            pltpu.VMEM((cols - 1, nb, 128), F32),
            pltpu.VMEM((na, 128), F32),
            pltpu.VMEM((nb, 128), F32),
            pltpu.VMEM((cols - 1, fin, 128), F32),
            pltpu.VMEM((ys - 1, fin, 128), F32),
            pltpu.VMEM((2, 2, n, 128), BF16),
            pltpu.SemaphoreType.DMA((copies,)),
            pltpu.SemaphoreType.DMA((copies,)),
        ],
        compiler_params=pltpu.CompilerParams(collective_id=1, has_side_effects=True, vmem_limit_bytes=56 * 2**20),
        name="post",
    )(rim, core, obj, grad)


def pre_kernel(rows, cols, tile, half, owner_ref, mine_ref, amp_ref, obj_ref, ext_ref, meta_ref, amps_ref,
               slots, gsend, grecv, lsem):
    row, col = lax.axis_index("row"), lax.axis_index("col")
    near = [around(row, col, dr, dc, rows, cols) for dr, dc in NEAR]
    c_peers = [(row, lax.rem(col + s, cols)) for s in range(1, cols)]
    held = amp_ref.shape[0]
    greet(c_peers + near)
    send = Sends(gsend, grecv)
    got = []
    for s in range(cols - 1):
        got.append(send(mine_ref, meta_ref.at[col], c_peers[s]))
    for i, (dr, dc) in enumerate(NEAR):
        r0, rl = {-1: (0, half), 0: (0, tile), 1: (tile - half, half)}[dr]
        c0, cl = {-1: (0, half), 0: (0, tile), 1: (tile - half, half)}[dc]
        tr, _ = span(-dr, tile, half)
        tc, _ = span(-dc, tile, half)
        got.append(send(obj_ref.at[:, r0:r0 + rl, c0:c0 + cl], ext_ref.at[:, tr:tr + rl, tc:tc + cl], near[i]))
    local = [
        pltpu.make_async_copy(obj_ref, ext_ref.at[:, half:half + tile, half:half + tile], lsem.at[0]),
        pltpu.make_async_copy(mine_ref, meta_ref.at[col], lsem.at[1]),
        pltpu.make_async_copy(slots.at[0], amps_ref.at[col], lsem.at[2]),
    ]
    local[0].start()
    local[1].start()
    for s in range(cols):
        to = lax.rem(col + s, cols)
        which = jnp.int32(0)
        for h in range(1, held):
            which = jnp.where(owner_ref[h] == to, h, which)
        slots[s] = amp_ref[which]
        if s == 0:
            local[2].start()
        else:
            got.append(send(slots.at[s], amps_ref.at[col], c_peers[s - 1]))
    for c in got:
        c.wait_recv()
    for c in local:
        c.wait()
    send.finish()


def pre_call(owner, mine, amp, obj, rows, cols):
    tile = obj.shape[1]
    half = amp.shape[1] // 2
    wide = tile + 2 * half
    copies = 8 + 2 * (cols - 1)
    V = pl.BlockSpec(memory_space=pltpu.VMEM)
    A = pl.BlockSpec(memory_space=pl.ANY)
    S = pl.BlockSpec(memory_space=pltpu.SMEM)
    return pl.pallas_call(
        functools.partial(pre_kernel, rows, cols, tile, half),
        out_shape=[
            jax.ShapeDtypeStruct((2, wide, wide), F32),
            jax.ShapeDtypeStruct((cols, 1, 128), jnp.int32),
            jax.ShapeDtypeStruct((cols,) + amp.shape[1:], BF16),
        ],
        in_specs=[S, V, V, A],
        out_specs=[A, A, A],
        scratch_shapes=[
            pltpu.VMEM((cols,) + amp.shape[1:], BF16),
            pltpu.SemaphoreType.DMA((copies,)),
            pltpu.SemaphoreType.DMA((copies,)),
            pltpu.SemaphoreType.DMA((3,)),
        ],
        compiler_params=pltpu.CompilerParams(collective_id=0, has_side_effects=True, vmem_limit_bytes=32 * 2**20),
        name="pre",
    )(owner, mine, amp, obj)


def on_device(object_field, probe, amplitudes, owner, offsets):
    rows, cols = lax.axis_size("row"), lax.axis_size("col")
    held = amplitudes.shape[0]
    mine = jnp.concatenate([owner, offsets.reshape(-1), jnp.zeros((128 - 3 * held,), jnp.int32)])[None]
    ext, meta, amps = pre_call(owner, mine, amplitudes, object_field, rows, cols)
    rim, core, grad = pattern_call(meta, ext, probe, amps, rows, cols, held)
    scale = 1.0 / math.sqrt(rows * cols * held)
    object_out, gradient = post_call(rim, core, object_field, grad, rows, cols, scale)
    return (object_out, gradient.reshape(probe.shape))


def solution(mesh):
    return jax.shard_map(
        on_device,
        mesh=mesh,
        in_specs=(
            P(None, "row", "col"),
            P(),
            P(("row", "col"), None, None),
            P(("row", "col")),
            P(("row", "col"), None),
        ),
        out_specs=(P(None, "row", "col"), P()),
        check_vma=False,
    )
```

time: 379 us -> 190 us (0.50); the launches traced: 372 us -> 189 us
  waiting for transfers between devices: 173 us -> 0 us
  Pallas kernels: 17.5 us -> 175 us
  starting transfers between devices: 95.3 us -> 0 us
  other arithmetic: 39.3 us -> 0.73 us
  local copies, waits for them, and re-layouts: 32 us -> 12.7 us
  between operations: 14.3 us -> 0.68 us
    pallas_call x1 -> x3, Pallas kernels: 17.5 us -> 175 us  [the longest x1 62.1 us: pattern_call(): pl.pallas_call(functools.partial(kernel, slots, modes, side, rows, cols,...]
    psum x1 -> x0, waiting for transfers between devices: 120 us -> none  [on_device(): gradient_total = lax.psum(gradient, ('row', 'col'))]
    ppermute x12 -> x0, starting transfers between devices: 76.6 us -> none  [the longest x8 65.5 us: shifted(): return lax.ppermute(value, axis, pairs)]
    ppermute x12 -> x0, waiting for transfers between devices: 53.2 us -> none  [the longest x8 22.5 us: shifted(): return lax.ppermute(value, axis, pairs)]
    all_to_all x2 -> x0, starting transfers between devices: 18.6 us -> none  [the longest x1 10.8 us: on_device(): lax.all_to_all(send_details, 'col', split_axis=0, concat_axis=0, tiled=True)]
    all_to_all x2 -> x0, other arithmetic: 16.6 us -> none  [on_device(): lax.all_to_all(send_amp, 'col', split_axis=0, concat_axis=0, tiled=True)]
    slice x8 -> x0, local copies, waits for them, and re-layouts: 9.33 us -> none  [the longest x2 2.21 us: settle(): from_below = pass_rows(numer[:, :half_width], weight[:half_width], -1)]
    unnamed x24 -> x17, local copies, waits for them, and re-layouts: 21.4 us -> 12.6 us
  transfers between devices with their start and end apart: 15 -> 0, of which waited for: 7 -> 0; matrix products, arithmetic and copies ran while one was open for 17% -> 0% of each run, Pallas kernels for 0% -> 0%
where the time goes in v2:
time: 190 us; the launch traced here: 189 us
  Pallas kernels  175 us (92%)
  local copies, waits for them, and re-layouts  12.7 us (7%)
    pallas_call x1, Pallas kernels, pattern_call(): pl.pallas_call(functools.partial(kernel, slots, modes, side, rows, cols,...  62.1 us
    pallas_call x1, Pallas kernels, post_call(): pl.pallas_call(functools.partial(post_kernel, rows, cols, tile, half, sca...  57.3 us
    pallas_call x1, Pallas kernels, pre_call(): pl.pallas_call(functools.partial(pre_kernel, rows, cols, tile, half), out...  55.9 us
    unnamed x17, local copies, waits for them, and re-layouts  12.6 us

profile of v2, /device:TPU:1, one launch (start us, length us, event | category | flops | bytes accessed | tf_op | source)
XLA Modules:
  0.0 189.5 jit_solution(8784195268025693953)
XLA Ops:
  0.6 0.8 copy.10
  1.4 0.1 reshape.10
  1.5 0.7 add_bitcast_fusion.mine_ref
  2.2 0.0 copy-start
  2.2 1.6 copy-done
  3.8 0.0 copy-start.3
  3.8 1.0 copy-done.3
  4.8 0.0 copy-start.5
  4.9 0.7 copy-done.5
  5.5 55.9 %pre.1 = (f32[2,768,768]{2,1,0:T(8,128)S(1)}, s32[16,1,128]{2,1,0:T(1,128)S(1)}, bf16[16,256,256]{2,1,0:T(8,128)(2,1)S(1)}) custom-call(s32[4]{0:T(128)S(1)} %copy-done.5, s32[1,128]{1,0:T(1,128)S(1)} %add_bitcast_fusion.mine_ref, bf16[4,256,256]{2,1,0:T(8,128)(2,1)S(1)} %copy-done.3, f32[2,512,512]{2,1,0:T(8,128)S(1)} %copy-done), custom_call_target="tpu_custom_call" | custom-call | tf_op jit(solution)/shard_map/pre/pallas_call | solution.py:397
  61.4 0.0 copy-start.1
  61.4 2.1 %copy-done.1 = f32[2,768,768]{2,1,0:T(8,128)} copy-done((f32[2,768,768]{2,1,0:T(8,128)}, f32[2,768,768]{2,1,0:T(8,128)S(1)}, u32[]{:S(2)}) %copy-start.1) | copy-done | bytes 4718616
  63.5 0.0 copy-start.2
  63.5 1.3 copy-done.2
  64.8 0.0 copy-start.4
  64.8 0.6 copy-done.4
  65.4 62.1 %patterns.1 = (bf16[3,768,768]{2,1,0:T(8,128)(2,1)}, f32[3,512,512]{2,1,0:T(8,128)}, f32[2048,256]{1,0:T(8,128)}) custom-call(s32[16,1,128]{2,1,0:T(1,128)} %copy-done.4, f32[2,768,768]{2,1,0:T(8,128)} %copy-done.1, f32[4,2,256,256]{3,2,1,0:T(8,128)} %probe_ref.1, bf16[16,256,256]{2,1,0:T(8,128)(2,1)} %copy-done.2, bf16[4,512,512]{2,1,0:T(8,128)(2,1)} %constant.22.tab_ref), custom_call_target="tpu_custom_call" | custom-call | tf_op jit(solution)/shard_map/patterns/pallas_call | solution.py:142
  127.6 57.3 %post.1 = (f32[2,512,512]{2,1,0:T(8,128)}, f32[2048,256]{1,0:T(8,128)}) custom-call(bf16[3,768,768]{2,1,0:T(8,128)(2,1)} %get-tuple-element.13.rim_ref, f32[3,512,512]{2,1,0:T(8,128)} %get-tuple-element.14.core_ref, f32[2,512,512]{2,1,0:T(8,128)} %obj_ref.3, f32[2048,256]{1,0:T(8,128)} %get-tuple-element.15.grad_ref), custom_call_target="tpu_custom_call" | custom-call | tf_op jit(solution)/shard_map/post/pallas_call | solution.py:322
  184.9 0.0 copy-start.6
  184.9 3.2 %copy.13 = f32[2,512,512]{2,1,0:T(8,128)} copy(f32[2,512,512]{2,1,0:T(8,128)} %get-tuple-element.20) | data formatting | bytes 4194304
  188.1 0.0 copy-done.6
  188.2 1.3 copy.14
  (1 shorter events, 0.0 us)
Async XLA Ops:
  2.2 1.6 copy-start
  3.8 1.0 copy-start.3
  4.8 0.7 copy-start.5
  61.4 2.1 %copy-start.1 = (f32[2,768,768]{2,1,0:T(8,128)}, f32[2,768,768]{2,1,0:T(8,128)S(1)}, u32[]{:S(2)}) copy-start(f32[2,768,768]{2,1,0:T(8,128)S(1)} %get-tuple-element.11.ext_hbm) | copy-start | bytes 14155780
  63.5 1.3 copy-start.2
  64.8 0.6 copy-start.4
  184.9 3.2 %copy-start.6 = (f32[2048,256]{1,0:T(8,128)S(1)}, f32[2048,256]{1,0:T(8,128)}, u32[]{:S(2)}) copy-start(f32[2048,256]{1,0:T(8,128)} %get-tuple-element.17) | copy-start | bytes 6291460

commit v3 on v2

v3 whole, which is shorter than its diff:
```python
import functools
import math

import jax
import jax.numpy as jnp
import numpy as np
from jax import lax
from jax.experimental import pallas as pl
from jax.experimental.pallas import tpu as pltpu
from jax.sharding import PartitionSpec as P

F32, BF16 = jnp.float32, jnp.bfloat16
MESH = pl.DeviceIdType.MESH

def tables(side):
    series = np.arange(side, dtype=np.int32)
    angles = (series[:, None] * series[None, :] % side).astype(np.float32) * np.float32(2.0 * math.pi / side)
    factor = np.float32(1.0 / math.sqrt(side))
    re = jnp.asarray(np.cos(angles) * factor).astype(BF16)
    im = jnp.asarray(-np.sin(angles) * factor).astype(BF16)
    return re, im

def dot(a, b):
    return jnp.dot(a, b, preferred_element_type=F32)

def around(row, col, dr, dc, rows, cols):
    return lax.rem(row + dr + rows, rows), lax.rem(col + dc + cols, cols)


NEAR = [(dr, dc) for dr in (-1, 0, 1) for dc in (-1, 0, 1) if (dr, dc) != (0, 0)]


def span(step, tile, half):
    return {-1: (0, half), 0: (half, tile), 1: (half + tile, half)}[step]


def landing(step, tile, half):
    return {-1: (tile - half, half), 0: (0, tile), 1: (0, half)}[step]


class Sends:
    def __init__(self, send_sem, recv_sem):
        self.send_sem, self.recv_sem, self.at, self.all = send_sem, recv_sem, 0, []

    def __call__(self, src, dst, device):
        n = self.at
        self.at += 1
        copy = pltpu.make_async_remote_copy(
            src_ref=src, dst_ref=dst, send_sem=self.send_sem.at[n], recv_sem=self.recv_sem.at[n],
            device_id=device, device_id_type=MESH)
        copy.start()
        self.all.append(copy)
        return copy

    def finish(self):
        for copy in self.all:
            copy.wait_send()


def greet(devices):
    barrier = pltpu.get_barrier_semaphore()
    for device in devices:
        pl.semaphore_signal(barrier, inc=1, device_id=device, device_id_type=MESH)
    pl.semaphore_wait(barrier, len(devices))


def post_kernel(rows, cols, tile, half, scale, rim_ref, core_ref, obj_ref, grad_ref, out_ref, all16,
                wsum, rims, mate, sum_a, sum_b, got_a, got_b, part_a, part_b, got_a2, got_b2, gsend, grecv):
    row, col = lax.axis_index("row"), lax.axis_index("col")
    core, y = lax.rem(row, 2), row // 2
    ys = rows // 2
    other = (row + 1 - 2 * core, col)
    y_peers = [(lax.rem(y + s, ys) * 2 + core, col) for s in range(1, ys)]
    c_peers = [(row, lax.rem(col + s, cols)) for s in range(1, cols)]
    near = [around(row, col, dr, dc, rows, cols) for dr, dc in NEAR]
    greet([other] + y_peers + c_peers + near)
    send = Sends(gsend, grecv)
    n = grad_ref.shape[0] // 2
    na, nb = n // ys, n // cols
    fin = n // (ys * cols)
    theirs = pl.ds(pl.multiple_of((1 - core) * n, n), n)
    mine = pl.ds(pl.multiple_of(core * n, n), n)
    pair = send(grad_ref.at[theirs], mate, other)
    rim_copies = []
    for i, (dr, dc) in enumerate(NEAR):
        r0, rl = span(dr, tile, half)
        c0, cl = span(dc, tile, half)
        rim_copies.append(send(rim_ref.at[:, r0:r0 + rl, c0:c0 + cl], rims.at[i, :, 0:rl, 0:cl], near[i]))
    pair.wait_recv()
    h = grad_ref[mine, :] + mate[...]
    sum_a[...] = h[:, :128]
    sum_b[...] = h[:, 128:]
    y_at = [lax.rem(y + s, ys) for s in range(1, ys)]
    c_at = [lax.rem(col + s, cols) for s in range(1, cols)]

    def piece(k, size):
        return pl.ds(pl.multiple_of(k * size, size), size)

    a1 = [send(sum_a.at[piece(y_at[s], na)], got_a.at[s], y_peers[s]) for s in range(ys - 1)]
    b1 = [send(sum_b.at[piece(c_at[s], nb)], got_b.at[s], c_peers[s]) for s in range(cols - 1)]
    for c in a1:
        c.wait_recv()
    tot = sum_a[piece(y, na), :]
    for s in range(ys - 1):
        tot += got_a[s]
    part_a[...] = tot
    a2 = [send(part_a.at[piece(c_at[s], fin)], got_a2.at[s], c_peers[s]) for s in range(cols - 1)]
    for c in b1:
        c.wait_recv()
    tot = sum_b[piece(col, nb), :]
    for s in range(cols - 1):
        tot += got_b[s]
    part_b[...] = tot
    b2 = [send(part_b.at[piece(y_at[s], fin)], got_b2.at[s], y_peers[s]) for s in range(ys - 1)]
    for c in a2:
        c.wait_recv()
    tot = part_a[piece(col, fin), :]
    for s in range(cols - 1):
        tot += got_a2[s]
    at_a = piece(y * cols + col, fin)
    all16[core, 0, at_a, :] = (tot * scale).astype(all16.dtype)
    a3 = [send(all16.at[core, 0, at_a], all16.at[core, 0, at_a], p) for p in c_peers]
    for c in b2:
        c.wait_recv()
    tot = part_b[piece(y, fin), :]
    for s in range(ys - 1):
        tot += got_b2[s]
    at_b = piece(col * ys + y, fin)
    all16[core, 1, at_b, :] = (tot * scale).astype(all16.dtype)
    b3 = [send(all16.at[core, 1, at_b], all16.at[core, 1, at_b], p) for p in y_peers]
    for c in a3:
        c.wait_recv()
    big_a = piece(y, na)
    a4 = [send(all16.at[core, 0, big_a], all16.at[core, 0, big_a], p) for p in y_peers]
    for c in b3:
        c.wait_recv()
    big_b = piece(col, nb)
    b4 = [send(all16.at[core, 1, big_b], all16.at[core, 1, big_b], p) for p in c_peers]
    for c in rim_copies:
        c.wait_recv()
    out_ref[...] = core_ref[0:2]
    wsum[...] = core_ref[2]
    for i, (dr, dc) in enumerate(NEAR):
        r0, rl = landing(dr, tile, half)
        c0, cl = landing(dc, tile, half)
        keep = (row != -1) & (col != -1)
        if dr:
            keep = keep & (row != (0 if dr == 1 else rows - 1))
        if dc:
            keep = keep & (col != (0 if dc == 1 else cols - 1))

        @pl.when(keep)
        def _(i=i, r0=r0, rl=rl, c0=c0, cl=cl):
            for q in range(2):
                out_ref[q, r0:r0 + rl, c0:c0 + cl] += rims[i, q, 0:rl, 0:cl].astype(F32)
            wsum[r0:r0 + rl, c0:c0 + cl] += rims[i, 2, 0:rl, 0:cl].astype(F32)

    for q in range(2):
        out_ref[q] = obj_ref[q] + out_ref[q] / (wsum[...] + 1.0)
    for c in a4 + b4:
        c.wait_recv()
    last = send(all16.at[core], all16.at[core], other)
    last.wait_recv()
    send.finish()


def post_call(rim, core, obj, grad, rows, cols, scale):
    tile, wide = obj.shape[1], rim.shape[1]
    half = (wide - tile) // 2
    total = grad.shape[0]
    ys, n = rows // 2, total // 2
    na, nb, fin = n // ys, n // cols, n // (ys * cols)
    copies = 1 + 8 + 2 * (ys - 1) + 2 * (cols - 1) + 2 * (ys - 1) + 2 * (cols - 1) + 1
    V = pl.BlockSpec(memory_space=pltpu.VMEM)
    A = pl.BlockSpec(memory_space=pl.ANY)
    return pl.pallas_call(
        functools.partial(post_kernel, rows, cols, tile, half, scale),
        out_shape=[jax.ShapeDtypeStruct(obj.shape, F32), jax.ShapeDtypeStruct((2, 2, n, 128), BF16)],
        in_specs=[A, V, V, V],
        out_specs=[V, V],
        scratch_shapes=[
            pltpu.VMEM((tile, tile), F32),
            pltpu.VMEM((8, 3, tile, tile), BF16),
            pltpu.VMEM((n, 256), F32),
            pltpu.VMEM((n, 128), F32),
            pltpu.VMEM((n, 128), F32),
            pltpu.VMEM((ys - 1, na, 128), F32),
            pltpu.VMEM((cols - 1, nb, 128), F32),
            pltpu.VMEM((na, 128), F32),
            pltpu.VMEM((nb, 128), F32),
            pltpu.VMEM((cols - 1, fin, 128), F32),
            pltpu.VMEM((ys - 1, fin, 128), F32),
            pltpu.SemaphoreType.DMA((copies,)),
            pltpu.SemaphoreType.DMA((copies,)),
        ],
        compiler_params=pltpu.CompilerParams(collective_id=1, has_side_effects=True, vmem_limit_bytes=56 * 2**20),
        name="post",
    )(rim, core, obj, grad)


def pre_kernel(rows, cols, tile, half, owner_ref, offsets_ref, obj_ref, ext_ref, meta_ref, mine, gsend, grecv, lsem):
    row, col = lax.axis_index("row"), lax.axis_index("col")
    near = [around(row, col, dr, dc, rows, cols) for dr, dc in NEAR]
    c_peers = [(row, lax.rem(col + s, cols)) for s in range(1, cols)]
    held = owner_ref.shape[0]
    core = pltpu.make_async_copy(obj_ref, ext_ref.at[:, half:half + tile, half:half + tile], lsem.at[0])
    core.start()
    lane = lax.broadcasted_iota(jnp.int32, (1, 128), 1)
    note = jnp.zeros((1, 128), jnp.int32)
    for h in range(held):
        note = jnp.where(lane == h, owner_ref[h], note)
        for k in range(2):
            note = jnp.where(lane == held + 2 * h + k, offsets_ref[h, k], note)
    mine[...] = note
    greet(c_peers + near)
    send = Sends(gsend, grecv)
    got = []
    for i, (dr, dc) in enumerate(NEAR):
        r0, rl = {-1: (0, half), 0: (0, tile), 1: (tile - half, half)}[dr]
        c0, cl = {-1: (0, half), 0: (0, tile), 1: (tile - half, half)}[dc]
        tr, _ = span(-dr, tile, half)
        tc, _ = span(-dc, tile, half)
        got.append(send(obj_ref.at[:, r0:r0 + rl, c0:c0 + cl], ext_ref.at[:, tr:tr + rl, tc:tc + cl], near[i]))
    for s in range(cols - 1):
        got.append(send(mine, meta_ref.at[col], c_peers[s]))
    own = pltpu.make_async_copy(mine, meta_ref.at[col], lsem.at[1])
    own.start()
    for c in got:
        c.wait_recv()
    core.wait()
    own.wait()
    send.finish()


def pre_call(owner, offsets, obj, side, rows, cols):
    tile, half = obj.shape[1], side // 2
    big = tile + side
    copies = 8 + cols - 1
    A = pl.BlockSpec(memory_space=pl.ANY)
    S = pl.BlockSpec(memory_space=pltpu.SMEM)
    return pl.pallas_call(
        functools.partial(pre_kernel, rows, cols, tile, half),
        out_shape=[jax.ShapeDtypeStruct((2, big, big), F32), jax.ShapeDtypeStruct((cols, 1, 128), jnp.int32)],
        in_specs=[S, S, A],
        out_specs=[A, A],
        scratch_shapes=[
            pltpu.VMEM((1, 128), jnp.int32),
            pltpu.SemaphoreType.DMA((copies,)),
            pltpu.SemaphoreType.DMA((copies,)),
            pltpu.SemaphoreType.DMA((2,)),
        ],
        compiler_params=pltpu.CompilerParams(collective_id=0, has_side_effects=True),
        name="pre",
    )(owner, offsets, obj)


def cut_kernel(rows, cols, tile, half, held, meta_ref, ext_hbm, patch_hbm, list_ref, ext, patch, esem, osem):
    row, col = lax.axis_index("row"), lax.axis_index("col")
    side = 2 * half
    big, tall, wide, most = tile + side, side + 8, side + 128, list_ref.shape[0]
    fetch = pltpu.make_async_copy(ext_hbm, ext, esem)
    fetch.start()

    def clear(p, carry):
        for k in range(4):
            list_ref[p, k] = 0
        return carry

    lax.fori_loop(0, most, clear, 0)

    def scan(s, count):
        live, r, c = jnp.int32(0), jnp.int32(0), jnp.int32(0)
        for h in range(held):
            hit = meta_ref[s, 0, h] == col
            live = jnp.where(hit, 1, live)
            r = jnp.where(hit, meta_ref[s, 0, held + 2 * h], r)
            c = jnp.where(hit, meta_ref[s, 0, held + 2 * h + 1], c)

        @pl.when((live == 1) & (count < most))
        def _():
            list_ref[count, 0] = 1
            list_ref[count, 1] = s
            list_ref[count, 2] = r
            list_ref[count, 3] = c
        return count + live

    lax.fori_loop(0, cols, scan, 0)
    fetch.wait()

    @pl.when(row == 0)
    def _():
        ext[:, :half, :] = jnp.zeros((2, half, big), F32)

    @pl.when(row == rows - 1)
    def _():
        ext[:, big - half:, :] = jnp.zeros((2, half, big), F32)

    @pl.when(col == 0)
    def _():
        ext[:, :, :half] = jnp.zeros((2, big, half), F32)

    @pl.when(col == cols - 1)
    def _():
        ext[:, :, big - half:] = jnp.zeros((2, big, half), F32)

    def out(p):
        return pltpu.make_async_copy(patch.at[p], patch_hbm.at[p], osem.at[p])

    def visit(p, carry):
        @pl.when(list_ref[p, 0] == 1)
        def _():
            r, c = list_ref[p, 2], list_ref[p, 3]
            c0 = pl.multiple_of((c // 128) * 128, 128)
            r0 = pl.multiple_of((r // 8) * 8, 8)
            for q in range(2):
                w = ext[q, pl.ds(r0, tall), pl.ds(c0, wide)]
                w = pltpu.roll(w, wide - (c - c0), 1)[:, :side]
                patch[p, q] = pltpu.roll(w, tall - (r - r0), 0)[:side]

        @pl.when(list_ref[p, 0] == 0)
        def _():
            patch[p] = jnp.zeros((2, side, side), F32)

        out(p).start()
        return carry

    lax.fori_loop(0, most, visit, 0)

    def drain(p, carry):
        out(p).wait()
        return carry

    lax.fori_loop(0, most, drain, 0)


def cut_call(meta, ext, tile, rows, cols, held, most):
    big = ext.shape[1]
    side = big - tile
    A = pl.BlockSpec(memory_space=pl.ANY)
    S = pl.BlockSpec(memory_space=pltpu.SMEM)
    return pl.pallas_call(
        functools.partial(cut_kernel, rows, cols, tile, side // 2, held),
        out_shape=[jax.ShapeDtypeStruct((most, 2, side, side), F32), jax.ShapeDtypeStruct((most, 4), jnp.int32)],
        in_specs=[S, A],
        out_specs=[A, S],
        scratch_shapes=[
            pltpu.VMEM((2, big, big), F32),
            pltpu.VMEM((most, 2, side, side), F32),
            pltpu.SemaphoreType.DMA,
            pltpu.SemaphoreType.DMA((most,)),
        ],
        compiler_params=pltpu.CompilerParams(vmem_limit_bytes=32 * 2**20),
        name="cut",
    )(meta, ext)


def main_kernel(rows, cols, list_ref, owner_ref, amp_hbm, patch_hbm, probe_hbm, tab_hbm,
                placed_ref, grad_ref, pow_ref,
                slots, amps, amp, probe, tab, patch, far, total, ebuf, hbuf, ssum,
                gsend, grecv, lsem):
    row, col = lax.axis_index("row"), lax.axis_index("col")
    c_peers = [(row, lax.rem(col + s, cols)) for s in range(1, cols)]
    held, side, modes, most = amp.shape[0], amp.shape[1], probe.shape[0], patch.shape[0]
    local = [
        pltpu.make_async_copy(amp_hbm, amp, lsem.at[0]),
        pltpu.make_async_copy(probe_hbm, probe, lsem.at[1]),
        pltpu.make_async_copy(tab_hbm, tab, lsem.at[2]),
        pltpu.make_async_copy(patch_hbm, patch, lsem.at[3]),
    ]
    for copy in local:
        copy.start()
    greet(c_peers)
    send = Sends(gsend, grecv)
    local[0].wait()
    amp_copies = []
    for s in range(cols):
        to = lax.rem(col + s, cols)
        which = jnp.int32(0)
        for h in range(1, held):
            which = jnp.where(owner_ref[h] == to, h, which)
        if s == 0:
            amps[col] = amp[which]
        else:
            slots[s] = amp[which]
            amp_copies.append(send(slots.at[s], amps.at[col], c_peers[s - 1]))
    local[1].wait()
    power = jnp.zeros((side, side), F32)
    for m in range(modes):
        power += probe[m, 0] * probe[m, 0] + probe[m, 1] * probe[m, 1]
    pow_ref[...] = power
    grad_ref[...] = jnp.zeros_like(grad_ref)
    ssum[...] = jnp.zeros_like(ssum)
    local[2].wait()
    local[3].wait()

    def there(p, carry):
        ssum[...] += patch[p, 0] * patch[p, 0] + patch[p, 1] * patch[p, 1]
        for m in range(modes):
            pr, pi = probe[m, 0], probe[m, 1]
            xr, xi = patch[p, 0], patch[p, 1]
            ebuf[m, :side] = (pr * xr - pi * xi).astype(BF16)
            ebuf[m, side:] = (pr * xi + pi * xr).astype(BF16)
            part = dot(tab[0], ebuf[m])
            hbuf[m, :, :side] = part[:side].astype(BF16)
            hbuf[m, :, side:] = part[side:].astype(BF16)
            far[p, m] = dot(hbuf[m], tab[1])
        return carry

    lax.fori_loop(0, most, there, 0)
    for copy in amp_copies:
        copy.wait_recv()

    def back(p, carry):
        slot = list_ref[p, 1]
        tot = jnp.zeros((side, side), F32)
        for m in range(modes):
            fr, fi = far[p, m, :, :side], far[p, m, :, side:]
            tot += fr * fr + fi * fi
        total[...] = amps[slot].astype(F32) * lax.rsqrt(jnp.maximum(tot, 0.25))
        for m in range(modes):
            ratio = total[...]
            ebuf[m, :side] = (far[p, m, :, :side] * ratio).astype(BF16)
            ebuf[m, side:] = (far[p, m, :, side:] * ratio).astype(BF16)
            part = dot(tab[2], ebuf[m])
            hbuf[m, :, :side] = part[:side].astype(BF16)
            hbuf[m, :, side:] = part[side:].astype(BF16)
            ret = dot(hbuf[m], tab[3])
            rr, ri = ret[:, :side], ret[:, side:]
            pr, pi = probe[m, 0], probe[m, 1]
            xr, xi = patch[p, 0], patch[p, 1]
            if m == 0:
                placed_ref[p, 0] = pr * rr + pi * ri - xr * pow_ref[...]
                placed_ref[p, 1] = pr * ri - pi * rr - xi * pow_ref[...]
            else:
                placed_ref[p, 0] += pr * rr + pi * ri
                placed_ref[p, 1] += pr * ri - pi * rr
            grad_ref[2 * m * side:(2 * m + 1) * side] += xr * rr + xi * ri
            grad_ref[(2 * m + 1) * side:(2 * m + 2) * side] += xr * ri - xi * rr
        return carry

    lax.fori_loop(0, most, back, 0)
    for m in range(modes):
        for q in range(2):
            grad_ref[(2 * m + q) * side:(2 * m + q + 1) * side] -= probe[m, q] * ssum[...]
    send.finish()


def main_call(items, owner, amp, patch, probe, rows, cols):
    side, modes, most = amp.shape[1], probe.shape[0], patch.shape[0]
    copies = cols - 1
    tr, ti = tables(side)

    def left(a, b):
        return jnp.concatenate([jnp.concatenate([a, -b], 1), jnp.concatenate([b, a], 1)], 0)

    def right(a, b):
        return jnp.concatenate([jnp.concatenate([a, b], 1), jnp.concatenate([-b, a], 1)], 0)

    tab = jnp.stack([left(tr, ti), right(tr, ti), left(tr, -ti), right(tr, -ti)])
    V = pl.BlockSpec(memory_space=pltpu.VMEM)
    A = pl.BlockSpec(memory_space=pl.ANY)
    S = pl.BlockSpec(memory_space=pltpu.SMEM)
    return pl.pallas_call(
        functools.partial(main_kernel, rows, cols),
        out_shape=[
            jax.ShapeDtypeStruct((most, 2, side, side), F32),
            jax.ShapeDtypeStruct((modes * 2 * side, side), F32),
            jax.ShapeDtypeStruct((side, side), F32),
        ],
        in_specs=[S, S, A, A, A, A],
        out_specs=[V, V, V],
        scratch_shapes=[
            pltpu.VMEM((cols, side, side), BF16),
            pltpu.VMEM((cols, side, side), BF16),
            pltpu.VMEM(amp.shape, BF16),
            pltpu.VMEM(probe.shape, F32),
            pltpu.VMEM(tab.shape, BF16),
            pltpu.VMEM((most, 2, side, side), F32),
            pltpu.VMEM((most, modes, side, 2 * side), F32),
            pltpu.VMEM((side, side), F32),
            pltpu.VMEM((modes, 2 * side, side), BF16),
            pltpu.VMEM((modes, side, 2 * side), BF16),
            pltpu.VMEM((side, side), F32),
            pltpu.SemaphoreType.DMA((copies,)),
            pltpu.SemaphoreType.DMA((copies,)),
            pltpu.SemaphoreType.DMA((4,)),
        ],
        compiler_params=pltpu.CompilerParams(collective_id=2, has_side_effects=True, vmem_limit_bytes=62 * 2**20),
        name="main",
    )(items, owner, amp, patch, probe, tab)


def place_kernel(tile, half, list_ref, placed_ref, pow_ref, rim_ref, core_ref, num, shift):
    side = 2 * half
    big, tall, wide = tile + side, side + 8, side + 128
    num[...] = jnp.zeros_like(num)
    shift[...] = jnp.zeros_like(shift)
    shift[2, :side, :side] = pow_ref[...]

    def visit(p, carry):
        @pl.when(list_ref[p, 0] == 1)
        def _():
            r, c = list_ref[p, 2], list_ref[p, 3]
            c0 = pl.multiple_of((c // 128) * 128, 128)
            r0 = pl.multiple_of((r // 8) * 8, 8)
            for q in range(3):
                if q < 2:
                    shift[q, :side, :side] = placed_ref[p, q]
                w = pltpu.roll(pltpu.roll(shift[q], r - r0, 0), c - c0, 1)
                num[q, pl.ds(r0, tall), pl.ds(c0, wide)] += w
        return carry

    lax.fori_loop(0, list_ref.shape[0], visit, 0)
    for q in range(3):
        rim_ref[q] = num[q].astype(BF16)
        core_ref[q] = num[q, half:big - half, half:big - half]


def place_call(items, placed, power, tile):
    side = power.shape[0]
    half = side // 2
    big = tile + side
    V = pl.BlockSpec(memory_space=pltpu.VMEM)
    S = pl.BlockSpec(memory_space=pltpu.SMEM)
    return pl.pallas_call(
        functools.partial(place_kernel, tile, half),
        out_shape=[jax.ShapeDtypeStruct((3, big, big), BF16), jax.ShapeDtypeStruct((3, tile, tile), F32)],
        in_specs=[S, V, V],
        out_specs=[V, V],
        scratch_shapes=[pltpu.VMEM((3, big, big), F32), pltpu.VMEM((3, side + 8, side + 128), F32)],
        compiler_params=pltpu.CompilerParams(vmem_limit_bytes=56 * 2**20),
        name="place",
    )(items, placed, power)


def widen_kernel(got_ref, out_ref):
    n = got_ref.shape[2]
    for c in range(2):
        for k in range(2):
            out_ref[c * n:(c + 1) * n, 128 * k:128 * (k + 1)] = got_ref[c, k].astype(F32)


def widen_call(got):
    n = got.shape[2]
    return pl.pallas_call(widen_kernel, out_shape=jax.ShapeDtypeStruct((2 * n, 256), F32), name="widen")(got)


def on_device(object_field, probe, amplitudes, owner, offsets):
    rows, cols = lax.axis_size("row"), lax.axis_size("col")
    held = amplitudes.shape[0]
    most = 4 * (held - 1)
    side, tile = probe.shape[-1], object_field.shape[1]
    ext, meta = pre_call(owner, offsets, object_field, side, rows, cols)
    patch, items = cut_call(meta, ext, tile, rows, cols, held, most)
    placed, grad, power = main_call(items, owner, amplitudes, patch, probe, rows, cols)
    rim, core = place_call(items, placed, power, tile)
    scale = 1.0 / math.sqrt(rows * cols * held)
    object_out, gradient = post_call(rim, core, object_field, grad, rows, cols, scale)
    return (object_out, widen_call(gradient).reshape(probe.shape))


def solution(mesh):
    return jax.shard_map(
        on_device,
        mesh=mesh,
        in_specs=(
            P(None, "row", "col"),
            P(),
            P(("row", "col"), None, None),
            P(("row", "col")),
            P(("row", "col"), None),
        ),
        out_specs=(P(None, "row", "col"), P()),
        check_vma=False,
    )
```

time: 190 us -> 236 us (1.24)
  Pallas kernels: 175 us -> 226 us
  local copies, waits for them, and re-layouts: 12.7 us -> 8.92 us
    pallas_call x1 -> x4, Pallas kernels: 62.1 us -> 84.7 us  [the longest x1 70.7 us: main_call(): pl.pallas_call(functools.partial(main_kernel, rows, cols), out_shape=[jax...]
    pallas_call x1, Pallas kernels: 57.3 us -> 75.1 us  [post_call(): pl.pallas_call(functools.partial(post_kernel, rows, cols, tile, half, sca...]
    pallas_call x1, Pallas kernels: 55.9 us -> 65.8 us  [pre_call(): pl.pallas_call(functools.partial(pre_kernel, rows, cols, tile, half), out...]
    unnamed x17 -> x12, local copies, waits for them, and re-layouts: 12.6 us -> 8.92 us
where the time goes in v3:
time: 236 us; the launch traced here: 235 us
  Pallas kernels  226 us (96%)
  local copies, waits for them, and re-layouts  8.92 us (4%)
    pallas_call x1, Pallas kernels, post_call(): pl.pallas_call(functools.partial(post_kernel, rows, cols, tile, half, sca...  75.1 us
    pallas_call x1, Pallas kernels, main_call(): pl.pallas_call(functools.partial(main_kernel, rows, cols), out_shape=[jax...  70.7 us
    pallas_call x1, Pallas kernels, pre_call(): pl.pallas_call(functools.partial(pre_kernel, rows, cols, tile, half), out...  65.8 us
    unnamed x12, local copies, waits for them, and re-layouts  8.92 us
    pallas_call x1, Pallas kernels, place_call(): pl.pallas_call(functools.partial(place_kernel, tile, half), out_shape=[ja...  7.33 us

profile of v3, /device:TPU:1, one launch (start us, length us, event | category | flops | bytes accessed | tf_op | source)
XLA Modules:
  0.0 235.2 jit_solution(14604405264247665223)
XLA Ops:
  0.6 1.3 copy.9.offsets_ref
  2.0 65.8 %pre.1 = (f32[2,768,768]{2,1,0:T(8,128)}, s32[16,1,128]{2,1,0:T(1,128)}) custom-call(s32[4]{0:T(128)} %owner_ref.3, s32[4,2]{1,0:T(4,128)} %copy.9.offsets_ref, f32[2,512,512]{2,1,0:T(8,128)} %obj_ref.3), custom_call_target="tpu_custom_call" | custom-call | tf_op jit(solution)/shard_map/pre/pallas_call | solution.py:241
  67.8 0.0 copy-start.1
  67.8 2.3 copy-done.1
  70.1 0.0 copy-start.3
  70.1 0.7 copy-done.3
  70.8 3.9 %cut.1 = (f32[12,2,256,256]{3,2,1,0:T(8,128)S(1)}, s32[12,4]{1,0:T(8,128)S(1)}) custom-call(s32[16,1,128]{2,1,0:T(1,128)S(1)} %copy-done.3, f32[2,768,768]{2,1,0:T(8,128)S(1)} %copy-done.1), custom_call_target="tpu_custom_call" | custom-call | tf_op jit(solution)/shard_map/cut/pallas_call | solution.py:341
  74.7 0.0 copy-start
  74.7 2.6 %copy-done = f32[12,2,256,256]{3,2,1,0:T(8,128)} copy-done((f32[12,2,256,256]{3,2,1,0:T(8,128)}, f32[12,2,256,256]{3,2,1,0:T(8,128)S(1)}, u32[]{:S(2)}) %copy-start) | copy-done | bytes 6291480
  77.4 0.0 copy-start.2
  77.4 0.6 copy-done.2
  78.0 70.7 %main.1 = (f32[12,2,256,256]{3,2,1,0:T(8,128)}, f32[2048,256]{1,0:T(8,128)}, f32[256,256]{1,0:T(8,128)}) custom-call(s32[12,4]{1,0:T(8,128)} %copy-done.2, s32[4]{0:T(128)} %owner_ref.3, bf16[4,256,256]{2,1,0:T(8,128)(2,1)} %amp_hbm.1, f32[12,2,256,256]{3,2,1,0:T(8,128)} %copy-done, f32[4,2,256,256]{3,2,1,0:T(8,128)} %probe_hbm.1, ...), custom_call_target="tpu_custom_call" | custom-call | tf_op jit(solution)/shard_map/main/pallas_call | solution.py:463
  148.6 7.3 %place.1 = (bf16[3,768,768]{2,1,0:T(8,128)(2,1)}, f32[3,512,512]{2,1,0:T(8,128)}) custom-call(s32[12,4]{1,0:T(8,128)} %copy-done.2, f32[12,2,256,256]{3,2,1,0:T(8,128)} %get-tuple-element.17.placed_ref, f32[256,256]{1,0:T(8,128)} %get-tuple-element.18.pow_ref), custom_call_target="tpu_custom_call" | custom-call | tf_op jit(solution)/shard_map/place/pallas_call | solution.py:525
  155.9 75.1 %post.1 = (f32[2,512,512]{2,1,0:T(8,128)}, bf16[2,2,1024,128]{3,2,1,0:T(8,128)(2,1)}) custom-call(bf16[3,768,768]{2,1,0:T(8,128)(2,1)} %get-tuple-element.19.rim_ref, f32[3,512,512]{2,1,0:T(8,128)} %get-tuple-element.20.core_ref, f32[2,512,512]{2,1,0:T(8,128)} %obj_ref.3, f32[2048,256]{1,0:T(8,128)} %get-tuple-element.21.grad_ref), custom_call_target="tpu_custom_call" | custom-call | tf_op jit(solution)/shard_map/post/pallas_call | solution.py:176
  231.0 0.0 copy-start.4
  231.0 2.8 %widen.1 = f32[2048,256]{1,0:T(8,128)} custom-call(bf16[2,2,1024,128]{3,2,1,0:T(8,128)(2,1)} %get-tuple-element.23.got_ref), custom_call_target="tpu_custom_call" | custom-call | tf_op jit(solution)/shard_map/widen/pallas_call | solution.py:545
  233.9 0.0 copy-done.4
  233.9 1.3 copy.11
Async XLA Ops:
  67.8 2.3 copy-start.1
  70.1 0.7 copy-start.3
  74.7 2.6 %copy-start = (f32[12,2,256,256]{3,2,1,0:T(8,128)}, f32[12,2,256,256]{3,2,1,0:T(8,128)S(1)}, u32[]{:S(2)}) copy-start(f32[12,2,256,256]{3,2,1,0:T(8,128)S(1)} %get-tuple-element.16.patch_hbm) | copy-start | bytes 18874372
  77.4 0.6 copy-start.2
  231.0 2.9 %copy-start.4 = (f32[2,512,512]{2,1,0:T(8,128)S(1)}, f32[2,512,512]{2,1,0:T(8,128)}, u32[]{:S(2)}) copy-start(f32[2,512,512]{2,1,0:T(8,128)} %get-tuple-element.26) | copy-start | bytes 6291460

commit v4 on v3

--- a/solution.py
+++ b/solution.py
@@ -36,6 +36,13 @@
 
 def landing(step, tile, half):
     return {-1: (tile - half, half), 0: (0, tile), 1: (0, half)}[step]
+
+
+def column_peers(row, col, cols):
+    depth = 4
+    steps = [(0, 1), (1, 0), (0, 3), (3, 0), (1, 1), (3, 3), (1, 3), (3, 1), (2, 0), (0, 2), (2, 2), (1, 2), (3, 2), (2, 1), (2, 3)]
+    x, z = col // depth, lax.rem(col, depth)
+    return [(row, lax.rem(x + dx, cols // depth) * depth + lax.rem(z + dz, depth)) for dx, dz in steps]
 
 
 class Sends:
@@ -65,13 +72,13 @@
 
 
 def post_kernel(rows, cols, tile, half, scale, rim_ref, core_ref, obj_ref, grad_ref, out_ref, all16,
-                wsum, rims, mate, sum_a, sum_b, got_a, got_b, part_a, part_b, got_a2, got_b2, gsend, grecv):
+                wsum, rim_rows, rim_cols, rim_corners, mate, sum_a, sum_b, got_a, got_b, part_a, part_b, got_a2, got_b2, gsend, grecv):
     row, col = lax.axis_index("row"), lax.axis_index("col")
     core, y = lax.rem(row, 2), row // 2
     ys = rows // 2
     other = (row + 1 - 2 * core, col)
     y_peers = [(lax.rem(y + s, ys) * 2 + core, col) for s in range(1, ys)]
-    c_peers = [(row, lax.rem(col + s, cols)) for s in range(1, cols)]
+    c_peers = column_peers(row, col, cols)
     near = [around(row, col, dr, dc, rows, cols) for dr, dc in NEAR]
     greet([other] + y_peers + c_peers + near)
     send = Sends(gsend, grecv)
@@ -82,16 +89,28 @@
     mine = pl.ds(pl.multiple_of(core * n, n), n)
     pair = send(grad_ref.at[theirs], mate, other)
     rim_copies = []
-    for i, (dr, dc) in enumerate(NEAR):
-        r0, rl = span(dr, tile, half)
-        c0, cl = span(dc, tile, half)
-        rim_copies.append(send(rim_ref.at[:, r0:r0 + rl, c0:c0 + cl], rims.at[i, :, 0:rl, 0:cl], near[i]))
+
+    def landed(i):
+        dr, dc = NEAR[i]
+        if dc == 0:
+            return rim_rows.at[(dr + 1) // 2]
+        if dr == 0:
+            return rim_cols.at[(dc + 1) // 2]
+        return rim_corners.at[dr + 1 + (dc + 1) // 2]
+
+    def send_rims(which):
+        for i in which:
+            r0, rl = span(NEAR[i][0], tile, half)
+            c0, cl = span(NEAR[i][1], tile, half)
+            rim_copies.append(send(rim_ref.at[:, r0:r0 + rl, c0:c0 + cl], landed(i), near[i]))
+
+    send_rims([1, 6])
     pair.wait_recv()
     h = grad_ref[mine, :] + mate[...]
     sum_a[...] = h[:, :128]
     sum_b[...] = h[:, 128:]
     y_at = [lax.rem(y + s, ys) for s in range(1, ys)]
-    c_at = [lax.rem(col + s, cols) for s in range(1, cols)]
+    c_at = [peer[1] for peer in c_peers]
 
     def piece(k, size):
         return pl.ds(pl.multiple_of(k * size, size), size)
@@ -112,6 +131,7 @@
         tot += got_b[s]
     part_b[...] = tot
     b2 = [send(part_b.at[piece(y_at[s], fin)], got_b2.at[s], y_peers[s]) for s in range(ys - 1)]
+    send_rims([3, 4])
     for c in a2:
         c.wait_recv()
     tot = part_a[piece(col, fin), :]
@@ -128,6 +148,7 @@
     at_b = piece(col * ys + y, fin)
     all16[core, 1, at_b, :] = (tot * scale).astype(all16.dtype)
     b3 = [send(all16.at[core, 1, at_b], all16.at[core, 1, at_b], p) for p in y_peers]
+    send_rims([0, 2, 5, 7])
     for c in a3:
         c.wait_recv()
     big_a = piece(y, na)
@@ -152,8 +173,8 @@
         @pl.when(keep)
         def _(i=i, r0=r0, rl=rl, c0=c0, cl=cl):
             for q in range(2):
-                out_ref[q, r0:r0 + rl, c0:c0 + cl] += rims[i, q, 0:rl, 0:cl].astype(F32)
-            wsum[r0:r0 + rl, c0:c0 + cl] += rims[i, 2, 0:rl, 0:cl].astype(F32)
+                out_ref[q, r0:r0 + rl, c0:c0 + cl] += landed(i)[q].astype(F32)
+            wsum[r0:r0 + rl, c0:c0 + cl] += landed(i)[2].astype(F32)
 
     for q in range(2):
         out_ref[q] = obj_ref[q] + out_ref[q] / (wsum[...] + 1.0)
@@ -172,15 +193,16 @@
     na, nb, fin = n // ys, n // cols, n // (ys * cols)
     copies = 1 + 8 + 2 * (ys - 1) + 2 * (cols - 1) + 2 * (ys - 1) + 2 * (cols - 1) + 1
     V = pl.BlockSpec(memory_space=pltpu.VMEM)
-    A = pl.BlockSpec(memory_space=pl.ANY)
     return pl.pallas_call(
         functools.partial(post_kernel, rows, cols, tile, half, scale),
         out_shape=[jax.ShapeDtypeStruct(obj.shape, F32), jax.ShapeDtypeStruct((2, 2, n, 128), BF16)],
-        in_specs=[A, V, V, V],
+        in_specs=[V, V, V, V],
         out_specs=[V, V],
         scratch_shapes=[
             pltpu.VMEM((tile, tile), F32),
-            pltpu.VMEM((8, 3, tile, tile), BF16),
+            pltpu.VMEM((2, 3, half, tile), BF16),
+            pltpu.VMEM((2, 3, tile, half), BF16),
+            pltpu.VMEM((4, 3, half, half), BF16),
             pltpu.VMEM((n, 256), F32),
             pltpu.VMEM((n, 128), F32),
             pltpu.VMEM((n, 128), F32),
@@ -193,7 +215,7 @@
             pltpu.SemaphoreType.DMA((copies,)),
             pltpu.SemaphoreType.DMA((copies,)),
         ],
-        compiler_params=pltpu.CompilerParams(collective_id=1, has_side_effects=True, vmem_limit_bytes=56 * 2**20),
+        compiler_params=pltpu.CompilerParams(collective_id=1, has_side_effects=True, vmem_limit_bytes=40 * 2**20),
         name="post",
     )(rim, core, obj, grad)
 
@@ -201,7 +223,7 @@
 def pre_kernel(rows, cols, tile, half, owner_ref, offsets_ref, obj_ref, ext_ref, meta_ref, mine, gsend, grecv, lsem):
     row, col = lax.axis_index("row"), lax.axis_index("col")
     near = [around(row, col, dr, dc, rows, cols) for dr, dc in NEAR]
-    c_peers = [(row, lax.rem(col + s, cols)) for s in range(1, cols)]
+    c_peers = column_peers(row, col, cols)
     held = owner_ref.shape[0]
     core = pltpu.make_async_copy(obj_ref, ext_ref.at[:, half:half + tile, half:half + tile], lsem.at[0])
     core.start()
@@ -213,6 +235,7 @@
             note = jnp.where(lane == held + 2 * h + k, offsets_ref[h, k], note)
     mine[...] = note
     greet(c_peers + near)
+    core.wait()
     send = Sends(gsend, grecv)
     got = []
     for i, (dr, dc) in enumerate(NEAR):
@@ -220,14 +243,14 @@
         c0, cl = {-1: (0, half), 0: (0, tile), 1: (tile - half, half)}[dc]
         tr, _ = span(-dr, tile, half)
         tc, _ = span(-dc, tile, half)
-        got.append(send(obj_ref.at[:, r0:r0 + rl, c0:c0 + cl], ext_ref.at[:, tr:tr + rl, tc:tc + cl], near[i]))
+        r0, c0 = r0 + half, c0 + half
+        got.append(send(ext_ref.at[:, r0:r0 + rl, c0:c0 + cl], ext_ref.at[:, tr:tr + rl, tc:tc + cl], near[i]))
     for s in range(cols - 1):
         got.append(send(mine, meta_ref.at[col], c_peers[s]))
     own = pltpu.make_async_copy(mine, meta_ref.at[col], lsem.at[1])
     own.start()
     for c in got:
         c.wait_recv()
-    core.wait()
     own.wait()
     send.finish()
 
@@ -236,20 +259,20 @@
     tile, half = obj.shape[1], side // 2
     big = tile + side
     copies = 8 + cols - 1
-    A = pl.BlockSpec(memory_space=pl.ANY)
+    V = pl.BlockSpec(memory_space=pltpu.VMEM)
     S = pl.BlockSpec(memory_space=pltpu.SMEM)
     return pl.pallas_call(
         functools.partial(pre_kernel, rows, cols, tile, half),
         out_shape=[jax.ShapeDtypeStruct((2, big, big), F32), jax.ShapeDtypeStruct((cols, 1, 128), jnp.int32)],
-        in_specs=[S, S, A],
-        out_specs=[A, A],
+        in_specs=[S, S, pl.BlockSpec(memory_space=pltpu.HBM)],
+        out_specs=[V, V],
         scratch_shapes=[
             pltpu.VMEM((1, 128), jnp.int32),
             pltpu.SemaphoreType.DMA((copies,)),
             pltpu.SemaphoreType.DMA((copies,)),
             pltpu.SemaphoreType.DMA((2,)),
         ],
-        compiler_params=pltpu.CompilerParams(collective_id=0, has_side_effects=True),
+        compiler_params=pltpu.CompilerParams(collective_id=0, has_side_effects=True, vmem_limit_bytes=57 * 2**20),
         name="pre",
     )(owner, offsets, obj)
 
@@ -336,7 +359,7 @@
 def cut_call(meta, ext, tile, rows, cols, held, most):
     big = ext.shape[1]
     side = big - tile
-    A = pl.BlockSpec(memory_space=pl.ANY)
+    A = pl.BlockSpec(memory_space=pltpu.HBM)
     S = pl.BlockSpec(memory_space=pltpu.SMEM)
     return pl.pallas_call(
         functools.partial(cut_kernel, rows, cols, tile, side // 2, held),
@@ -349,17 +372,17 @@
             pltpu.SemaphoreType.DMA,
             pltpu.SemaphoreType.DMA((most,)),
         ],
-        compiler_params=pltpu.CompilerParams(vmem_limit_bytes=32 * 2**20),
+        compiler_params=pltpu.CompilerParams(vmem_limit_bytes=57 * 2**20),
         name="cut",
     )(meta, ext)
 
 
 def main_kernel(rows, cols, list_ref, owner_ref, amp_hbm, patch_hbm, probe_hbm, tab_hbm,
-                placed_ref, grad_ref, pow_ref,
-                slots, amps, amp, probe, tab, patch, far, total, ebuf, hbuf, ssum,
+                placed_hbm, grad_ref, pow_ref,
+                placed_ref, psem, slots, amps, amp, probe, tab, patch, far, total, ratio, ebuf, hbuf, ssum,
                 gsend, grecv, lsem):
     row, col = lax.axis_index("row"), lax.axis_index("col")
-    c_peers = [(row, lax.rem(col + s, cols)) for s in range(1, cols)]
+    c_peers = column_peers(row, col, cols)
     held, side, modes, most = amp.shape[0], amp.shape[1], probe.shape[0], patch.shape[0]
     local = [
         pltpu.make_async_copy(amp_hbm, amp, lsem.at[0]),
@@ -374,7 +397,7 @@
     local[0].wait()
     amp_copies = []
     for s in range(cols):
-        to = lax.rem(col + s, cols)
+        to = col if s == 0 else c_peers[s - 1][1]
         which = jnp.int32(0)
         for h in range(1, held):
             which = jnp.where(owner_ref[h] == to, h, which)
@@ -393,55 +416,85 @@
     local[2].wait()
     local[3].wait()
 
-    def there(p, carry):
+    chunk = hbuf.shape[2] // modes
+    chunks = side // chunk
+
+    def left_pass(k, fields, halves):
+        for m in range(modes):
+            for h in range(2):
+                part = dot(tab[k, h * side:(h + 1) * side], fields[m])
+                for c in range(chunks):
+                    rows_c = slice(c * chunk, (c + 1) * chunk)
+                    halves[c, m * chunk:(m + 1) * chunk, h * side:(h + 1) * side] = part[rows_c].astype(BF16)
+
+    def there(p, fields, halves):
         ssum[...] += patch[p, 0] * patch[p, 0] + patch[p, 1] * patch[p, 1]
         for m in range(modes):
             pr, pi = probe[m, 0], probe[m, 1]
             xr, xi = patch[p, 0], patch[p, 1]
-            ebuf[m, :side] = (pr * xr - pi * xi).astype(BF16)
-            ebuf[m, side:] = (pr * xi + pi * xr).astype(BF16)
-            part = dot(tab[0], ebuf[m])
-            hbuf[m, :, :side] = part[:side].astype(BF16)
-            hbuf[m, :, side:] = part[side:].astype(BF16)
-            far[p, m] = dot(hbuf[m], tab[1])
-        return carry
-
-    lax.fori_loop(0, most, there, 0)
+            fields[m, :side] = (pr * xr - pi * xi).astype(BF16)
+            fields[m, side:] = (pr * xi + pi * xr).astype(BF16)
+        left_pass(0, fields, halves)
+        for c in range(chunks):
+            rows_c = slice(c * chunk, (c + 1) * chunk)
+            out = dot(halves[c], tab[1])
+            tot = jnp.zeros((chunk, side), F32)
+            for m in range(modes):
+                one = out[m * chunk:(m + 1) * chunk]
+                far[p, m, rows_c] = one
+                tot += one[:, :side] * one[:, :side] + one[:, side:] * one[:, side:]
+            total[p, rows_c] = tot
+
+    def there_two(k, carry):
+        for u in range(2):
+            there(2 * k + u, ebuf.at[u], hbuf.at[u])
+        return carry
+
+    lax.fori_loop(0, most // 2, there_two, 0)
+    for p in range(most - most % 2, most):
+        there(p, ebuf.at[0], hbuf.at[0])
     for copy in amp_copies:
         copy.wait_recv()
 
+    def out(p):
+        return pltpu.make_async_copy(placed_ref.at[p], placed_hbm.at[p], psem.at[p])
+
+    def drain(p, carry):
+        out(p).wait()
+        return carry
+
     def back(p, carry):
-        slot = list_ref[p, 1]
-        tot = jnp.zeros((side, side), F32)
+        fields, halves = ebuf.at[0], hbuf.at[0]
+        ratio[...] = amps[list_ref[p, 1]].astype(F32) * lax.rsqrt(jnp.maximum(total[p], 0.25))
         for m in range(modes):
-            fr, fi = far[p, m, :, :side], far[p, m, :, side:]
-            tot += fr * fr + fi * fi
-        total[...] = amps[slot].astype(F32) * lax.rsqrt(jnp.maximum(tot, 0.25))
-        for m in range(modes):
-            ratio = total[...]
-            ebuf[m, :side] = (far[p, m, :, :side] * ratio).astype(BF16)
-            ebuf[m, side:] = (far[p, m, :, side:] * ratio).astype(BF16)
-            part = dot(tab[2], ebuf[m])
-            hbuf[m, :, :side] = part[:side].astype(BF16)
-            hbuf[m, :, side:] = part[side:].astype(BF16)
-            ret = dot(hbuf[m], tab[3])
-            rr, ri = ret[:, :side], ret[:, side:]
-            pr, pi = probe[m, 0], probe[m, 1]
-            xr, xi = patch[p, 0], patch[p, 1]
-            if m == 0:
-                placed_ref[p, 0] = pr * rr + pi * ri - xr * pow_ref[...]
-                placed_ref[p, 1] = pr * ri - pi * rr - xi * pow_ref[...]
-            else:
-                placed_ref[p, 0] += pr * rr + pi * ri
-                placed_ref[p, 1] += pr * ri - pi * rr
-            grad_ref[2 * m * side:(2 * m + 1) * side] += xr * rr + xi * ri
-            grad_ref[(2 * m + 1) * side:(2 * m + 2) * side] += xr * ri - xi * rr
+            fields[m, :side] = (far[p, m, :, :side] * ratio[...]).astype(BF16)
+            fields[m, side:] = (far[p, m, :, side:] * ratio[...]).astype(BF16)
+        left_pass(2, fields, halves)
+        for c in range(chunks):
+            rows_c = slice(c * chunk, (c + 1) * chunk)
+            ret = dot(halves[c], tab[3])
+            xr, xi = patch[p, 0, rows_c], patch[p, 1, rows_c]
+            nr, ni = -xr * pow_ref[rows_c], -xi * pow_ref[rows_c]
+            for m in range(modes):
+                one = ret[m * chunk:(m + 1) * chunk]
+                rr, ri = one[:, :side], one[:, side:]
+                pr, pi = probe[m, 0, rows_c], probe[m, 1, rows_c]
+                nr += pr * rr + pi * ri
+                ni += pr * ri - pi * rr
+                at_r = 2 * m * side + c * chunk
+                at_i = at_r + side
+                grad_ref[at_r:at_r + chunk] += xr * rr + xi * ri
+                grad_ref[at_i:at_i + chunk] += xr * ri - xi * rr
+            placed_ref[p, 0, rows_c] = nr
+            placed_ref[p, 1, rows_c] = ni
+        out(p).start()
         return carry
 
     lax.fori_loop(0, most, back, 0)
     for m in range(modes):
         for q in range(2):
             grad_ref[(2 * m + q) * side:(2 * m + q + 1) * side] -= probe[m, q] * ssum[...]
+    lax.fori_loop(0, most, drain, 0)
     send.finish()
 
 
@@ -458,7 +511,7 @@
 
     tab = jnp.stack([left(tr, ti), right(tr, ti), left(tr, -ti), right(tr, -ti)])
     V = pl.BlockSpec(memory_space=pltpu.VMEM)
-    A = pl.BlockSpec(memory_space=pl.ANY)
+    A = pl.BlockSpec(memory_space=pltpu.HBM)
     S = pl.BlockSpec(memory_space=pltpu.SMEM)
     return pl.pallas_call(
         functools.partial(main_kernel, rows, cols),
@@ -468,8 +521,10 @@
             jax.ShapeDtypeStruct((side, side), F32),
         ],
         in_specs=[S, S, A, A, A, A],
-        out_specs=[V, V, V],
+        out_specs=[A, V, V],
         scratch_shapes=[
+            pltpu.VMEM((most, 2, side, side), F32),
+            pltpu.SemaphoreType.DMA((most,)),
             pltpu.VMEM((cols, side, side), BF16),
             pltpu.VMEM((cols, side, side), BF16),
             pltpu.VMEM(amp.shape, BF16),
@@ -477,9 +532,10 @@
             pltpu.VMEM(tab.shape, BF16),
             pltpu.VMEM((most, 2, side, side), F32),
             pltpu.VMEM((most, modes, side, 2 * side), F32),
+            pltpu.VMEM((most, side, side), F32),
             pltpu.VMEM((side, side), F32),
-            pltpu.VMEM((modes, 2 * side, side), BF16),
-            pltpu.VMEM((modes, side, 2 * side), BF16),
+            pltpu.VMEM((2, modes, 2 * side, side), BF16),
+            pltpu.VMEM((2, 4, modes * side // 4, 2 * side), BF16),
             pltpu.VMEM((side, side), F32),
             pltpu.SemaphoreType.DMA((copies,)),
             pltpu.SemaphoreType.DMA((copies,)),
@@ -490,14 +546,25 @@
     )(items, owner, amp, patch, probe, tab)
 
 
-def place_kernel(tile, half, list_ref, placed_ref, pow_ref, rim_ref, core_ref, num, shift):
+def place_kernel(tile, half, list_ref, placed_hbm, pow_ref, rim_ref, core_ref, placed_ref, psem, num, shift):
     side = 2 * half
     big, tall, wide = tile + side, side + 8, side + 128
+
+    def fetch(p):
+        return pltpu.make_async_copy(placed_hbm.at[p], placed_ref.at[p], psem.at[p])
+
+    def start(p, carry):
+        fetch(p).start()
+        return carry
+
+    lax.fori_loop(0, list_ref.shape[0], start, 0)
     num[...] = jnp.zeros_like(num)
     shift[...] = jnp.zeros_like(shift)
     shift[2, :side, :side] = pow_ref[...]
 
     def visit(p, carry):
+        fetch(p).wait()
+
         @pl.when(list_ref[p, 0] == 1)
         def _():
             r, c = list_ref[p, 2], list_ref[p, 3]
@@ -525,10 +592,13 @@
     return pl.pallas_call(
         functools.partial(place_kernel, tile, half),
         out_shape=[jax.ShapeDtypeStruct((3, big, big), BF16), jax.ShapeDtypeStruct((3, tile, tile), F32)],
-        in_specs=[S, V, V],
+        in_specs=[S, pl.BlockSpec(memory_space=pltpu.HBM), V],
         out_specs=[V, V],
-        scratch_shapes=[pltpu.VMEM((3, big, big), F32), pltpu.VMEM((3, side + 8, side + 128), F32)],
-        compiler_params=pltpu.CompilerParams(vmem_limit_bytes=56 * 2**20),
+        scratch_shapes=[
+            pltpu.VMEM(placed.shape, F32),
+            pltpu.SemaphoreType.DMA((placed.shape[0],)),
+            pltpu.VMEM((3, big, big), F32), pltpu.VMEM((3, side + 8, side + 128), F32)],
+        compiler_params=pltpu.CompilerParams(vmem_limit_bytes=50 * 2**20),
         name="place",
     )(items, placed, power)
 

time: 236 us -> 161 us (0.68)
  Pallas kernels: 226 us -> 153 us
    pallas_call x1, Pallas kernels: 65.8 us -> 30.7 us  [pre_call(): pl.pallas_call(functools.partial(pre_kernel, rows, cols, tile, half), out...]
    pallas_call x1, Pallas kernels: 70.7 us -> 50.4 us  [main_call(): pl.pallas_call(functools.partial(main_kernel, rows, cols), out_shape=[jax...]
    pallas_call x1, Pallas kernels: 75.1 us -> 56.5 us  [post_call(): pl.pallas_call(functools.partial(post_kernel, rows, cols, tile, half, sca...]
    pallas_call x1, Pallas kernels: 3.86 us -> 7.02 us  [cut_call(): pl.pallas_call(functools.partial(cut_kernel, rows, cols, tile, side // 2,...]
    unnamed x12 -> x14, local copies, waits for them, and re-layouts: 8.92 us -> 6.57 us
where the time goes in v4:
time: 161 us
  Pallas kernels  153 us (95%)
  local copies, waits for them, and re-layouts  6.57 us (4%)
    pallas_call x1, Pallas kernels, post_call(): pl.pallas_call(functools.partial(post_kernel, rows, cols, tile, half, sca...  56.5 us
    pallas_call x1, Pallas kernels, main_call(): pl.pallas_call(functools.partial(main_kernel, rows, cols), out_shape=[jax...  50.4 us
    pallas_call x1, Pallas kernels, pre_call(): pl.pallas_call(functools.partial(pre_kernel, rows, cols, tile, half), out...  30.7 us
    pallas_call x1, Pallas kernels, cut_call(): pl.pallas_call(functools.partial(cut_kernel, rows, cols, tile, side // 2,...  7.02 us
    unnamed x14, local copies, waits for them, and re-layouts  6.57 us
    pallas_call x1, Pallas kernels, place_call(): pl.pallas_call(functools.partial(place_kernel, tile, half), out_shape=[ja...  6.07 us

profile of v4, /device:TPU:1, one launch (start us, length us, event | category | flops | bytes accessed | tf_op | source)
XLA Modules:
  0.0 160.7 jit_solution(13226360474452394785)
XLA Ops:
  0.6 1.3 copy.9.offsets_ref
  2.0 30.7 %pre.1 = (f32[2,768,768]{2,1,0:T(8,128)}, s32[16,1,128]{2,1,0:T(1,128)}) custom-call(s32[4]{0:T(128)} %owner_ref.3, s32[4,2]{1,0:T(4,128)} %copy.9.offsets_ref, f32[2,512,512]{2,1,0:T(8,128)} %obj_ref.3), custom_call_target="tpu_custom_call" | custom-call | tf_op jit(solution)/shard_map/pre/pallas_call | solution.py:264
  32.7 7.0 %cut.1 = (f32[12,2,256,256]{3,2,1,0:T(8,128)}, s32[12,4]{1,0:T(8,128)}) custom-call(s32[16,1,128]{2,1,0:T(1,128)} %get-tuple-element.13.meta_ref, f32[2,768,768]{2,1,0:T(8,128)} %get-tuple-element.14.ext_hbm), custom_call_target="tpu_custom_call" | custom-call | tf_op jit(solution)/shard_map/cut/pallas_call | solution.py:364
  39.7 0.0 copy-start.5
  39.7 50.4 %main.1 = (f32[12,2,256,256]{3,2,1,0:T(8,128)}, f32[2048,256]{1,0:T(8,128)}, f32[256,256]{1,0:T(8,128)}) custom-call(s32[12,4]{1,0:T(8,128)} %get-tuple-element.15.list_ref, s32[4]{0:T(128)} %owner_ref.3, bf16[4,256,256]{2,1,0:T(8,128)(2,1)} %amp_hbm.1, f32[12,2,256,256]{3,2,1,0:T(8,128)} %get-tuple-element.16.patch_hbm, f32[4,2,256,256]{3,2,1,0:T(8,128)} %probe_hbm.1, ...), custom_call_target="tpu_custom_call" | custom-call | tf_op jit(solution)/shard_map/main/pallas_call | solution.py:516
  90.2 0.0 copy-done.5
  90.2 0.0 copy-start.4
  90.2 0.9 copy-done.4
  91.1 0.0 copy-start
  91.1 0.0 copy-start.2
  91.1 6.1 %place.1 = (bf16[3,768,768]{2,1,0:T(8,128)(2,1)}, f32[3,512,512]{2,1,0:T(8,128)S(1)}) custom-call(s32[12,4]{1,0:T(8,128)S(1)} %copy-done.5, f32[12,2,256,256]{3,2,1,0:T(8,128)} %get-tuple-element.17.placed_hbm, f32[256,256]{1,0:T(8,128)S(1)} %copy-done.4), custom_call_target="tpu_custom_call" | custom-call | tf_op jit(solution)/shard_map/place/pallas_call | solution.py:592
  97.2 0.0 copy-done
  97.2 0.0 copy-done.2
  97.2 0.0 copy-start.1
  97.2 2.0 %copy-done.1 = bf16[3,768,768]{2,1,0:T(8,128)(2,1)S(1)} copy-done((bf16[3,768,768]{2,1,0:T(8,128)(2,1)S(1)}, bf16[3,768,768]{2,1,0:T(8,128)(2,1)}, u32[]{:S(2)}) %copy-start.1) | copy-done | bytes 3538968
  99.2 56.5 %post.1 = (f32[2,512,512]{2,1,0:T(8,128)S(1)}, bf16[2,2,1024,128]{3,2,1,0:T(8,128)(2,1)S(1)}) custom-call(bf16[3,768,768]{2,1,0:T(8,128)(2,1)S(1)} %copy-done.1, f32[3,512,512]{2,1,0:T(8,128)S(1)} %get-tuple-element.20.core_ref, f32[2,512,512]{2,1,0:T(8,128)S(1)} %copy-done, f32[2048,256]{1,0:T(8,128)S(1)} %copy-done.2), custom_call_target="tpu_custom_call" | custom-call | tf_op jit(solution)/shard_map/post/pallas_call | solution.py:196
  155.7 0.0 copy-start.3
  155.7 1.0 copy-done.3
  156.7 2.7 %widen.1 = f32[2048,256]{1,0:T(8,128)} custom-call(bf16[2,2,1024,128]{3,2,1,0:T(8,128)(2,1)} %copy-done.3), custom_call_target="tpu_custom_call" | custom-call | tf_op jit(solution)/shard_map/widen/pallas_call | solution.py:615
  159.4 1.3 copy.11
Async XLA Ops:
  39.7 50.4 %copy-start.5 = (s32[12,4]{1,0:T(8,128)S(1)}, s32[12,4]{1,0:T(8,128)}, u32[]{:S(2)}) copy-start(s32[12,4]{1,0:T(8,128)} %get-tuple-element.15.list_ref) | copy-start | bytes 580
  90.2 1.0 copy-start.4
  91.1 6.1 %copy-start = (f32[2,512,512]{2,1,0:T(8,128)S(1)}, f32[2,512,512]{2,1,0:T(8,128)}, u32[]{:S(2)}) copy-start(f32[2,512,512]{2,1,0:T(8,128)} %obj_ref.3) | copy-start | bytes 6291460
  91.1 6.1 %copy-start.2 = (f32[2048,256]{1,0:T(8,128)S(1)}, f32[2048,256]{1,0:T(8,128)}, u32[]{:S(2)}) copy-start(f32[2048,256]{1,0:T(8,128)} %get-tuple-element.21.grad_ref) | copy-start | bytes 6291460
  97.2 2.0 %copy-start.1 = (bf16[3,768,768]{2,1,0:T(8,128)(2,1)S(1)}, bf16[3,768,768]{2,1,0:T(8,128)(2,1)}, u32[]{:S(2)}) copy-start(bf16[3,768,768]{2,1,0:T(8,128)(2,1)} %get-tuple-element.19.rim_ref) | copy-start | bytes 10616836
  155.7 1.0 copy-start.3

commit v5 on v4

--- a/solution.py
+++ b/solution.py
@@ -71,7 +71,7 @@
     pl.semaphore_wait(barrier, len(devices))
 
 
-def post_kernel(rows, cols, tile, half, scale, rim_ref, core_ref, obj_ref, grad_ref, out_ref, all16,
+def post_kernel(rows, cols, tile, half, scale, rows_ref, cols_ref, corners_ref, core_ref, obj_ref, grad_ref, out_ref, all16,
                 wsum, rim_rows, rim_cols, rim_corners, mate, sum_a, sum_b, got_a, got_b, part_a, part_b, got_a2, got_b2, gsend, grecv):
     row, col = lax.axis_index("row"), lax.axis_index("col")
     core, y = lax.rem(row, 2), row // 2
@@ -90,19 +90,20 @@
     pair = send(grad_ref.at[theirs], mate, other)
     rim_copies = []
 
-    def landed(i):
+    def place(i, by_rows, by_cols, at_corners):
         dr, dc = NEAR[i]
         if dc == 0:
-            return rim_rows.at[(dr + 1) // 2]
+            return by_rows.at[(dr + 1) // 2]
         if dr == 0:
-            return rim_cols.at[(dc + 1) // 2]
-        return rim_corners.at[dr + 1 + (dc + 1) // 2]
+            return by_cols.at[(dc + 1) // 2]
+        return at_corners.at[dr + 1 + (dc + 1) // 2]
+
+    def landed(i):
+        return place(i, rim_rows, rim_cols, rim_corners)
 
     def send_rims(which):
         for i in which:
-            r0, rl = span(NEAR[i][0], tile, half)
-            c0, cl = span(NEAR[i][1], tile, half)
-            rim_copies.append(send(rim_ref.at[:, r0:r0 + rl, c0:c0 + cl], landed(i), near[i]))
+            rim_copies.append(send(place(i, rows_ref, cols_ref, corners_ref), landed(i), near[i]))
 
     send_rims([1, 6])
     pair.wait_recv()
@@ -185,9 +186,8 @@
     send.finish()
 
 
-def post_call(rim, core, obj, grad, rows, cols, scale):
-    tile, wide = obj.shape[1], rim.shape[1]
-    half = (wide - tile) // 2
+def post_call(rims, core, obj, grad, rows, cols, scale):
+    tile, half = obj.shape[1], rims[0].shape[2]
     total = grad.shape[0]
     ys, n = rows // 2, total // 2
     na, nb, fin = n // ys, n // cols, n // (ys * cols)
@@ -196,7 +196,7 @@
     return pl.pallas_call(
         functools.partial(post_kernel, rows, cols, tile, half, scale),
         out_shape=[jax.ShapeDtypeStruct(obj.shape, F32), jax.ShapeDtypeStruct((2, 2, n, 128), BF16)],
-        in_specs=[V, V, V, V],
+        in_specs=[V] * 6,
         out_specs=[V, V],
         scratch_shapes=[
             pltpu.VMEM((tile, tile), F32),
@@ -217,7 +217,7 @@
         ],
         compiler_params=pltpu.CompilerParams(collective_id=1, has_side_effects=True, vmem_limit_bytes=40 * 2**20),
         name="post",
-    )(rim, core, obj, grad)
+    )(*rims, core, obj, grad)
 
 
 def pre_kernel(rows, cols, tile, half, owner_ref, offsets_ref, obj_ref, ext_ref, meta_ref, mine, gsend, grecv, lsem):
@@ -285,7 +285,7 @@
     fetch.start()
 
     def clear(p, carry):
-        for k in range(4):
+        for k in range(8):
             list_ref[p, k] = 0
         return carry
 
@@ -303,8 +303,10 @@
         def _():
             list_ref[count, 0] = 1
             list_ref[count, 1] = s
-            list_ref[count, 2] = r
-            list_ref[count, 3] = c
+            list_ref[count, 2] = r // 8
+            list_ref[count, 3] = lax.rem(r, 8)
+            list_ref[count, 4] = c // 128
+            list_ref[count, 5] = lax.rem(c, 128)
         return count + live
 
     lax.fori_loop(0, cols, scan, 0)
@@ -332,13 +334,12 @@
     def visit(p, carry):
         @pl.when(list_ref[p, 0] == 1)
         def _():
-            r, c = list_ref[p, 2], list_ref[p, 3]
-            c0 = pl.multiple_of((c // 128) * 128, 128)
-            r0 = pl.multiple_of((r // 8) * 8, 8)
+            r0 = pl.multiple_of(list_ref[p, 2] * 8, 8)
+            c0 = pl.multiple_of(list_ref[p, 4] * 128, 128)
             for q in range(2):
                 w = ext[q, pl.ds(r0, tall), pl.ds(c0, wide)]
-                w = pltpu.roll(w, wide - (c - c0), 1)[:, :side]
-                patch[p, q] = pltpu.roll(w, tall - (r - r0), 0)[:side]
+                w = pltpu.roll(w, wide - list_ref[p, 5], 1)[:, :side]
+                patch[p, q] = pltpu.roll(w, tall - list_ref[p, 3], 0)[:side]
 
         @pl.when(list_ref[p, 0] == 0)
         def _():
@@ -363,7 +364,7 @@
     S = pl.BlockSpec(memory_space=pltpu.SMEM)
     return pl.pallas_call(
         functools.partial(cut_kernel, rows, cols, tile, side // 2, held),
-        out_shape=[jax.ShapeDtypeStruct((most, 2, side, side), F32), jax.ShapeDtypeStruct((most, 4), jnp.int32)],
+        out_shape=[jax.ShapeDtypeStruct((most, 2, side, side), F32), jax.ShapeDtypeStruct((most, 8), jnp.int32)],
         in_specs=[S, A],
         out_specs=[A, S],
         scratch_shapes=[
@@ -546,7 +547,7 @@
     )(items, owner, amp, patch, probe, tab)
 
 
-def place_kernel(tile, half, list_ref, placed_hbm, pow_ref, rim_ref, core_ref, placed_ref, psem, num, shift):
+def place_kernel(tile, half, list_ref, placed_hbm, pow_ref, rows_ref, cols_ref, corners_ref, core_ref, placed_ref, psem, num, shift):
     side = 2 * half
     big, tall, wide = tile + side, side + 8, side + 128
 
@@ -567,19 +568,27 @@
 
         @pl.when(list_ref[p, 0] == 1)
         def _():
-            r, c = list_ref[p, 2], list_ref[p, 3]
-            c0 = pl.multiple_of((c // 128) * 128, 128)
-            r0 = pl.multiple_of((r // 8) * 8, 8)
+            r0 = pl.multiple_of(list_ref[p, 2] * 8, 8)
+            c0 = pl.multiple_of(list_ref[p, 4] * 128, 128)
             for q in range(3):
                 if q < 2:
                     shift[q, :side, :side] = placed_ref[p, q]
-                w = pltpu.roll(pltpu.roll(shift[q], r - r0, 0), c - c0, 1)
+                w = pltpu.roll(pltpu.roll(shift[q], list_ref[p, 3], 0), list_ref[p, 5], 1)
                 num[q, pl.ds(r0, tall), pl.ds(c0, wide)] += w
         return carry
 
     lax.fori_loop(0, list_ref.shape[0], visit, 0)
     for q in range(3):
-        rim_ref[q] = num[q].astype(BF16)
+        for dr, dc in NEAR:
+            r0, rl = span(dr, tile, half)
+            c0, cl = span(dc, tile, half)
+            rim = num[q, r0:r0 + rl, c0:c0 + cl].astype(BF16)
+            if dc == 0:
+                rows_ref[(dr + 1) // 2, q] = rim
+            elif dr == 0:
+                cols_ref[(dc + 1) // 2, q] = rim
+            else:
+                corners_ref[dr + 1 + (dc + 1) // 2, q] = rim
         core_ref[q] = num[q, half:big - half, half:big - half]
 
 
@@ -591,28 +600,53 @@
     S = pl.BlockSpec(memory_space=pltpu.SMEM)
     return pl.pallas_call(
         functools.partial(place_kernel, tile, half),
-        out_shape=[jax.ShapeDtypeStruct((3, big, big), BF16), jax.ShapeDtypeStruct((3, tile, tile), F32)],
+        out_shape=[
+            jax.ShapeDtypeStruct((2, 3, half, tile), BF16),
+            jax.ShapeDtypeStruct((2, 3, tile, half), BF16),
+            jax.ShapeDtypeStruct((4, 3, half, half), BF16),
+            jax.ShapeDtypeStruct((3, tile, tile), F32)],
         in_specs=[S, pl.BlockSpec(memory_space=pltpu.HBM), V],
-        out_specs=[V, V],
+        out_specs=[V, V, V, V],
         scratch_shapes=[
             pltpu.VMEM(placed.shape, F32),
             pltpu.SemaphoreType.DMA((placed.shape[0],)),
             pltpu.VMEM((3, big, big), F32), pltpu.VMEM((3, side + 8, side + 128), F32)],
-        compiler_params=pltpu.CompilerParams(vmem_limit_bytes=50 * 2**20),
+        compiler_params=pltpu.CompilerParams(vmem_limit_bytes=46 * 2**20),
         name="place",
     )(items, placed, power)
 
 
-def widen_kernel(got_ref, out_ref):
+def finish_kernel(obj_ref, got_ref, out_hbm, grad_hbm, wide, sem):
     n = got_ref.shape[2]
-    for c in range(2):
-        for k in range(2):
-            out_ref[c * n:(c + 1) * n, 128 * k:128 * (k + 1)] = got_ref[c, k].astype(F32)
-
-
-def widen_call(got):
+    whole = pltpu.make_async_copy(obj_ref, out_hbm, sem.at[4])
+    whole.start()
+    parts = []
+    for k in range(4):
+        c, at = k // 2, (k % 2) * (n // 2)
+        rows_k = pl.ds(k * (n // 2), n // 2)
+        for h in range(2):
+            wide[rows_k, 128 * h:128 * (h + 1)] = got_ref[c, h, at:at + n // 2].astype(F32)
+        part = pltpu.make_async_copy(wide.at[rows_k], grad_hbm.at[rows_k], sem.at[k])
+        part.start()
+        parts.append(part)
+    for part in parts:
+        part.wait()
+    whole.wait()
+
+
+def finish_call(obj, got):
     n = got.shape[2]
-    return pl.pallas_call(widen_kernel, out_shape=jax.ShapeDtypeStruct((2 * n, 256), F32), name="widen")(got)
+    V = pl.BlockSpec(memory_space=pltpu.VMEM)
+    A = pl.BlockSpec(memory_space=pltpu.HBM)
+    return pl.pallas_call(
+        finish_kernel,
+        out_shape=[jax.ShapeDtypeStruct(obj.shape, F32), jax.ShapeDtypeStruct((2 * n, 256), F32)],
+        in_specs=[V, V],
+        out_specs=[A, A],
+        scratch_shapes=[pltpu.VMEM((2 * n, 256), F32), pltpu.SemaphoreType.DMA((5,))],
+        compiler_params=pltpu.CompilerParams(vmem_limit_bytes=16 * 2**20),
+        name="finish",
+    )(obj, got)
 
 
 def on_device(object_field, probe, amplitudes, owner, offsets):
@@ -623,10 +657,11 @@
     ext, meta = pre_call(owner, offsets, object_field, side, rows, cols)
     patch, items = cut_call(meta, ext, tile, rows, cols, held, most)
     placed, grad, power = main_call(items, owner, amplitudes, patch, probe, rows, cols)
-    rim, core = place_call(items, placed, power, tile)
+    *rims, core = place_call(items, placed, power, tile)
     scale = 1.0 / math.sqrt(rows * cols * held)
-    object_out, gradient = post_call(rim, core, object_field, grad, rows, cols, scale)
-    return (object_out, widen_call(gradient).reshape(probe.shape))
+    object_out, gradient = post_call(rims, core, object_field, grad, rows, cols, scale)
+    object_out, gradient = finish_call(object_out, gradient)
+    return (object_out, gradient.reshape(probe.shape))
 
 
 def solution(mesh):

time: 161 us -> 155 us (0.963)
  local copies, waits for them, and re-layouts: 6.57 us -> 2.29 us
  Pallas kernels: 153 us -> 151 us
    pallas_call x1, Pallas kernels: 56.5 us -> 51.9 us  [post_call(): pl.pallas_call(functools.partial(post_kernel, rows, cols, tile, half, sca...]
    unnamed x14 -> x9, local copies, waits for them, and re-layouts: 6.57 us -> 2.29 us
    pallas_call x1, Pallas kernels: 6.07 us -> 9.91 us  [place_call(): pl.pallas_call(functools.partial(place_kernel, tile, half), out_shape=[ja...]
    pallas_call x1, Pallas kernels: 50.4 us -> 47 us  [main_call(): pl.pallas_call(functools.partial(main_kernel, rows, cols), out_shape=[jax...]
    pallas_call x1, Pallas kernels: 7.02 us -> 9.75 us  [cut_call(): pl.pallas_call(functools.partial(cut_kernel, rows, cols, tile, side // 2,...]
where the time goes in v5:
time: 155 us; the launch traced here: 154 us
  Pallas kernels  151 us (97%)
  local copies, waits for them, and re-layouts  2.29 us (1%)
    pallas_call x1, Pallas kernels, post_call(): pl.pallas_call(functools.partial(post_kernel, rows, cols, tile, half, sca...  51.9 us
    pallas_call x1, Pallas kernels, main_call(): pl.pallas_call(functools.partial(main_kernel, rows, cols), out_shape=[jax...  47 us
    pallas_call x1, Pallas kernels, pre_call(): pl.pallas_call(functools.partial(pre_kernel, rows, cols, tile, half), out...  30.7 us
    pallas_call x1, Pallas kernels, place_call(): pl.pallas_call(functools.partial(place_kernel, tile, half), out_shape=[ja...  9.91 us
    pallas_call x1, Pallas kernels, cut_call(): pl.pallas_call(functools.partial(cut_kernel, rows, cols, tile, side // 2,...  9.75 us

profile of v5, /device:TPU:1, one launch (start us, length us, event | category | flops | bytes accessed | tf_op | source)
XLA Modules:
  0.0 154.3 jit_solution(10693765384658943564)
XLA Ops:
  0.6 1.3 copy.9.offsets_ref
  2.0 30.7 %pre.1 = (f32[2,768,768]{2,1,0:T(8,128)}, s32[16,1,128]{2,1,0:T(1,128)}) custom-call(s32[4]{0:T(128)} %owner_ref.3, s32[4,2]{1,0:T(4,128)} %copy.9.offsets_ref, f32[2,512,512]{2,1,0:T(8,128)} %obj_ref.3), custom_call_target="tpu_custom_call" | custom-call | tf_op jit(solution)/shard_map/pre/pallas_call | solution.py:264
  32.7 9.8 %cut.1 = (f32[12,2,256,256]{3,2,1,0:T(8,128)}, s32[12,8]{1,0:T(8,128)}) custom-call(s32[16,1,128]{2,1,0:T(1,128)} %get-tuple-element.17.meta_ref, f32[2,768,768]{2,1,0:T(8,128)} %get-tuple-element.18.ext_hbm), custom_call_target="tpu_custom_call" | custom-call | tf_op jit(solution)/shard_map/cut/pallas_call | solution.py:365
  42.5 0.0 copy-start.3
  42.5 47.0 %main.1 = (f32[12,2,256,256]{3,2,1,0:T(8,128)}, f32[2048,256]{1,0:T(8,128)}, f32[256,256]{1,0:T(8,128)}) custom-call(s32[12,8]{1,0:T(8,128)} %get-tuple-element.19.list_ref, s32[4]{0:T(128)} %owner_ref.3, bf16[4,256,256]{2,1,0:T(8,128)(2,1)} %amp_hbm.1, f32[12,2,256,256]{3,2,1,0:T(8,128)} %get-tuple-element.20.patch_hbm, f32[4,2,256,256]{3,2,1,0:T(8,128)} %probe_hbm.1, ...), custom_call_target="tpu_custom_call" | custom-call | tf_op jit(solution)/shard_map/main/pallas_call | solution.py:517
  89.5 0.0 copy-done.3
  89.5 0.0 copy-start.2
  89.5 0.9 copy-done.2
  90.5 0.0 copy-start
  90.5 0.0 copy-start.1
  90.5 9.9 %place.1 = (bf16[2,3,128,512]{3,2,1,0:T(8,128)(2,1)S(1)}, bf16[2,3,512,128]{3,2,1,0:T(8,128)(2,1)S(1)}, bf16[4,3,128,128]{3,2,1,0:T(8,128)(2,1)S(1)}, f32[3,512,512]{2,1,0:T(8,128)S(1)}) custom-call(s32[12,8]{1,0:T(8,128)S(1)} %copy-done.3, f32[12,2,256,256]{3,2,1,0:T(8,128)} %get-tuple-element.21.placed_hbm, f32[256,256]{1,0:T(8,128)S(1)} %copy-done.2), custom_call_target="tpu_custom_call" | custom-call | tf_op jit(solution)/shard_map/place/pallas_call | solution.py:601
  100.4 0.0 copy-done
  100.4 0.0 copy-done.1
  100.4 51.9 %post.1 = (f32[2,512,512]{2,1,0:T(8,128)S(1)}, bf16[2,2,1024,128]{3,2,1,0:T(8,128)(2,1)S(1)}) custom-call(bf16[2,3,128,512]{3,2,1,0:T(8,128)(2,1)S(1)} %get-tuple-element.23.rows_ref, bf16[2,3,512,128]{3,2,1,0:T(8,128)(2,1)S(1)} %get-tuple-element.24.cols_ref, bf16[4,3,128,128]{3,2,1,0:T(8,128)(2,1)S(1)} %get-tuple-element.25.corners_ref, ...), custom_call_target="tpu_custom_call" | custom-call | tf_op jit(solution)/shard_map/post/pallas_call | solution.py:196
  152.3 2.0 %finish.1 = (f32[2,512,512]{2,1,0:T(8,128)}, f32[2048,256]{1,0:T(8,128)}) custom-call(f32[2,512,512]{2,1,0:T(8,128)S(1)} %get-tuple-element.28.obj_ref, bf16[2,2,1024,128]{3,2,1,0:T(8,128)(2,1)S(1)} %get-tuple-element.29.got_ref), custom_call_target="tpu_custom_call" | custom-call | tf_op jit(solution)/shard_map/finish/pallas_call | solution.py:641
Async XLA Ops:
  42.5 47.0 %copy-start.3 = (s32[12,8]{1,0:T(8,128)S(1)}, s32[12,8]{1,0:T(8,128)}, u32[]{:S(2)}) copy-start(s32[12,8]{1,0:T(8,128)} %get-tuple-element.19.list_ref) | copy-start | bytes 1156
  89.5 1.0 copy-start.2
  90.5 9.9 %copy-start = (f32[2,512,512]{2,1,0:T(8,128)S(1)}, f32[2,512,512]{2,1,0:T(8,128)}, u32[]{:S(2)}) copy-start(f32[2,512,512]{2,1,0:T(8,128)} %obj_ref.3) | copy-start | bytes 6291460
  90.5 9.9 %copy-start.1 = (f32[2048,256]{1,0:T(8,128)S(1)}, f32[2048,256]{1,0:T(8,128)}, u32[]{:S(2)}) copy-start(f32[2048,256]{1,0:T(8,128)} %get-tuple-element.27.grad_ref) | copy-start | bytes 6291460

commit v6 on v5

--- a/solution.py
+++ b/solution.py
@@ -22,6 +22,30 @@
 
 def dot(a, b):
     return jnp.dot(a, b, preferred_element_type=F32)
+
+def moved_back(w, rows, lanes):
+    tall, wide = w.shape
+    t = pltpu.roll(w.reshape(tall // 8, 8, wide), lax.rem(8 - rows, 8), 1)
+    sub = lax.broadcasted_iota(jnp.int32, (tall // 8 - 1, 8, wide), 1)
+    w = jnp.where(sub < 8 - rows, t[:-1], t[1:]).reshape(tall - 8, wide)
+    lane = lax.broadcasted_iota(jnp.int32, (tall - 8, 128), 1)
+    parts = [pltpu.roll(w[:, k:k + 128], lax.rem(128 - lanes, 128), 1) for k in range(0, wide, 128)]
+    return jnp.concatenate([jnp.where(lane < 128 - lanes, a, b) for a, b in zip(parts[:-1], parts[1:])], 1)
+
+
+def moved_on(w, rows, lanes):
+    tall, wide = w.shape
+    lane = lax.broadcasted_iota(jnp.int32, (tall, 128), 1)
+    none = jnp.zeros((tall, 128), F32)
+    parts = [none] + [pltpu.roll(w[:, k:k + 128], lanes, 1) for k in range(0, wide, 128)] + [none]
+    w = jnp.concatenate([jnp.where(lane < lanes, a, b) for a, b in zip(parts[:-1], parts[1:])], 1)
+    wide += 128
+    t = pltpu.roll(w.reshape(tall // 8, 8, wide), rows, 1)
+    none = jnp.zeros((1, 8, wide), F32)
+    sub = lax.broadcasted_iota(jnp.int32, (tall // 8 + 1, 8, wide), 1)
+    both = jnp.where(sub < rows, jnp.concatenate([none, t], 0), jnp.concatenate([t, none], 0))
+    return both.reshape(tall + 8, wide)
+
 
 def around(row, col, dr, dc, rows, cols):
     return lax.rem(row + dr + rows, rows), lax.rem(col + dc + cols, cols)
@@ -220,7 +244,8 @@
     )(*rims, core, obj, grad)
 
 
-def pre_kernel(rows, cols, tile, half, owner_ref, offsets_ref, obj_ref, ext_ref, meta_ref, mine, gsend, grecv, lsem):
+def pre_kernel(rows, cols, tile, half, owner_ref, offsets_ref, obj_ref, ext_ref, meta_ref,
+               mine, out_rows, out_cols, in_rows, in_cols, in_corners, gsend, grecv, lsem):
     row, col = lax.axis_index("row"), lax.axis_index("col")
     near = [around(row, col, dr, dc, rows, cols) for dr, dc in NEAR]
     c_peers = column_peers(row, col, cols)
@@ -234,17 +259,41 @@
         for k in range(2):
             note = jnp.where(lane == held + 2 * h + k, offsets_ref[h, k], note)
     mine[...] = note
+    core.wait()
+    lead, end = 16, half + tile
+
+    def code(out, x):
+        top = jnp.max(jnp.abs(x), axis=0, keepdims=True)
+        power = jnp.floor(jnp.log2(jnp.maximum(top, 1e-30)))
+        out[:lead] = jnp.broadcast_to(power, (lead, x.shape[1])).astype(jnp.int32).astype(jnp.int16)
+        x = jnp.clip(jnp.round(x * jnp.exp2(14.0 - power)), -32767.0, 32767.0)
+        out[lead:] = x.astype(jnp.int32).astype(jnp.int16)
+
+    for q in range(2):
+        for k, at in enumerate((half, end - half)):
+            code(out_rows.at[k, q], ext_ref[q, at:at + half, half:end])
+            code(out_cols.at[k, q], ext_ref[q, half:end, at:at + half])
     greet(c_peers + near)
-    core.wait()
     send = Sends(gsend, grecv)
     got = []
+
+    def edge(dr, dc):
+        if dc == 0:
+            return out_rows.at[(dr + 1) // 2]
+        if dr == 0:
+            return out_cols.at[(dc + 1) // 2]
+        at = 0 if dc < 0 else tile - half
+        return out_rows.at[(dr + 1) // 2, :, :, at:at + half]
+
+    def landed(dr, dc):
+        if dc == 0:
+            return in_rows.at[(dr + 1) // 2]
+        if dr == 0:
+            return in_cols.at[(dc + 1) // 2]
+        return in_corners.at[dr + 1 + (dc + 1) // 2]
+
     for i, (dr, dc) in enumerate(NEAR):
-        r0, rl = {-1: (0, half), 0: (0, tile), 1: (tile - half, half)}[dr]
-        c0, cl = {-1: (0, half), 0: (0, tile), 1: (tile - half, half)}[dc]
-        tr, _ = span(-dr, tile, half)
-        tc, _ = span(-dc, tile, half)
-        r0, c0 = r0 + half, c0 + half
-        got.append(send(ext_ref.at[:, r0:r0 + rl, c0:c0 + cl], ext_ref.at[:, tr:tr + rl, tc:tc + cl], near[i]))
+        got.append(send(edge(dr, dc), landed(dr, dc), near[i]))
     for s in range(cols - 1):
         got.append(send(mine, meta_ref.at[col], c_peers[s]))
     own = pltpu.make_async_copy(mine, meta_ref.at[col], lsem.at[1])
@@ -252,7 +301,31 @@
     for c in got:
         c.wait_recv()
     own.wait()
+    for dr, dc in NEAR:
+        tr, rl = span(-dr, tile, half)
+        tc, cl = span(-dc, tile, half)
+        ref = landed(dr, dc)
+        for q in range(2):
+            power = ref[q, :lead].astype(jnp.int32).astype(F32)[:1]
+            ext_ref[q, tr:tr + rl, tc:tc + cl] = ref[q, lead:].astype(jnp.int32).astype(F32) * jnp.exp2(power - 14.0)
     send.finish()
+    big = tile + 2 * half
+
+    @pl.when(row == 0)
+    def _():
+        ext_ref[:, :half, :] = jnp.zeros((2, half, big), F32)
+
+    @pl.when(row == rows - 1)
+    def _():
+        ext_ref[:, big - half:, :] = jnp.zeros((2, half, big), F32)
+
+    @pl.when(col == 0)
+    def _():
+        ext_ref[:, :, :half] = jnp.zeros((2, big, half), F32)
+
+    @pl.when(col == cols - 1)
+    def _():
+        ext_ref[:, :, big - half:] = jnp.zeros((2, big, half), F32)
 
 
 def pre_call(owner, offsets, obj, side, rows, cols):
@@ -268,21 +341,24 @@
         out_specs=[V, V],
         scratch_shapes=[
             pltpu.VMEM((1, 128), jnp.int32),
+            pltpu.VMEM((2, 2, half + 16, tile), jnp.int16),
+            pltpu.VMEM((2, 2, tile + 16, half), jnp.int16),
+            pltpu.VMEM((2, 2, half + 16, tile), jnp.int16),
+            pltpu.VMEM((2, 2, tile + 16, half), jnp.int16),
+            pltpu.VMEM((4, 2, half + 16, half), jnp.int16),
             pltpu.SemaphoreType.DMA((copies,)),
             pltpu.SemaphoreType.DMA((copies,)),
             pltpu.SemaphoreType.DMA((2,)),
         ],
-        compiler_params=pltpu.CompilerParams(collective_id=0, has_side_effects=True, vmem_limit_bytes=57 * 2**20),
+        compiler_params=pltpu.CompilerParams(collective_id=0, has_side_effects=True, vmem_limit_bytes=32 * 2**20),
         name="pre",
     )(owner, offsets, obj)
 
 
-def cut_kernel(rows, cols, tile, half, held, meta_ref, ext_hbm, patch_hbm, list_ref, ext, patch, esem, osem):
-    row, col = lax.axis_index("row"), lax.axis_index("col")
+def cut_kernel(cols, half, held, meta_ref, ext, patch_hbm, list_ref, patch, osem):
+    col = lax.axis_index("col")
     side = 2 * half
-    big, tall, wide, most = tile + side, side + 8, side + 128, list_ref.shape[0]
-    fetch = pltpu.make_async_copy(ext_hbm, ext, esem)
-    fetch.start()
+    tall, wide, most = side + 8, side + 128, list_ref.shape[0]
 
     def clear(p, carry):
         for k in range(8):
@@ -310,23 +386,6 @@
         return count + live
 
     lax.fori_loop(0, cols, scan, 0)
-    fetch.wait()
-
-    @pl.when(row == 0)
-    def _():
-        ext[:, :half, :] = jnp.zeros((2, half, big), F32)
-
-    @pl.when(row == rows - 1)
-    def _():
-        ext[:, big - half:, :] = jnp.zeros((2, half, big), F32)
-
-    @pl.when(col == 0)
-    def _():
-        ext[:, :, :half] = jnp.zeros((2, big, half), F32)
-
-    @pl.when(col == cols - 1)
-    def _():
-        ext[:, :, big - half:] = jnp.zeros((2, big, half), F32)
 
     def out(p):
         return pltpu.make_async_copy(patch.at[p], patch_hbm.at[p], osem.at[p])
@@ -338,8 +397,7 @@
             c0 = pl.multiple_of(list_ref[p, 4] * 128, 128)
             for q in range(2):
                 w = ext[q, pl.ds(r0, tall), pl.ds(c0, wide)]
-                w = pltpu.roll(w, wide - list_ref[p, 5], 1)[:, :side]
-                patch[p, q] = pltpu.roll(w, tall - list_ref[p, 3], 0)[:side]
+                patch[p, q] = moved_back(w, list_ref[p, 3], list_ref[p, 5])
 
         @pl.when(list_ref[p, 0] == 0)
         def _():
@@ -357,23 +415,21 @@
     lax.fori_loop(0, most, drain, 0)
 
 
-def cut_call(meta, ext, tile, rows, cols, held, most):
+def cut_call(meta, ext, tile, cols, held, most):
     big = ext.shape[1]
     side = big - tile
     A = pl.BlockSpec(memory_space=pltpu.HBM)
     S = pl.BlockSpec(memory_space=pltpu.SMEM)
     return pl.pallas_call(
-        functools.partial(cut_kernel, rows, cols, tile, side // 2, held),
+        functools.partial(cut_kernel, cols, side // 2, held),
         out_shape=[jax.ShapeDtypeStruct((most, 2, side, side), F32), jax.ShapeDtypeStruct((most, 8), jnp.int32)],
-        in_specs=[S, A],
+        in_specs=[S, pl.BlockSpec(memory_space=pltpu.VMEM)],
         out_specs=[A, S],
         scratch_shapes=[
-            pltpu.VMEM((2, big, big), F32),
             pltpu.VMEM((most, 2, side, side), F32),
-            pltpu.SemaphoreType.DMA,
             pltpu.SemaphoreType.DMA((most,)),
         ],
-        compiler_params=pltpu.CompilerParams(vmem_limit_bytes=57 * 2**20),
+        compiler_params=pltpu.CompilerParams(vmem_limit_bytes=47 * 2**20),
         name="cut",
     )(meta, ext)
 
@@ -547,7 +603,7 @@
     )(items, owner, amp, patch, probe, tab)
 
 
-def place_kernel(tile, half, list_ref, placed_hbm, pow_ref, rows_ref, cols_ref, corners_ref, core_ref, placed_ref, psem, num, shift):
+def place_kernel(tile, half, list_ref, placed_hbm, pow_ref, rows_ref, cols_ref, corners_ref, core_ref, placed_ref, psem, num):
     side = 2 * half
     big, tall, wide = tile + side, side + 8, side + 128
 
@@ -560,8 +616,6 @@
 
     lax.fori_loop(0, list_ref.shape[0], start, 0)
     num[...] = jnp.zeros_like(num)
-    shift[...] = jnp.zeros_like(shift)
-    shift[2, :side, :side] = pow_ref[...]
 
     def visit(p, carry):
         fetch(p).wait()
@@ -571,9 +625,7 @@
             r0 = pl.multiple_of(list_ref[p, 2] * 8, 8)
             c0 = pl.multiple_of(list_ref[p, 4] * 128, 128)
             for q in range(3):
-                if q < 2:
-                    shift[q, :side, :side] = placed_ref[p, q]
-                w = pltpu.roll(pltpu.roll(shift[q], list_ref[p, 3], 0), list_ref[p, 5], 1)
+                w = moved_on(placed_ref[p, q] if q < 2 else pow_ref[...], list_ref[p, 3], list_ref[p, 5])
                 num[q, pl.ds(r0, tall), pl.ds(c0, wide)] += w
         return carry
 
@@ -610,7 +662,7 @@
         scratch_shapes=[
             pltpu.VMEM(placed.shape, F32),
             pltpu.SemaphoreType.DMA((placed.shape[0],)),
-            pltpu.VMEM((3, big, big), F32), pltpu.VMEM((3, side + 8, side + 128), F32)],
+            pltpu.VMEM((3, big, big), F32)],
         compiler_params=pltpu.CompilerParams(vmem_limit_bytes=46 * 2**20),
         name="place",
     )(items, placed, power)
@@ -655,7 +707,7 @@
     most = 4 * (held - 1)
     side, tile = probe.shape[-1], object_field.shape[1]
     ext, meta = pre_call(owner, offsets, object_field, side, rows, cols)
-    patch, items = cut_call(meta, ext, tile, rows, cols, held, most)
+    patch, items = cut_call(meta, ext, tile, cols, held, most)
     placed, grad, power = main_call(items, owner, amplitudes, patch, probe, rows, cols)
     *rims, core = place_call(items, placed, power, tile)
     scale = 1.0 / math.sqrt(rows * cols * held)

time: 155 us -> 140 us (0.903)
  Pallas kernels: 151 us -> 134 us
  local copies, waits for them, and re-layouts: 2.29 us -> 4.56 us
    pallas_call x1, Pallas kernels: 30.7 us -> 21.2 us  [pre_call(): pl.pallas_call(functools.partial(pre_kernel, rows, cols, tile, half), out...]
    pallas_call x1, Pallas kernels: 9.91 us -> 6.05 us  [place_call(): pl.pallas_call(functools.partial(place_kernel, tile, half), out_shape=[ja...]
    pallas_call x1, Pallas kernels: 9.75 us -> 6.4 us  [cut_call(): pl.pallas_call(functools.partial(cut_kernel, cols, side // 2, held), out_...]
    unnamed x9 -> x15, local copies, waits for them, and re-layouts: 2.29 us -> 4.56 us
    pallas_call x1, Pallas kernels: 51.9 us -> 50.2 us  [post_call(): pl.pallas_call(functools.partial(post_kernel, rows, cols, tile, half, sca...]
where the time goes in v6:
time: 140 us; the launch traced here: 139 us
  Pallas kernels  134 us (96%)
  local copies, waits for them, and re-layouts  4.56 us (3%)
    pallas_call x1, Pallas kernels, post_call(): pl.pallas_call(functools.partial(post_kernel, rows, cols, tile, half, sca...  50.2 us
    pallas_call x1, Pallas kernels, main_call(): pl.pallas_call(functools.partial(main_kernel, rows, cols), out_shape=[jax...  48.1 us
    pallas_call x1, Pallas kernels, pre_call(): pl.pallas_call(functools.partial(pre_kernel, rows, cols, tile, half), out...  21.2 us
    pallas_call x1, Pallas kernels, cut_call(): pl.pallas_call(functools.partial(cut_kernel, cols, side // 2, held), out_...  6.4 us
    pallas_call x1, Pallas kernels, place_call(): pl.pallas_call(functools.partial(place_kernel, tile, half), out_shape=[ja...  6.05 us
    unnamed x15, local copies, waits for them, and re-layouts  4.56 us

profile of v6, /device:TPU:1, one launch (start us, length us, event | category | flops | bytes accessed | tf_op | source)
XLA Modules:
  0.0 139.3 jit_solution(16356095876816723652)
XLA Ops:
  0.6 0.8 copy.9.offsets_ref
  1.4 0.0 copy-start
  1.4 1.6 %copy-done = f32[2,512,512]{2,1,0:T(8,128)S(1)} copy-done((f32[2,512,512]{2,1,0:T(8,128)S(1)}, f32[2,512,512]{2,1,0:T(8,128)}, u32[]{:S(2)}) %copy-start) | copy-done | bytes 2097176
  3.0 0.0 copy-start.6
  3.0 0.7 copy-done.6
  3.6 21.2 %pre.1 = (f32[2,768,768]{2,1,0:T(8,128)S(1)}, s32[16,1,128]{2,1,0:T(1,128)S(1)}) custom-call(s32[4]{0:T(128)S(1)} %copy-done.6, s32[4,2]{1,0:T(4,128)S(1)} %copy.9.offsets_ref, f32[2,512,512]{2,1,0:T(8,128)S(1)} %copy-done), custom_call_target="tpu_custom_call" | custom-call | tf_op jit(solution)/shard_map/pre/pallas_call | solution.py:337
  24.8 6.4 %cut.1 = (f32[12,2,256,256]{3,2,1,0:T(8,128)}, s32[12,8]{1,0:T(8,128)S(1)}) custom-call(s32[16,1,128]{2,1,0:T(1,128)S(1)} %get-tuple-element.17.meta_ref, f32[2,768,768]{2,1,0:T(8,128)S(1)} %get-tuple-element.18.ext), custom_call_target="tpu_custom_call" | custom-call | tf_op jit(solution)/shard_map/cut/pallas_call | solution.py:423
  31.3 0.0 copy-start.4
  31.3 0.6 copy-done.4
  31.9 0.0 copy-start.5
  31.9 48.1 %main.1 = (f32[12,2,256,256]{3,2,1,0:T(8,128)}, f32[2048,256]{1,0:T(8,128)}, f32[256,256]{1,0:T(8,128)}) custom-call(s32[12,8]{1,0:T(8,128)} %copy-done.4, s32[4]{0:T(128)} %owner_ref.3, bf16[4,256,256]{2,1,0:T(8,128)(2,1)} %amp_hbm.1, f32[12,2,256,256]{3,2,1,0:T(8,128)} %get-tuple-element.20.patch_hbm, f32[4,2,256,256]{3,2,1,0:T(8,128)} %probe_hbm.1, ...), custom_call_target="tpu_custom_call" | custom-call | tf_op jit(solution)/shard_map/main/pallas_call | solution.py:573
  80.0 0.0 copy-done.5
  80.0 0.0 copy-start.3
  80.0 0.9 copy-done.3
  81.0 0.0 copy-start.1
  81.0 0.0 copy-start.2
  81.0 6.0 %place.1 = (bf16[2,3,128,512]{3,2,1,0:T(8,128)(2,1)S(1)}, bf16[2,3,512,128]{3,2,1,0:T(8,128)(2,1)S(1)}, bf16[4,3,128,128]{3,2,1,0:T(8,128)(2,1)S(1)}, f32[3,512,512]{2,1,0:T(8,128)S(1)}) custom-call(s32[12,8]{1,0:T(8,128)S(1)} %copy-done.5, f32[12,2,256,256]{3,2,1,0:T(8,128)} %get-tuple-element.21.placed_hbm, f32[256,256]{1,0:T(8,128)S(1)} %copy-done.3), custom_call_target="tpu_custom_call" | custom-call | tf_op jit(solution)/shard_map/place/pallas_call | solution.py:653
  87.0 0.0 copy-done.1
  87.1 0.0 copy-done.2
  87.1 50.2 %post.1 = (f32[2,512,512]{2,1,0:T(8,128)S(1)}, bf16[2,2,1024,128]{3,2,1,0:T(8,128)(2,1)S(1)}) custom-call(bf16[2,3,128,512]{3,2,1,0:T(8,128)(2,1)S(1)} %get-tuple-element.23.rows_ref, bf16[2,3,512,128]{3,2,1,0:T(8,128)(2,1)S(1)} %get-tuple-element.24.cols_ref, bf16[4,3,128,128]{3,2,1,0:T(8,128)(2,1)S(1)} %get-tuple-element.25.corners_ref, ...), custom_call_target="tpu_custom_call" | custom-call | tf_op jit(solution)/shard_map/post/pallas_call | solution.py:220
  137.2 2.0 %finish.1 = (f32[2,512,512]{2,1,0:T(8,128)}, f32[2048,256]{1,0:T(8,128)}) custom-call(f32[2,512,512]{2,1,0:T(8,128)S(1)} %get-tuple-element.28.obj_ref, bf16[2,2,1024,128]{3,2,1,0:T(8,128)(2,1)S(1)} %get-tuple-element.29.got_ref), custom_call_target="tpu_custom_call" | custom-call | tf_op jit(solution)/shard_map/finish/pallas_call | solution.py:693
Async XLA Ops:
  1.4 1.6 %copy-start = (f32[2,512,512]{2,1,0:T(8,128)S(1)}, f32[2,512,512]{2,1,0:T(8,128)}, u32[]{:S(2)}) copy-start(f32[2,512,512]{2,1,0:T(8,128)} %obj_ref.3) | copy-start | bytes 6291460
  3.0 0.7 copy-start.6
  31.3 0.6 copy-start.4
  31.9 48.2 %copy-start.5 = (s32[12,8]{1,0:T(8,128)S(1)}, s32[12,8]{1,0:T(8,128)}, u32[]{:S(2)}) copy-start(s32[12,8]{1,0:T(8,128)} %copy-done.4) | copy-start | bytes 1156
  80.0 1.0 copy-start.3
  81.0 6.1 %copy-start.1 = (f32[2,512,512]{2,1,0:T(8,128)S(1)}, f32[2,512,512]{2,1,0:T(8,128)}, u32[]{:S(2)}) copy-start(f32[2,512,512]{2,1,0:T(8,128)} %obj_ref.3) | copy-start | bytes 6291460
  81.0 6.1 %copy-start.2 = (f32[2048,256]{1,0:T(8,128)S(1)}, f32[2048,256]{1,0:T(8,128)}, u32[]{:S(2)}) copy-start(f32[2048,256]{1,0:T(8,128)} %get-tuple-element.27.grad_ref) | copy-start | bytes 6291460

commit v7 on v6

--- a/solution.py
+++ b/solution.py
@@ -62,11 +62,29 @@
     return {-1: (tile - half, half), 0: (0, tile), 1: (0, half)}[step]
 
 
-def column_peers(row, col, cols):
-    depth = 4
-    steps = [(0, 1), (1, 0), (0, 3), (3, 0), (1, 1), (3, 3), (1, 3), (3, 1), (2, 0), (0, 2), (2, 2), (1, 2), (3, 2), (2, 1), (2, 3)]
-    x, z = col // depth, lax.rem(col, depth)
-    return [(row, lax.rem(x + dx, cols // depth) * depth + lax.rem(z + dz, depth)) for dx, dz in steps]
+EARLY = [(1, 0), (3, 0), (2, 0), (2, 1), (2, 3), (2, 2)]
+LATE = [(0, 1), (0, 3), (1, 1), (3, 3), (1, 3), (3, 1), (0, 2), (1, 2), (3, 2)]
+DEPTH = 4
+
+
+def stepped(col, cols, step):
+    x, z = col // DEPTH, lax.rem(col, DEPTH)
+    return lax.rem(x + step[0], cols // DEPTH) * DEPTH + lax.rem(z + step[1], DEPTH)
+
+
+def column_peers(row, col, cols, steps):
+    return [(row, stepped(col, cols, step)) for step in steps]
+
+
+def senders(col, cols, steps):
+    return [stepped(col, cols, (cols // DEPTH - dx, DEPTH - dz)) for dx, dz in steps]
+
+
+def owned_by(to, owner_ref, held):
+    which = jnp.int32(0)
+    for h in range(1, held):
+        which = jnp.where(owner_ref[h] == to, h, which)
+    return which
 
 
 class Sends:
@@ -102,7 +120,7 @@
     ys = rows // 2
     other = (row + 1 - 2 * core, col)
     y_peers = [(lax.rem(y + s, ys) * 2 + core, col) for s in range(1, ys)]
-    c_peers = column_peers(row, col, cols)
+    c_peers = column_peers(row, col, cols, LATE + EARLY)
     near = [around(row, col, dr, dc, rows, cols) for dr, dc in NEAR]
     greet([other] + y_peers + c_peers + near)
     send = Sends(gsend, grecv)
@@ -244,14 +262,16 @@
     )(*rims, core, obj, grad)
 
 
-def pre_kernel(rows, cols, tile, half, owner_ref, offsets_ref, obj_ref, ext_ref, meta_ref,
-               mine, out_rows, out_cols, in_rows, in_cols, in_corners, gsend, grecv, lsem):
+def pre_kernel(rows, cols, tile, half, owner_ref, offsets_ref, obj_ref, amp_hbm, ext_ref, meta_ref, early_ref,
+               amp, slots, mine, out_rows, out_cols, in_rows, in_cols, in_corners, gsend, grecv, lsem):
     row, col = lax.axis_index("row"), lax.axis_index("col")
     near = [around(row, col, dr, dc, rows, cols) for dr, dc in NEAR]
-    c_peers = column_peers(row, col, cols)
+    c_peers = column_peers(row, col, cols, LATE + EARLY)
     held = owner_ref.shape[0]
     core = pltpu.make_async_copy(obj_ref, ext_ref.at[:, half:half + tile, half:half + tile], lsem.at[0])
     core.start()
+    own_amp = pltpu.make_async_copy(amp_hbm, amp, lsem.at[2])
+    own_amp.start()
     lane = lax.broadcasted_iota(jnp.int32, (1, 128), 1)
     note = jnp.zeros((1, 128), jnp.int32)
     for h in range(held):
@@ -296,6 +316,10 @@
         got.append(send(edge(dr, dc), landed(dr, dc), near[i]))
     for s in range(cols - 1):
         got.append(send(mine, meta_ref.at[col], c_peers[s]))
+    own_amp.wait()
+    for k, peer in enumerate(column_peers(row, col, cols, EARLY)):
+        slots[k] = amp[owned_by(peer[1], owner_ref, held)]
+        got.append(send(slots.at[k], early_ref.at[k], peer))
     own = pltpu.make_async_copy(mine, meta_ref.at[col], lsem.at[1])
     own.start()
     for c in got:
@@ -328,18 +352,24 @@
         ext_ref[:, :, big - half:] = jnp.zeros((2, big, half), F32)
 
 
-def pre_call(owner, offsets, obj, side, rows, cols):
+def pre_call(owner, offsets, obj, amp, rows, cols):
+    side, early = amp.shape[1], len(EARLY)
     tile, half = obj.shape[1], side // 2
     big = tile + side
-    copies = 8 + cols - 1
+    copies = 8 + cols - 1 + early
     V = pl.BlockSpec(memory_space=pltpu.VMEM)
     S = pl.BlockSpec(memory_space=pltpu.SMEM)
     return pl.pallas_call(
         functools.partial(pre_kernel, rows, cols, tile, half),
-        out_shape=[jax.ShapeDtypeStruct((2, big, big), F32), jax.ShapeDtypeStruct((cols, 1, 128), jnp.int32)],
-        in_specs=[S, S, pl.BlockSpec(memory_space=pltpu.HBM)],
-        out_specs=[V, V],
+        out_shape=[
+            jax.ShapeDtypeStruct((2, big, big), F32), jax.ShapeDtypeStruct((cols, 1, 128), jnp.int32),
+            jax.ShapeDtypeStruct((early, side, side), BF16),
+        ],
+        in_specs=[S, S, pl.BlockSpec(memory_space=pltpu.HBM), pl.BlockSpec(memory_space=pltpu.HBM)],
+        out_specs=[V, V, V],
         scratch_shapes=[
+            pltpu.VMEM(amp.shape, BF16),
+            pltpu.VMEM((early, side, side), BF16),
             pltpu.VMEM((1, 128), jnp.int32),
             pltpu.VMEM((2, 2, half + 16, tile), jnp.int16),
             pltpu.VMEM((2, 2, tile + 16, half), jnp.int16),
@@ -348,11 +378,11 @@
             pltpu.VMEM((4, 2, half + 16, half), jnp.int16),
             pltpu.SemaphoreType.DMA((copies,)),
             pltpu.SemaphoreType.DMA((copies,)),
-            pltpu.SemaphoreType.DMA((2,)),
+            pltpu.SemaphoreType.DMA((3,)),
         ],
         compiler_params=pltpu.CompilerParams(collective_id=0, has_side_effects=True, vmem_limit_bytes=32 * 2**20),
         name="pre",
-    )(owner, offsets, obj)
+    )(owner, offsets, obj, amp)
 
 
 def cut_kernel(cols, half, held, meta_ref, ext, patch_hbm, list_ref, patch, osem):
@@ -434,12 +464,12 @@
     )(meta, ext)
 
 
-def main_kernel(rows, cols, list_ref, owner_ref, amp_hbm, patch_hbm, probe_hbm, tab_hbm,
+def main_kernel(rows, cols, list_ref, owner_ref, amp_hbm, early_hbm, patch_hbm, probe_hbm, tab_hbm,
                 placed_hbm, grad_ref, pow_ref,
                 placed_ref, psem, slots, amps, amp, probe, tab, patch, far, total, ratio, ebuf, hbuf, ssum,
                 gsend, grecv, lsem):
     row, col = lax.axis_index("row"), lax.axis_index("col")
-    c_peers = column_peers(row, col, cols)
+    c_peers = column_peers(row, col, cols, LATE)
     held, side, modes, most = amp.shape[0], amp.shape[1], probe.shape[0], patch.shape[0]
     local = [
         pltpu.make_async_copy(amp_hbm, amp, lsem.at[0]),
@@ -449,20 +479,20 @@
     ]
     for copy in local:
         copy.start()
+    early = [
+        pltpu.make_async_copy(early_hbm.at[k], amps.at[at], lsem.at[4 + k])
+        for k, at in enumerate(senders(col, cols, EARLY))
+    ]
+    for copy in early:
+        copy.start()
     greet(c_peers)
     send = Sends(gsend, grecv)
     local[0].wait()
     amp_copies = []
-    for s in range(cols):
-        to = col if s == 0 else c_peers[s - 1][1]
-        which = jnp.int32(0)
-        for h in range(1, held):
-            which = jnp.where(owner_ref[h] == to, h, which)
-        if s == 0:
-            amps[col] = amp[which]
-        else:
-            slots[s] = amp[which]
-            amp_copies.append(send(slots.at[s], amps.at[col], c_peers[s - 1]))
+    for k, peer in enumerate(c_peers):
+        slots[k] = amp[owned_by(peer[1], owner_ref, held)]
+        amp_copies.append(send(slots.at[k], amps.at[col], peer))
+    amps[col] = amp[owned_by(col, owner_ref, held)]
     local[1].wait()
     power = jnp.zeros((side, side), F32)
     for m in range(modes):
@@ -512,6 +542,8 @@
         there(p, ebuf.at[0], hbuf.at[0])
     for copy in amp_copies:
         copy.wait_recv()
+    for copy in early:
+        copy.wait()
 
     def out(p):
         return pltpu.make_async_copy(placed_ref.at[p], placed_hbm.at[p], psem.at[p])
@@ -555,9 +587,9 @@
     send.finish()
 
 
-def main_call(items, owner, amp, patch, probe, rows, cols):
+def main_call(items, owner, amp, early, patch, probe, rows, cols):
     side, modes, most = amp.shape[1], probe.shape[0], patch.shape[0]
-    copies = cols - 1
+    copies = len(LATE)
     tr, ti = tables(side)
 
     def left(a, b):
@@ -577,12 +609,12 @@
             jax.ShapeDtypeStruct((modes * 2 * side, side), F32),
             jax.ShapeDtypeStruct((side, side), F32),
         ],
-        in_specs=[S, S, A, A, A, A],
+        in_specs=[S, S, A, A, A, A, A],
         out_specs=[A, V, V],
         scratch_shapes=[
             pltpu.VMEM((most, 2, side, side), F32),
             pltpu.SemaphoreType.DMA((most,)),
-            pltpu.VMEM((cols, side, side), BF16),
+            pltpu.VMEM((copies, side, side), BF16),
             pltpu.VMEM((cols, side, side), BF16),
             pltpu.VMEM(amp.shape, BF16),
             pltpu.VMEM(probe.shape, F32),
@@ -596,11 +628,11 @@
             pltpu.VMEM((side, side), F32),
             pltpu.SemaphoreType.DMA((copies,)),
             pltpu.SemaphoreType.DMA((copies,)),
-            pltpu.SemaphoreType.DMA((4,)),
+            pltpu.SemaphoreType.DMA((4 + len(EARLY),)),
         ],
         compiler_params=pltpu.CompilerParams(collective_id=2, has_side_effects=True, vmem_limit_bytes=62 * 2**20),
         name="main",
-    )(items, owner, amp, patch, probe, tab)
+    )(items, owner, amp, early, patch, probe, tab)
 
 
 def place_kernel(tile, half, list_ref, placed_hbm, pow_ref, rows_ref, cols_ref, corners_ref, core_ref, placed_ref, psem, num):
@@ -705,10 +737,10 @@
     rows, cols = lax.axis_size("row"), lax.axis_size("col")
     held = amplitudes.shape[0]
     most = 4 * (held - 1)
-    side, tile = probe.shape[-1], object_field.shape[1]
-    ext, meta = pre_call(owner, offsets, object_field, side, rows, cols)
+    tile = object_field.shape[1]
+    ext, meta, early = pre_call(owner, offsets, object_field, amplitudes, rows, cols)
     patch, items = cut_call(meta, ext, tile, cols, held, most)
-    placed, grad, power = main_call(items, owner, amplitudes, patch, probe, rows, cols)
+    placed, grad, power = main_call(items, owner, amplitudes, early, patch, probe, rows, cols)
     *rims, core = place_call(items, placed, power, tile)
     scale = 1.0 / math.sqrt(rows * cols * held)
     object_out, gradient = post_call(rims, core, object_field, grad, rows, cols, scale)

time: 140 us -> 146 us (1.043)
  Pallas kernels: 134 us -> 139 us
  local copies, waits for them, and re-layouts: 4.56 us -> 6.47 us
    pallas_call x1, Pallas kernels: 21.2 us -> 28.4 us  [pre_call(): pl.pallas_call(functools.partial(pre_kernel, rows, cols, tile, half), out...]
    pallas_call x1, Pallas kernels: 48.1 us -> 44.4 us  [main_call(): pl.pallas_call(functools.partial(main_kernel, rows, cols), out_shape=[jax...]
    unnamed x15 -> x19, local copies, waits for them, and re-layouts: 4.56 us -> 6.47 us
where the time goes in v7:
time: 146 us
  Pallas kernels  139 us (95%)
  local copies, waits for them, and re-layouts  6.47 us (4%)
    pallas_call x1, Pallas kernels, post_call(): pl.pallas_call(functools.partial(post_kernel, rows, cols, tile, half, sca...  51.6 us
    pallas_call x1, Pallas kernels, main_call(): pl.pallas_call(functools.partial(main_kernel, rows, cols), out_shape=[jax...  44.4 us
    pallas_call x1, Pallas kernels, pre_call(): pl.pallas_call(functools.partial(pre_kernel, rows, cols, tile, half), out...  28.4 us
    unnamed x19, local copies, waits for them, and re-layouts  6.47 us
    pallas_call x1, Pallas kernels, cut_call(): pl.pallas_call(functools.partial(cut_kernel, cols, side // 2, held), out_...  6.42 us
    pallas_call x1, Pallas kernels, place_call(): pl.pallas_call(functools.partial(place_kernel, tile, half), out_shape=[ja...  6.06 us

profile of v7, /device:TPU:1, one launch (start us, length us, event | category | flops | bytes accessed | tf_op | source)
XLA Modules:
  0.0 146.1 jit_solution(108555833698549053)
XLA Ops:
  0.6 0.8 copy.9.offsets_ref
  1.4 0.0 copy-start
  1.4 1.6 %copy-done = f32[2,512,512]{2,1,0:T(8,128)S(1)} copy-done((f32[2,512,512]{2,1,0:T(8,128)S(1)}, f32[2,512,512]{2,1,0:T(8,128)}, u32[]{:S(2)}) %copy-start) | copy-done | bytes 2097176
  3.0 0.0 copy-start.2
  3.0 1.0 copy-done.2
  4.0 0.0 copy-start.8
  4.0 0.7 copy-done.8
  4.7 28.4 %pre.1 = (f32[2,768,768]{2,1,0:T(8,128)S(1)}, s32[16,1,128]{2,1,0:T(1,128)S(1)}, bf16[6,256,256]{2,1,0:T(8,128)(2,1)S(1)}) custom-call(s32[4]{0:T(128)S(1)} %copy-done.8, s32[4,2]{1,0:T(4,128)S(1)} %copy.9.offsets_ref, f32[2,512,512]{2,1,0:T(8,128)S(1)} %copy-done, bf16[4,256,256]{2,1,0:T(8,128)(2,1)S(1)} %copy-done.2), custom_call_target="tpu_custom_call" | custom-call | tf_op jit(solution)/shard_map/pre/pallas_call | solution.py:362
  33.1 0.0 copy-start.4
  33.1 0.9 copy-done.4
  34.0 6.4 %cut.1 = (f32[12,2,256,256]{3,2,1,0:T(8,128)}, s32[12,8]{1,0:T(8,128)S(1)}) custom-call(s32[16,1,128]{2,1,0:T(1,128)S(1)} %get-tuple-element.18.meta_ref, f32[2,768,768]{2,1,0:T(8,128)S(1)} %get-tuple-element.19.ext), custom_call_target="tpu_custom_call" | custom-call | tf_op jit(solution)/shard_map/cut/pallas_call | solution.py:453
  40.4 0.0 copy-start.6
  40.4 0.6 copy-done.6
  41.0 0.0 copy-start.7
  41.0 44.4 %main.1 = (f32[12,2,256,256]{3,2,1,0:T(8,128)}, f32[2048,256]{1,0:T(8,128)}, f32[256,256]{1,0:T(8,128)}) custom-call(s32[12,8]{1,0:T(8,128)} %copy-done.6, s32[4]{0:T(128)} %owner_ref.3, bf16[4,256,256]{2,1,0:T(8,128)(2,1)} %amp_hbm.3, bf16[6,256,256]{2,1,0:T(8,128)(2,1)} %copy-done.4, f32[12,2,256,256]{3,2,1,0:T(8,128)} %get-tuple-element.22.patch_hbm, ...), custom_call_target="tpu_custom_call" | custom-call | tf_op jit(solution)/shard_map/main/pallas_call | solution.py:605
  85.4 0.0 copy-done.7
  85.4 0.0 copy-start.5
  85.4 0.9 copy-done.5
  86.4 0.0 copy-start.1
  86.4 0.0 copy-start.3
  86.4 6.1 %place.1 = (bf16[2,3,128,512]{3,2,1,0:T(8,128)(2,1)S(1)}, bf16[2,3,512,128]{3,2,1,0:T(8,128)(2,1)S(1)}, bf16[4,3,128,128]{3,2,1,0:T(8,128)(2,1)S(1)}, f32[3,512,512]{2,1,0:T(8,128)S(1)}) custom-call(s32[12,8]{1,0:T(8,128)S(1)} %copy-done.7, f32[12,2,256,256]{3,2,1,0:T(8,128)} %get-tuple-element.23.placed_hbm, f32[256,256]{1,0:T(8,128)S(1)} %copy-done.5), custom_call_target="tpu_custom_call" | custom-call | tf_op jit(solution)/shard_map/place/pallas_call | solution.py:685
  92.5 0.0 copy-done.1
  92.5 0.0 copy-done.3
  92.5 51.6 %post.1 = (f32[2,512,512]{2,1,0:T(8,128)S(1)}, bf16[2,2,1024,128]{3,2,1,0:T(8,128)(2,1)S(1)}) custom-call(bf16[2,3,128,512]{3,2,1,0:T(8,128)(2,1)S(1)} %get-tuple-element.25.rows_ref, bf16[2,3,512,128]{3,2,1,0:T(8,128)(2,1)S(1)} %get-tuple-element.26.cols_ref, bf16[4,3,128,128]{3,2,1,0:T(8,128)(2,1)S(1)} %get-tuple-element.27.corners_ref, ...), custom_call_target="tpu_custom_call" | custom-call | tf_op jit(solution)/shard_map/post/pallas_call | solution.py:238
  144.0 2.0 %finish.1 = (f32[2,512,512]{2,1,0:T(8,128)}, f32[2048,256]{1,0:T(8,128)}) custom-call(f32[2,512,512]{2,1,0:T(8,128)S(1)} %get-tuple-element.30.obj_ref, bf16[2,2,1024,128]{3,2,1,0:T(8,128)(2,1)S(1)} %get-tuple-element.31.got_ref), custom_call_target="tpu_custom_call" | custom-call | tf_op jit(solution)/shard_map/finish/pallas_call | solution.py:725
Async XLA Ops:
  1.4 1.6 %copy-start = (f32[2,512,512]{2,1,0:T(8,128)S(1)}, f32[2,512,512]{2,1,0:T(8,128)}, u32[]{:S(2)}) copy-start(f32[2,512,512]{2,1,0:T(8,128)} %obj_ref.3) | copy-start | bytes 6291460
  3.0 1.0 copy-start.2
  4.0 0.7 copy-start.8
  33.1 0.9 copy-start.4
  40.4 0.6 copy-start.6
  41.0 44.4 %copy-start.7 = (s32[12,8]{1,0:T(8,128)S(1)}, s32[12,8]{1,0:T(8,128)}, u32[]{:S(2)}) copy-start(s32[12,8]{1,0:T(8,128)} %copy-done.6) | copy-start | bytes 1156
  85.4 1.0 copy-start.5
  86.4 6.1 %copy-start.1 = (f32[2,512,512]{2,1,0:T(8,128)S(1)}, f32[2,512,512]{2,1,0:T(8,128)}, u32[]{:S(2)}) copy-start(f32[2,512,512]{2,1,0:T(8,128)} %obj_ref.3) | copy-start | bytes 6291460
  86.4 6.1 %copy-start.3 = (f32[2048,256]{1,0:T(8,128)S(1)}, f32[2048,256]{1,0:T(8,128)}, u32[]{:S(2)}) copy-start(f32[2048,256]{1,0:T(8,128)} %get-tuple-element.29.grad_ref) | copy-start | bytes 6291460

commit v8 on v6

--- a/solution.py
+++ b/solution.py
@@ -69,6 +69,33 @@
     return [(row, lax.rem(x + dx, cols // depth) * depth + lax.rem(z + dz, depth)) for dx, dz in steps]
 
 
+LEAD = 16
+
+
+def power_of(x):
+    top = jnp.max(jnp.abs(x), axis=0, keepdims=True)
+    return jnp.floor(jnp.log2(jnp.maximum(top, 1e-30)))
+
+
+def code(out, x, power=None):
+    power = power_of(x) if power is None else power
+    out[:LEAD] = jnp.broadcast_to(power, (LEAD, x.shape[1])).astype(jnp.int32).astype(jnp.int16)
+    x = jnp.clip(jnp.round(x * jnp.exp2(14.0 - power)), -32767.0, 32767.0)
+    out[LEAD:] = x.astype(jnp.int32).astype(jnp.int16)
+
+
+def decoded(ref):
+    power = ref[:LEAD].astype(jnp.int32).astype(F32)[:1]
+    return ref[LEAD:].astype(jnp.int32).astype(F32) * jnp.exp2(power - 14.0)
+
+
+def code_pieces(out, ref):
+    power = power_of(ref[...])
+    size = ref.shape[0] // out.shape[0]
+    for k in range(out.shape[0]):
+        code(out.at[k], ref[k * size:(k + 1) * size], power)
+
+
 class Sends:
     def __init__(self, send_sem, recv_sem):
         self.send_sem, self.recv_sem, self.at, self.all = send_sem, recv_sem, 0, []
@@ -96,7 +123,8 @@
 
 
 def post_kernel(rows, cols, tile, half, scale, rows_ref, cols_ref, corners_ref, core_ref, obj_ref, grad_ref, out_ref, all16,
-                wsum, rim_rows, rim_cols, rim_corners, mate, sum_a, sum_b, got_a, got_b, part_a, part_b, got_a2, got_b2, gsend, grecv):
+                wsum, rim_rows, rim_cols, rim_corners, mate, sum_a, sum_b, got_a, got_b, part_a, part_b, got_a2, got_b2,
+                code_a, code_b, gsend, grecv):
     row, col = lax.axis_index("row"), lax.axis_index("col")
     core, y = lax.rem(row, 2), row // 2
     ys = rows // 2
@@ -129,34 +157,35 @@
         for i in which:
             rim_copies.append(send(place(i, rows_ref, cols_ref, corners_ref), landed(i), near[i]))
 
-    send_rims([1, 6])
+    send_rims([1, 6, 3, 4])
     pair.wait_recv()
-    h = grad_ref[mine, :] + mate[...]
-    sum_a[...] = h[:, :128]
-    sum_b[...] = h[:, 128:]
+    sum_a[...] = grad_ref[mine, :128] + mate[:, :128]
+    sum_b[...] = grad_ref[mine, 128:] + mate[:, 128:]
+    code_pieces(code_a, sum_a)
+    code_pieces(code_b, sum_b)
     y_at = [lax.rem(y + s, ys) for s in range(1, ys)]
     c_at = [peer[1] for peer in c_peers]
 
     def piece(k, size):
         return pl.ds(pl.multiple_of(k * size, size), size)
 
-    a1 = [send(sum_a.at[piece(y_at[s], na)], got_a.at[s], y_peers[s]) for s in range(ys - 1)]
-    b1 = [send(sum_b.at[piece(c_at[s], nb)], got_b.at[s], c_peers[s]) for s in range(cols - 1)]
+    a1 = [send(code_a.at[y_at[s]], got_a.at[s], y_peers[s]) for s in range(ys - 1)]
+    b1 = [send(code_b.at[c_at[s]], got_b.at[s], c_peers[s]) for s in range(cols - 1)]
     for c in a1:
         c.wait_recv()
     tot = sum_a[piece(y, na), :]
     for s in range(ys - 1):
-        tot += got_a[s]
+        tot += decoded(got_a.at[s])
     part_a[...] = tot
     a2 = [send(part_a.at[piece(c_at[s], fin)], got_a2.at[s], c_peers[s]) for s in range(cols - 1)]
     for c in b1:
         c.wait_recv()
     tot = sum_b[piece(col, nb), :]
     for s in range(cols - 1):
-        tot += got_b[s]
+        tot += decoded(got_b.at[s])
     part_b[...] = tot
     b2 = [send(part_b.at[piece(y_at[s], fin)], got_b2.at[s], y_peers[s]) for s in range(ys - 1)]
-    send_rims([3, 4])
+    send_rims([0, 2, 5, 7])
     for c in a2:
         c.wait_recv()
     tot = part_a[piece(col, fin), :]
@@ -173,7 +202,6 @@
     at_b = piece(col * ys + y, fin)
     all16[core, 1, at_b, :] = (tot * scale).astype(all16.dtype)
     b3 = [send(all16.at[core, 1, at_b], all16.at[core, 1, at_b], p) for p in y_peers]
-    send_rims([0, 2, 5, 7])
     for c in a3:
         c.wait_recv()
     big_a = piece(y, na)
@@ -182,6 +210,9 @@
         c.wait_recv()
     big_b = piece(col, nb)
     b4 = [send(all16.at[core, 1, big_b], all16.at[core, 1, big_b], p) for p in c_peers]
+    for c in a4 + b4:
+        c.wait_recv()
+    last = send(all16.at[core], all16.at[core], other)
     for c in rim_copies:
         c.wait_recv()
     out_ref[...] = core_ref[0:2]
@@ -203,9 +234,6 @@
 
     for q in range(2):
         out_ref[q] = obj_ref[q] + out_ref[q] / (wsum[...] + 1.0)
-    for c in a4 + b4:
-        c.wait_recv()
-    last = send(all16.at[core], all16.at[core], other)
     last.wait_recv()
     send.finish()
 
@@ -230,12 +258,14 @@
             pltpu.VMEM((n, 256), F32),
             pltpu.VMEM((n, 128), F32),
             pltpu.VMEM((n, 128), F32),
-            pltpu.VMEM((ys - 1, na, 128), F32),
-            pltpu.VMEM((cols - 1, nb, 128), F32),
+            pltpu.VMEM((ys - 1, LEAD + na, 128), jnp.int16),
+            pltpu.VMEM((cols - 1, LEAD + nb, 128), jnp.int16),
             pltpu.VMEM((na, 128), F32),
             pltpu.VMEM((nb, 128), F32),
             pltpu.VMEM((cols - 1, fin, 128), F32),
             pltpu.VMEM((ys - 1, fin, 128), F32),
+            pltpu.VMEM((ys, LEAD + na, 128), jnp.int16),
+            pltpu.VMEM((cols, LEAD + nb, 128), jnp.int16),
             pltpu.SemaphoreType.DMA((copies,)),
             pltpu.SemaphoreType.DMA((copies,)),
         ],
@@ -260,15 +290,7 @@
             note = jnp.where(lane == held + 2 * h + k, offsets_ref[h, k], note)
     mine[...] = note
     core.wait()
-    lead, end = 16, half + tile
-
-    def code(out, x):
-        top = jnp.max(jnp.abs(x), axis=0, keepdims=True)
-        power = jnp.floor(jnp.log2(jnp.maximum(top, 1e-30)))
-        out[:lead] = jnp.broadcast_to(power, (lead, x.shape[1])).astype(jnp.int32).astype(jnp.int16)
-        x = jnp.clip(jnp.round(x * jnp.exp2(14.0 - power)), -32767.0, 32767.0)
-        out[lead:] = x.astype(jnp.int32).astype(jnp.int16)
-
+    end = half + tile
     for q in range(2):
         for k, at in enumerate((half, end - half)):
             code(out_rows.at[k, q], ext_ref[q, at:at + half, half:end])
@@ -306,8 +328,7 @@
         tc, cl = span(-dc, tile, half)
         ref = landed(dr, dc)
         for q in range(2):
-            power = ref[q, :lead].astype(jnp.int32).astype(F32)[:1]
-            ext_ref[q, tr:tr + rl, tc:tc + cl] = ref[q, lead:].astype(jnp.int32).astype(F32) * jnp.exp2(power - 14.0)
+            ext_ref[q, tr:tr + rl, tc:tc + cl] = decoded(ref.at[q])
     send.finish()
     big = tile + 2 * half
 
@@ -341,11 +362,11 @@
         out_specs=[V, V],
         scratch_shapes=[
             pltpu.VMEM((1, 128), jnp.int32),
-            pltpu.VMEM((2, 2, half + 16, tile), jnp.int16),
-            pltpu.VMEM((2, 2, tile + 16, half), jnp.int16),
-            pltpu.VMEM((2, 2, half + 16, tile), jnp.int16),
-            pltpu.VMEM((2, 2, tile + 16, half), jnp.int16),
-            pltpu.VMEM((4, 2, half + 16, half), jnp.int16),
+            pltpu.VMEM((2, 2, half + LEAD, tile), jnp.int16),
+            pltpu.VMEM((2, 2, tile + LEAD, half), jnp.int16),
+            pltpu.VMEM((2, 2, half + LEAD, tile), jnp.int16),
+            pltpu.VMEM((2, 2, tile + LEAD, half), jnp.int16),
+            pltpu.VMEM((4, 2, half + LEAD, half), jnp.int16),
             pltpu.SemaphoreType.DMA((copies,)),
             pltpu.SemaphoreType.DMA((copies,)),
             pltpu.SemaphoreType.DMA((2,)),
@@ -500,7 +521,7 @@
                 one = out[m * chunk:(m + 1) * chunk]
                 far[p, m, rows_c] = one
                 tot += one[:, :side] * one[:, :side] + one[:, side:] * one[:, side:]
-            total[p, rows_c] = tot
+            total[p, rows_c] = lax.rsqrt(jnp.maximum(tot, 0.25))
 
     def there_two(k, carry):
         for u in range(2):
@@ -522,7 +543,7 @@
 
     def back(p, carry):
         fields, halves = ebuf.at[0], hbuf.at[0]
-        ratio[...] = amps[list_ref[p, 1]].astype(F32) * lax.rsqrt(jnp.maximum(total[p], 0.25))
+        ratio[...] = amps[list_ref[p, 1]].astype(F32) * total[p]
         for m in range(modes):
             fields[m, :side] = (far[p, m, :, :side] * ratio[...]).astype(BF16)
             fields[m, side:] = (far[p, m, :, side:] * ratio[...]).astype(BF16)

time: 140 us -> 135 us (0.964)
  Pallas kernels: 134 us -> 129 us
    pallas_call x1, Pallas kernels: 50.2 us -> 48.3 us  [post_call(): pl.pallas_call(functools.partial(post_kernel, rows, cols, tile, half, sca...]
    pallas_call x1, Pallas kernels: 6.05 us -> 4.27 us  [place_call(): pl.pallas_call(functools.partial(place_kernel, tile, half), out_shape=[ja...]
where the time goes in v8:
time: 135 us; the launch traced here: 134 us
  Pallas kernels  129 us (96%)
  local copies, waits for them, and re-layouts  4.56 us (3%)
    pallas_call x1, Pallas kernels, post_call(): pl.pallas_call(functools.partial(post_kernel, rows, cols, tile, half, sca...  48.3 us
    pallas_call x1, Pallas kernels, main_call(): pl.pallas_call(functools.partial(main_kernel, rows, cols), out_shape=[jax...  48.2 us
    pallas_call x1, Pallas kernels, pre_call(): pl.pallas_call(functools.partial(pre_kernel, rows, cols, tile, half), out...  21.2 us
    pallas_call x1, Pallas kernels, cut_call(): pl.pallas_call(functools.partial(cut_kernel, cols, side // 2, held), out_...  5.15 us
    unnamed x15, local copies, waits for them, and re-layouts  4.56 us
    pallas_call x1, Pallas kernels, place_call(): pl.pallas_call(functools.partial(place_kernel, tile, half), out_shape=[ja...  4.27 us

profile of v8, /device:TPU:1, one launch (start us, length us, event | category | flops | bytes accessed | tf_op | source)
XLA Modules:
  0.0 134.4 jit_solution(8639800184895768791)
XLA Ops:
  0.6 0.8 copy.9.offsets_ref
  1.4 0.0 copy-start
  1.4 1.6 %copy-done = f32[2,512,512]{2,1,0:T(8,128)S(1)} copy-done((f32[2,512,512]{2,1,0:T(8,128)S(1)}, f32[2,512,512]{2,1,0:T(8,128)}, u32[]{:S(2)}) %copy-start) | copy-done | bytes 2097176
  3.0 0.0 copy-start.6
  3.0 0.7 copy-done.6
  3.6 21.2 %pre.1 = (f32[2,768,768]{2,1,0:T(8,128)S(1)}, s32[16,1,128]{2,1,0:T(1,128)S(1)}) custom-call(s32[4]{0:T(128)S(1)} %copy-done.6, s32[4,2]{1,0:T(4,128)S(1)} %copy.9.offsets_ref, f32[2,512,512]{2,1,0:T(8,128)S(1)} %copy-done), custom_call_target="tpu_custom_call" | custom-call | tf_op jit(solution)/shard_map/pre/pallas_call | solution.py:358
  24.8 5.2 %cut.1 = (f32[12,2,256,256]{3,2,1,0:T(8,128)}, s32[12,8]{1,0:T(8,128)S(1)}) custom-call(s32[16,1,128]{2,1,0:T(1,128)S(1)} %get-tuple-element.17.meta_ref, f32[2,768,768]{2,1,0:T(8,128)S(1)} %get-tuple-element.18.ext), custom_call_target="tpu_custom_call" | custom-call | tf_op jit(solution)/shard_map/cut/pallas_call | solution.py:444
  30.0 0.0 copy-start.4
  30.0 0.6 copy-done.4
  30.6 0.0 copy-start.5
  30.6 48.2 %main.1 = (f32[12,2,256,256]{3,2,1,0:T(8,128)}, f32[2048,256]{1,0:T(8,128)}, f32[256,256]{1,0:T(8,128)}) custom-call(s32[12,8]{1,0:T(8,128)} %copy-done.4, s32[4]{0:T(128)} %owner_ref.3, bf16[4,256,256]{2,1,0:T(8,128)(2,1)} %amp_hbm.1, f32[12,2,256,256]{3,2,1,0:T(8,128)} %get-tuple-element.20.patch_hbm, f32[4,2,256,256]{3,2,1,0:T(8,128)} %probe_hbm.1, ...), custom_call_target="tpu_custom_call" | custom-call | tf_op jit(solution)/shard_map/main/pallas_call | solution.py:594
  78.8 0.0 copy-done.5
  78.8 0.0 copy-start.3
  78.8 0.9 copy-done.3
  79.8 0.0 copy-start.1
  79.8 0.0 copy-start.2
  79.8 4.3 %place.1 = (bf16[2,3,128,512]{3,2,1,0:T(8,128)(2,1)S(1)}, bf16[2,3,512,128]{3,2,1,0:T(8,128)(2,1)S(1)}, bf16[4,3,128,128]{3,2,1,0:T(8,128)(2,1)S(1)}, f32[3,512,512]{2,1,0:T(8,128)S(1)}) custom-call(s32[12,8]{1,0:T(8,128)S(1)} %copy-done.5, f32[12,2,256,256]{3,2,1,0:T(8,128)} %get-tuple-element.21.placed_hbm, f32[256,256]{1,0:T(8,128)S(1)} %copy-done.3), custom_call_target="tpu_custom_call" | custom-call | tf_op jit(solution)/shard_map/place/pallas_call | solution.py:674
  84.0 0.0 copy-done.1
  84.1 0.0 copy-done.2
  84.1 48.3 %post.1 = (f32[2,512,512]{2,1,0:T(8,128)S(1)}, bf16[2,2,1024,128]{3,2,1,0:T(8,128)(2,1)S(1)}) custom-call(bf16[2,3,128,512]{3,2,1,0:T(8,128)(2,1)S(1)} %get-tuple-element.23.rows_ref, bf16[2,3,512,128]{3,2,1,0:T(8,128)(2,1)S(1)} %get-tuple-element.24.cols_ref, bf16[4,3,128,128]{3,2,1,0:T(8,128)(2,1)S(1)} %get-tuple-element.25.corners_ref, ...), custom_call_target="tpu_custom_call" | custom-call | tf_op jit(solution)/shard_map/post/pallas_call | solution.py:248
  132.4 2.0 %finish.1 = (f32[2,512,512]{2,1,0:T(8,128)}, f32[2048,256]{1,0:T(8,128)}) custom-call(f32[2,512,512]{2,1,0:T(8,128)S(1)} %get-tuple-element.28.obj_ref, bf16[2,2,1024,128]{3,2,1,0:T(8,128)(2,1)S(1)} %get-tuple-element.29.got_ref), custom_call_target="tpu_custom_call" | custom-call | tf_op jit(solution)/shard_map/finish/pallas_call | solution.py:714
Async XLA Ops:
  1.4 1.6 %copy-start = (f32[2,512,512]{2,1,0:T(8,128)S(1)}, f32[2,512,512]{2,1,0:T(8,128)}, u32[]{:S(2)}) copy-start(f32[2,512,512]{2,1,0:T(8,128)} %obj_ref.3) | copy-start | bytes 6291460
  3.0 0.7 copy-start.6
  30.0 0.6 copy-start.4
  30.6 48.2 %copy-start.5 = (s32[12,8]{1,0:T(8,128)S(1)}, s32[12,8]{1,0:T(8,128)}, u32[]{:S(2)}) copy-start(s32[12,8]{1,0:T(8,128)} %copy-done.4) | copy-start | bytes 1156
  78.8 1.0 copy-start.3
  79.8 4.3 %copy-start.1 = (f32[2,512,512]{2,1,0:T(8,128)S(1)}, f32[2,512,512]{2,1,0:T(8,128)}, u32[]{:S(2)}) copy-start(f32[2,512,512]{2,1,0:T(8,128)} %obj_ref.3) | copy-start | bytes 6291460
  79.8 4.3 %copy-start.2 = (f32[2048,256]{1,0:T(8,128)S(1)}, f32[2048,256]{1,0:T(8,128)}, u32[]{:S(2)}) copy-start(f32[2048,256]{1,0:T(8,128)} %get-tuple-element.27.grad_ref) | copy-start | bytes 6291460

commit v9 on v8

--- a/solution.py
+++ b/solution.py
@@ -64,7 +64,7 @@
 
 def column_peers(row, col, cols):
     depth = 4
-    steps = [(0, 1), (1, 0), (0, 3), (3, 0), (1, 1), (3, 3), (1, 3), (3, 1), (2, 0), (0, 2), (2, 2), (1, 2), (3, 2), (2, 1), (2, 3)]
+    steps = [(2, 1), (1, 2), (2, 3), (3, 2), (2, 2), (1, 1), (3, 3), (1, 3), (3, 1), (2, 0), (0, 2), (0, 1), (1, 0), (0, 3), (3, 0)]
     x, z = col // depth, lax.rem(col, depth)
     return [(row, lax.rem(x + dx, cols // depth) * depth + lax.rem(z + dz, depth)) for dx, dz in steps]
 
@@ -94,6 +94,13 @@
     size = ref.shape[0] // out.shape[0]
     for k in range(out.shape[0]):
         code(out.at[k], ref[k * size:(k + 1) * size], power)
+
+
+def owned_by(to, owner_ref, held):
+    which = jnp.int32(0)
+    for h in range(1, held):
+        which = jnp.where(owner_ref[h] == to, h, which)
+    return which
 
 
 class Sends:
@@ -139,7 +146,7 @@
     fin = n // (ys * cols)
     theirs = pl.ds(pl.multiple_of((1 - core) * n, n), n)
     mine = pl.ds(pl.multiple_of(core * n, n), n)
-    pair = send(grad_ref.at[theirs], mate, other)
+    pair = [send(grad_ref.at[theirs, k:k + 128], mate.at[:, k:k + 128], other) for k in (0, 128)]
     rim_copies = []
 
     def place(i, by_rows, by_cols, at_corners):
@@ -158,18 +165,18 @@
             rim_copies.append(send(place(i, rows_ref, cols_ref, corners_ref), landed(i), near[i]))
 
     send_rims([1, 6, 3, 4])
-    pair.wait_recv()
-    sum_a[...] = grad_ref[mine, :128] + mate[:, :128]
-    sum_b[...] = grad_ref[mine, 128:] + mate[:, 128:]
-    code_pieces(code_a, sum_a)
-    code_pieces(code_b, sum_b)
     y_at = [lax.rem(y + s, ys) for s in range(1, ys)]
     c_at = [peer[1] for peer in c_peers]
-
+    pair[0].wait_recv()
+    sum_a[...] = grad_ref[mine, :128] + mate[:, :128]
+    code_pieces(code_a, sum_a)
     def piece(k, size):
         return pl.ds(pl.multiple_of(k * size, size), size)
 
     a1 = [send(code_a.at[y_at[s]], got_a.at[s], y_peers[s]) for s in range(ys - 1)]
+    pair[1].wait_recv()
+    sum_b[...] = grad_ref[mine, 128:] + mate[:, 128:]
+    code_pieces(code_b, sum_b)
     b1 = [send(code_b.at[c_at[s]], got_b.at[s], c_peers[s]) for s in range(cols - 1)]
     for c in a1:
         c.wait_recv()
@@ -210,9 +217,11 @@
         c.wait_recv()
     big_b = piece(col, nb)
     b4 = [send(all16.at[core, 1, big_b], all16.at[core, 1, big_b], p) for p in c_peers]
-    for c in a4 + b4:
-        c.wait_recv()
-    last = send(all16.at[core], all16.at[core], other)
+    last = []
+    for k, copies in enumerate((a4, b4)):
+        for c in copies:
+            c.wait_recv()
+        last.append(send(all16.at[core, k], all16.at[core, k], other))
     for c in rim_copies:
         c.wait_recv()
     out_ref[...] = core_ref[0:2]
@@ -234,7 +243,8 @@
 
     for q in range(2):
         out_ref[q] = obj_ref[q] + out_ref[q] / (wsum[...] + 1.0)
-    last.wait_recv()
+    for c in last:
+        c.wait_recv()
     send.finish()
 
 
@@ -243,7 +253,7 @@
     total = grad.shape[0]
     ys, n = rows // 2, total // 2
     na, nb, fin = n // ys, n // cols, n // (ys * cols)
-    copies = 1 + 8 + 2 * (ys - 1) + 2 * (cols - 1) + 2 * (ys - 1) + 2 * (cols - 1) + 1
+    copies = 2 + 8 + 4 * (ys - 1) + 4 * (cols - 1) + 2
     V = pl.BlockSpec(memory_space=pltpu.VMEM)
     return pl.pallas_call(
         functools.partial(post_kernel, rows, cols, tile, half, scale),
@@ -287,7 +297,7 @@
     for h in range(held):
         note = jnp.where(lane == h, owner_ref[h], note)
         for k in range(2):
-            note = jnp.where(lane == held + 2 * h + k, offsets_ref[h, k], note)
+            note = jnp.where(lane == held + 2 * h + k, offsets_ref[k, h], note)
     mine[...] = note
     core.wait()
     end = half + tile
@@ -456,8 +466,8 @@
 
 
 def main_kernel(rows, cols, list_ref, owner_ref, amp_hbm, patch_hbm, probe_hbm, tab_hbm,
-                placed_hbm, grad_ref, pow_ref,
-                placed_ref, psem, slots, amps, amp, probe, tab, patch, far, total, ratio, ebuf, hbuf, ssum,
+                placed_hbm, grad_ref,
+                placed_ref, pow_ref, psem, slots, amps, amp, probe, tab, patch, far, total, ratio, ebuf, hbuf, ssum,
                 gsend, grecv, lsem):
     row, col = lax.axis_index("row"), lax.axis_index("col")
     c_peers = column_peers(row, col, cols)
@@ -474,21 +484,20 @@
     send = Sends(gsend, grecv)
     local[0].wait()
     amp_copies = []
-    for s in range(cols):
-        to = col if s == 0 else c_peers[s - 1][1]
-        which = jnp.int32(0)
-        for h in range(1, held):
-            which = jnp.where(owner_ref[h] == to, h, which)
-        if s == 0:
-            amps[col] = amp[which]
-        else:
-            slots[s] = amp[which]
-            amp_copies.append(send(slots.at[s], amps.at[col], c_peers[s - 1]))
+    for h in range(2):
+        part = pl.ds(h * (side // 2), side // 2)
+        for k, peer in enumerate(c_peers):
+            if h == 0:
+                slots[k] = amp[owned_by(peer[1], owner_ref, held)]
+            amp_copies.append(send(slots.at[k, part], amps.at[col, part], peer))
+    amps[col] = amp[owned_by(col, owner_ref, held)]
     local[1].wait()
     power = jnp.zeros((side, side), F32)
     for m in range(modes):
         power += probe[m, 0] * probe[m, 0] + probe[m, 1] * probe[m, 1]
     pow_ref[...] = power
+    weight = pltpu.make_async_copy(pow_ref, placed_hbm.at[most, 0], psem.at[most])
+    weight.start()
     grad_ref[...] = jnp.zeros_like(grad_ref)
     ssum[...] = jnp.zeros_like(ssum)
     local[2].wait()
@@ -573,12 +582,13 @@
         for q in range(2):
             grad_ref[(2 * m + q) * side:(2 * m + q + 1) * side] -= probe[m, q] * ssum[...]
     lax.fori_loop(0, most, drain, 0)
+    weight.wait()
     send.finish()
 
 
 def main_call(items, owner, amp, patch, probe, rows, cols):
     side, modes, most = amp.shape[1], probe.shape[0], patch.shape[0]
-    copies = cols - 1
+    copies = 2 * (cols - 1)
     tr, ti = tables(side)
 
     def left(a, b):
@@ -594,16 +604,16 @@
     return pl.pallas_call(
         functools.partial(main_kernel, rows, cols),
         out_shape=[
-            jax.ShapeDtypeStruct((most, 2, side, side), F32),
+            jax.ShapeDtypeStruct((most + 1, 2, side, side), F32),
             jax.ShapeDtypeStruct((modes * 2 * side, side), F32),
-            jax.ShapeDtypeStruct((side, side), F32),
         ],
         in_specs=[S, S, A, A, A, A],
-        out_specs=[A, V, V],
+        out_specs=[A, V],
         scratch_shapes=[
             pltpu.VMEM((most, 2, side, side), F32),
-            pltpu.SemaphoreType.DMA((most,)),
-            pltpu.VMEM((cols, side, side), BF16),
+            pltpu.VMEM((side, side), F32),
+            pltpu.SemaphoreType.DMA((most + 1,)),
+            pltpu.VMEM((cols - 1, side, side), BF16),
             pltpu.VMEM((cols, side, side), BF16),
             pltpu.VMEM(amp.shape, BF16),
             pltpu.VMEM(probe.shape, F32),
@@ -624,7 +634,7 @@
     )(items, owner, amp, patch, probe, tab)
 
 
-def place_kernel(tile, half, list_ref, placed_hbm, pow_ref, rows_ref, cols_ref, corners_ref, core_ref, placed_ref, psem, num):
+def place_kernel(tile, half, list_ref, placed_hbm, rows_ref, cols_ref, corners_ref, core_ref, placed_ref, pow_ref, psem, num):
     side = 2 * half
     big, tall, wide = tile + side, side + 8, side + 128
 
@@ -635,8 +645,12 @@
         fetch(p).start()
         return carry
 
-    lax.fori_loop(0, list_ref.shape[0], start, 0)
+    most = list_ref.shape[0]
+    weight = pltpu.make_async_copy(placed_hbm.at[most, 0], pow_ref, psem.at[most])
+    weight.start()
+    lax.fori_loop(0, most, start, 0)
     num[...] = jnp.zeros_like(num)
+    weight.wait()
 
     def visit(p, carry):
         fetch(p).wait()
@@ -665,8 +679,8 @@
         core_ref[q] = num[q, half:big - half, half:big - half]
 
 
-def place_call(items, placed, power, tile):
-    side = power.shape[0]
+def place_call(items, placed, tile):
+    most, side = items.shape[0], placed.shape[-1]
     half = side // 2
     big = tile + side
     V = pl.BlockSpec(memory_space=pltpu.VMEM)
@@ -678,15 +692,16 @@
             jax.ShapeDtypeStruct((2, 3, tile, half), BF16),
             jax.ShapeDtypeStruct((4, 3, half, half), BF16),
             jax.ShapeDtypeStruct((3, tile, tile), F32)],
-        in_specs=[S, pl.BlockSpec(memory_space=pltpu.HBM), V],
+        in_specs=[S, pl.BlockSpec(memory_space=pltpu.HBM)],
         out_specs=[V, V, V, V],
         scratch_shapes=[
-            pltpu.VMEM(placed.shape, F32),
-            pltpu.SemaphoreType.DMA((placed.shape[0],)),
+            pltpu.VMEM((most, 2, side, side), F32),
+            pltpu.VMEM((side, side), F32),
+            pltpu.SemaphoreType.DMA((most + 1,)),
             pltpu.VMEM((3, big, big), F32)],
         compiler_params=pltpu.CompilerParams(vmem_limit_bytes=46 * 2**20),
         name="place",
-    )(items, placed, power)
+    )(items, placed)
 
 
 def finish_kernel(obj_ref, got_ref, out_hbm, grad_hbm, wide, sem):
@@ -727,10 +742,10 @@
     held = amplitudes.shape[0]
     most = 4 * (held - 1)
     side, tile = probe.shape[-1], object_field.shape[1]
-    ext, meta = pre_call(owner, offsets, object_field, side, rows, cols)
+    ext, meta = pre_call(owner, offsets.T, object_field, side, rows, cols)
     patch, items = cut_call(meta, ext, tile, cols, held, most)
-    placed, grad, power = main_call(items, owner, amplitudes, patch, probe, rows, cols)
-    *rims, core = place_call(items, placed, power, tile)
+    placed, grad = main_call(items, owner, amplitudes, patch, probe, rows, cols)
+    *rims, core = place_call(items, placed, tile)
     scale = 1.0 / math.sqrt(rows * cols * held)
     object_out, gradient = post_call(rims, core, object_field, grad, rows, cols, scale)
     object_out, gradient = finish_call(object_out, gradient)

time: 135 us -> 129 us (0.956)
  Pallas kernels: 129 us -> 125 us
    pallas_call x1, Pallas kernels: 48.3 us -> 44.4 us  [post_call(): pl.pallas_call(functools.partial(post_kernel, rows, cols, tile, half, sca...]
    unnamed x15 -> x14, local copies, waits for them, and re-layouts: 4.56 us -> 3.53 us
where the time goes in v9:
time: 129 us
  Pallas kernels  125 us (97%)
  local copies, waits for them, and re-layouts  3.53 us (3%)
    pallas_call x1, Pallas kernels, main_call(): pl.pallas_call(functools.partial(main_kernel, rows, cols), out_shape=[jax...  47.7 us
    pallas_call x1, Pallas kernels, post_call(): pl.pallas_call(functools.partial(post_kernel, rows, cols, tile, half, sca...  44.4 us
    pallas_call x1, Pallas kernels, pre_call(): pl.pallas_call(functools.partial(pre_kernel, rows, cols, tile, half), out...  21.2 us
    pallas_call x1, Pallas kernels, cut_call(): pl.pallas_call(functools.partial(cut_kernel, cols, side // 2, held), out_...  5.15 us
    pallas_call x1, Pallas kernels, place_call(): pl.pallas_call(functools.partial(place_kernel, tile, half), out_shape=[ja...  4.36 us
    unnamed x14, local copies, waits for them, and re-layouts  3.53 us

profile of v9, /device:TPU:1, one launch (start us, length us, event | category | flops | bytes accessed | tf_op | source)
XLA Modules:
  0.0 129.2 jit_solution(17668963023384080532)
XLA Ops:
  0.6 0.0 copy-start
  0.6 1.6 %copy-done = f32[2,512,512]{2,1,0:T(8,128)S(1)} copy-done((f32[2,512,512]{2,1,0:T(8,128)S(1)}, f32[2,512,512]{2,1,0:T(8,128)}, u32[]{:S(2)}) %copy-start) | copy-done | bytes 2097176
  2.2 0.0 copy-start.5
  2.2 0.7 copy-done.5
  2.9 0.0 copy-start.6
  2.9 0.7 copy-done.6
  3.6 21.2 %pre.1 = (f32[2,768,768]{2,1,0:T(8,128)S(1)}, s32[16,1,128]{2,1,0:T(1,128)S(1)}) custom-call(s32[4]{0:T(128)S(1)} %copy-done.5, s32[2,4]{1,0:T(2,128)S(1)} %bitcast.2, f32[2,512,512]{2,1,0:T(8,128)S(1)} %copy-done), custom_call_target="tpu_custom_call" | custom-call | tf_op jit(solution)/shard_map/pre/pallas_call | solution.py:368
  24.8 5.1 %cut.1 = (f32[12,2,256,256]{3,2,1,0:T(8,128)}, s32[12,8]{1,0:T(8,128)S(1)}) custom-call(s32[16,1,128]{2,1,0:T(1,128)S(1)} %get-tuple-element.16.meta_ref, f32[2,768,768]{2,1,0:T(8,128)S(1)} %get-tuple-element.17.ext), custom_call_target="tpu_custom_call" | custom-call | tf_op jit(solution)/shard_map/cut/pallas_call | solution.py:454
  29.9 0.0 copy-start.3
  29.9 0.6 copy-done.3
  30.5 0.0 copy-start.4
  30.5 47.7 %main.1 = (f32[13,2,256,256]{3,2,1,0:T(8,128)}, f32[2048,256]{1,0:T(8,128)}) custom-call(s32[12,8]{1,0:T(8,128)} %copy-done.3, s32[4]{0:T(128)} %owner_ref.3, bf16[4,256,256]{2,1,0:T(8,128)(2,1)} %amp_hbm.1, f32[12,2,256,256]{3,2,1,0:T(8,128)} %get-tuple-element.19.patch_hbm, f32[4,2,256,256]{3,2,1,0:T(8,128)} %probe_hbm.1, ...), custom_call_target="tpu_custom_call" | custom-call | tf_op jit(solution)/shard_map/main/pallas_call | solution.py:604
  78.2 0.0 copy-done.4
  78.3 0.0 copy-start.1
  78.3 0.0 copy-start.2
  78.3 4.4 %place.1 = (bf16[2,3,128,512]{3,2,1,0:T(8,128)(2,1)S(1)}, bf16[2,3,512,128]{3,2,1,0:T(8,128)(2,1)S(1)}, bf16[4,3,128,128]{3,2,1,0:T(8,128)(2,1)S(1)}, f32[3,512,512]{2,1,0:T(8,128)S(1)}) custom-call(s32[12,8]{1,0:T(8,128)S(1)} %copy-done.4, f32[13,2,256,256]{3,2,1,0:T(8,128)} %get-tuple-element.20.placed_hbm), custom_call_target="tpu_custom_call" | custom-call | tf_op jit(solution)/shard_map/place/pallas_call | solution.py:688
  82.6 0.0 copy-done.1
  82.7 0.0 copy-done.2
  82.7 44.4 %post.1 = (f32[2,512,512]{2,1,0:T(8,128)S(1)}, bf16[2,2,1024,128]{3,2,1,0:T(8,128)(2,1)S(1)}) custom-call(bf16[2,3,128,512]{3,2,1,0:T(8,128)(2,1)S(1)} %get-tuple-element.21.rows_ref, bf16[2,3,512,128]{3,2,1,0:T(8,128)(2,1)S(1)} %get-tuple-element.22.cols_ref, bf16[4,3,128,128]{3,2,1,0:T(8,128)(2,1)S(1)} %get-tuple-element.23.corners_ref, ...), custom_call_target="tpu_custom_call" | custom-call | tf_op jit(solution)/shard_map/post/pallas_call | solution.py:258
  127.1 2.0 %finish.1 = (f32[2,512,512]{2,1,0:T(8,128)}, f32[2048,256]{1,0:T(8,128)}) custom-call(f32[2,512,512]{2,1,0:T(8,128)S(1)} %get-tuple-element.26.obj_ref, bf16[2,2,1024,128]{3,2,1,0:T(8,128)(2,1)S(1)} %get-tuple-element.27.got_ref), custom_call_target="tpu_custom_call" | custom-call | tf_op jit(solution)/shard_map/finish/pallas_call | solution.py:729
Async XLA Ops:
  0.6 1.6 %copy-start = (f32[2,512,512]{2,1,0:T(8,128)S(1)}, f32[2,512,512]{2,1,0:T(8,128)}, u32[]{:S(2)}) copy-start(f32[2,512,512]{2,1,0:T(8,128)} %obj_ref.3) | copy-start | bytes 6291460
  2.2 0.7 copy-start.5
  2.9 0.7 copy-start.6
  29.9 0.6 copy-start.3
  30.5 47.7 %copy-start.4 = (s32[12,8]{1,0:T(8,128)S(1)}, s32[12,8]{1,0:T(8,128)}, u32[]{:S(2)}) copy-start(s32[12,8]{1,0:T(8,128)} %copy-done.3) | copy-start | bytes 1156
  78.3 4.4 %copy-start.1 = (f32[2,512,512]{2,1,0:T(8,128)S(1)}, f32[2,512,512]{2,1,0:T(8,128)}, u32[]{:S(2)}) copy-start(f32[2,512,512]{2,1,0:T(8,128)} %obj_ref.3) | copy-start | bytes 6291460
  78.3 4.4 %copy-start.2 = (f32[2048,256]{1,0:T(8,128)S(1)}, f32[2048,256]{1,0:T(8,128)}, u32[]{:S(2)}) copy-start(f32[2048,256]{1,0:T(8,128)} %get-tuple-element.25.grad_ref) | copy-start | bytes 6291460

commit v10 on v9

--- a/solution.py
+++ b/solution.py
@@ -122,11 +122,14 @@
             copy.wait_send()
 
 
-def greet(devices):
+def arrive(devices):
     barrier = pltpu.get_barrier_semaphore()
     for device in devices:
         pl.semaphore_signal(barrier, inc=1, device_id=device, device_id_type=MESH)
-    pl.semaphore_wait(barrier, len(devices))
+
+
+def greeted(devices):
+    pl.semaphore_wait(pltpu.get_barrier_semaphore(), len(devices))
 
 
 def post_kernel(rows, cols, tile, half, scale, rows_ref, cols_ref, corners_ref, core_ref, obj_ref, grad_ref, out_ref, all16,
@@ -139,7 +142,9 @@
     y_peers = [(lax.rem(y + s, ys) * 2 + core, col) for s in range(1, ys)]
     c_peers = column_peers(row, col, cols)
     near = [around(row, col, dr, dc, rows, cols) for dr, dc in NEAR]
-    greet([other] + y_peers + c_peers + near)
+    peers = [other] + y_peers + c_peers + near
+    arrive(peers)
+    greeted(peers)
     send = Sends(gsend, grecv)
     n = grad_ref.shape[0] // 2
     na, nb = n // ys, n // cols
@@ -292,6 +297,7 @@
     held = owner_ref.shape[0]
     core = pltpu.make_async_copy(obj_ref, ext_ref.at[:, half:half + tile, half:half + tile], lsem.at[0])
     core.start()
+    arrive(c_peers + near)
     lane = lax.broadcasted_iota(jnp.int32, (1, 128), 1)
     note = jnp.zeros((1, 128), jnp.int32)
     for h in range(held):
@@ -305,7 +311,7 @@
         for k, at in enumerate((half, end - half)):
             code(out_rows.at[k, q], ext_ref[q, at:at + half, half:end])
             code(out_cols.at[k, q], ext_ref[q, half:end, at:at + half])
-    greet(c_peers + near)
+    greeted(c_peers + near)
     send = Sends(gsend, grecv)
     got = []
 
@@ -480,17 +486,18 @@
     ]
     for copy in local:
         copy.start()
-    greet(c_peers)
+    arrive(c_peers)
     send = Sends(gsend, grecv)
     local[0].wait()
+    for k, peer in enumerate(c_peers):
+        slots[k] = amp[owned_by(peer[1], owner_ref, held)]
+    amps[col] = amp[owned_by(col, owner_ref, held)]
+    greeted(c_peers)
     amp_copies = []
     for h in range(2):
         part = pl.ds(h * (side // 2), side // 2)
         for k, peer in enumerate(c_peers):
-            if h == 0:
-                slots[k] = amp[owned_by(peer[1], owner_ref, held)]
             amp_copies.append(send(slots.at[k, part], amps.at[col, part], peer))
-    amps[col] = amp[owned_by(col, owner_ref, held)]
     local[1].wait()
     power = jnp.zeros((side, side), F32)
     for m in range(modes):

time: 129 us -> 129 us (level); the launches traced: 129 us -> 128 us
  Pallas kernels: 125 us -> 123 us
    pallas_call x1, Pallas kernels: 44.4 us -> 41.6 us  [post_call(): pl.pallas_call(functools.partial(post_kernel, rows, cols, tile, half, sca...]
    pallas_call x1, Pallas kernels: 47.7 us -> 49.6 us  [main_call(): pl.pallas_call(functools.partial(main_kernel, rows, cols), out_shape=[jax...]
where the time goes in v10:
time: 129 us; the launch traced here: 128 us
  Pallas kernels  123 us (95%)
  local copies, waits for them, and re-layouts  3.53 us (3%)
    pallas_call x1, Pallas kernels, main_call(): pl.pallas_call(functools.partial(main_kernel, rows, cols), out_shape=[jax...  49.6 us
    pallas_call x1, Pallas kernels, post_call(): pl.pallas_call(functools.partial(post_kernel, rows, cols, tile, half, sca...  41.6 us
    pallas_call x1, Pallas kernels, pre_call(): pl.pallas_call(functools.partial(pre_kernel, rows, cols, tile, half), out...  20.8 us
    pallas_call x1, Pallas kernels, cut_call(): pl.pallas_call(functools.partial(cut_kernel, cols, side // 2, held), out_...  5.01 us
    pallas_call x1, Pallas kernels, place_call(): pl.pallas_call(functools.partial(place_kernel, tile, half), out_shape=[ja...  4.36 us
    unnamed x14, local copies, waits for them, and re-layouts  3.53 us

profile of v10, /device:TPU:1, one launch (start us, length us, event | category | flops | bytes accessed | tf_op | source)
XLA Modules:
  0.0 127.7 jit_solution(13787325678914851777)
XLA Ops:
  0.6 0.0 copy-start
  0.6 1.6 %copy-done = f32[2,512,512]{2,1,0:T(8,128)S(1)} copy-done((f32[2,512,512]{2,1,0:T(8,128)S(1)}, f32[2,512,512]{2,1,0:T(8,128)}, u32[]{:S(2)}) %copy-start) | copy-done | bytes 2097176
  2.2 0.0 copy-start.5
  2.2 0.7 copy-done.5
  2.9 0.0 copy-start.6
  2.9 0.7 copy-done.6
  3.6 20.8 %pre.1 = (f32[2,768,768]{2,1,0:T(8,128)S(1)}, s32[16,1,128]{2,1,0:T(1,128)S(1)}) custom-call(s32[4]{0:T(128)S(1)} %copy-done.5, s32[2,4]{1,0:T(2,128)S(1)} %bitcast.2, f32[2,512,512]{2,1,0:T(8,128)S(1)} %copy-done), custom_call_target="tpu_custom_call" | custom-call | tf_op jit(solution)/shard_map/pre/pallas_call | solution.py:374
  24.4 5.0 %cut.1 = (f32[12,2,256,256]{3,2,1,0:T(8,128)}, s32[12,8]{1,0:T(8,128)S(1)}) custom-call(s32[16,1,128]{2,1,0:T(1,128)S(1)} %get-tuple-element.16.meta_ref, f32[2,768,768]{2,1,0:T(8,128)S(1)} %get-tuple-element.17.ext), custom_call_target="tpu_custom_call" | custom-call | tf_op jit(solution)/shard_map/cut/pallas_call | solution.py:460
  29.4 0.0 copy-start.3
  29.4 0.6 copy-done.3
  30.0 0.0 copy-start.4
  30.0 49.6 %main.1 = (f32[13,2,256,256]{3,2,1,0:T(8,128)}, f32[2048,256]{1,0:T(8,128)}) custom-call(s32[12,8]{1,0:T(8,128)} %copy-done.3, s32[4]{0:T(128)} %owner_ref.3, bf16[4,256,256]{2,1,0:T(8,128)(2,1)} %amp_hbm.1, f32[12,2,256,256]{3,2,1,0:T(8,128)} %get-tuple-element.19.patch_hbm, f32[4,2,256,256]{3,2,1,0:T(8,128)} %probe_hbm.1, ...), custom_call_target="tpu_custom_call" | custom-call | tf_op jit(solution)/shard_map/main/pallas_call | solution.py:611
  79.6 0.0 copy-done.4
  79.6 0.0 copy-start.1
  79.6 0.0 copy-start.2
  79.7 4.4 %place.1 = (bf16[2,3,128,512]{3,2,1,0:T(8,128)(2,1)S(1)}, bf16[2,3,512,128]{3,2,1,0:T(8,128)(2,1)S(1)}, bf16[4,3,128,128]{3,2,1,0:T(8,128)(2,1)S(1)}, f32[3,512,512]{2,1,0:T(8,128)S(1)}) custom-call(s32[12,8]{1,0:T(8,128)S(1)} %copy-done.4, f32[13,2,256,256]{3,2,1,0:T(8,128)} %get-tuple-element.20.placed_hbm), custom_call_target="tpu_custom_call" | custom-call | tf_op jit(solution)/shard_map/place/pallas_call | solution.py:695
  84.0 0.0 copy-done.1
  84.0 0.0 copy-done.2
  84.0 41.6 %post.1 = (f32[2,512,512]{2,1,0:T(8,128)S(1)}, bf16[2,2,1024,128]{3,2,1,0:T(8,128)(2,1)S(1)}) custom-call(bf16[2,3,128,512]{3,2,1,0:T(8,128)(2,1)S(1)} %get-tuple-element.21.rows_ref, bf16[2,3,512,128]{3,2,1,0:T(8,128)(2,1)S(1)} %get-tuple-element.22.cols_ref, bf16[4,3,128,128]{3,2,1,0:T(8,128)(2,1)S(1)} %get-tuple-element.23.corners_ref, ...), custom_call_target="tpu_custom_call" | custom-call | tf_op jit(solution)/shard_map/post/pallas_call | solution.py:263
  125.6 2.0 %finish.1 = (f32[2,512,512]{2,1,0:T(8,128)}, f32[2048,256]{1,0:T(8,128)}) custom-call(f32[2,512,512]{2,1,0:T(8,128)S(1)} %get-tuple-element.26.obj_ref, bf16[2,2,1024,128]{3,2,1,0:T(8,128)(2,1)S(1)} %get-tuple-element.27.got_ref), custom_call_target="tpu_custom_call" | custom-call | tf_op jit(solution)/shard_map/finish/pallas_call | solution.py:736
Async XLA Ops:
  0.6 1.6 %copy-start = (f32[2,512,512]{2,1,0:T(8,128)S(1)}, f32[2,512,512]{2,1,0:T(8,128)}, u32[]{:S(2)}) copy-start(f32[2,512,512]{2,1,0:T(8,128)} %obj_ref.3) | copy-start | bytes 6291460
  2.2 0.7 copy-start.5
  2.9 0.7 copy-start.6
  29.4 0.6 copy-start.3
  30.0 49.7 %copy-start.4 = (s32[12,8]{1,0:T(8,128)S(1)}, s32[12,8]{1,0:T(8,128)}, u32[]{:S(2)}) copy-start(s32[12,8]{1,0:T(8,128)} %copy-done.3) | copy-start | bytes 1156
  79.6 4.4 %copy-start.1 = (f32[2,512,512]{2,1,0:T(8,128)S(1)}, f32[2,512,512]{2,1,0:T(8,128)}, u32[]{:S(2)}) copy-start(f32[2,512,512]{2,1,0:T(8,128)} %obj_ref.3) | copy-start | bytes 6291460
  79.6 4.4 %copy-start.2 = (f32[2048,256]{1,0:T(8,128)S(1)}, f32[2048,256]{1,0:T(8,128)}, u32[]{:S(2)}) copy-start(f32[2048,256]{1,0:T(8,128)} %get-tuple-element.25.grad_ref) | copy-start | bytes 6291460
